TPU v7x, 128 devices: a whole 4x4x4 slice. The times are simulated.
128 devices in a mesh: pop: 8 (over z, y_lo), mp: 16 (over x, y_hi, core).
Axes of the slice: x: 4, y: 4 (y_hi: 2, y_lo: 2; y = y_hi * 2 + y_lo), z: 4, core: 2. Of those that a mesh axis runs over, the one named last changes fastest.
Arguments:
- tokens: bfloat16 [4096, 3584], P('pop', 'mp'), may hold values from -6 to 6
- w_gate: bfloat16 [3584, 18944], P(None, 'mp'), may hold values from -0.09375 to 0.09375
- w_up: bfloat16 [3584, 18944], P(None, 'mp'), may hold values from -0.09375 to 0.09375
- a_gate: bfloat16 [2048, 4, 3584], P('pop', None, 'mp'), may hold values from -0.125 to 0.125
- a_up: bfloat16 [2048, 4, 3584], P('pop', None, 'mp'), may hold values from -0.09375 to 0.09375
- b_gate: bfloat16 [2048, 4, 18944], P('pop', None, 'mp'), may hold values from -6 to 6
- b_up: bfloat16 [2048, 4, 18944], P('pop', None, 'mp'), may hold values from -6 to 6
- fitness: float32 [2048], P('pop'), may hold values from -4 to 4
Outputs:
- hidden: bfloat16 [4096, 18944], P('pop', 'mp')
- new_gate: bfloat16 [3584, 18944], P('pop', 'mp')
- new_up: bfloat16 [3584, 18944], P('pop', 'mp')
All inputs are finite; a program needn't handle non-finite values.
Results may differ from a plain program's by a relative error of at most 0.015.
Values may be sent and summed in bfloat16 or wider, within the bound.
No kernel may reach another device: no remote copies, remote signals or barrier semaphores. Data moves between devices by JAX's collectives and lax.ppermute only.
A program may use at most 192 MiB of HBM per device.

v0:
```python
import functools

import jax
import jax.numpy as jnp
from jax import lax
from jax.experimental import pallas as pl
from jax.experimental.pallas import tpu as pltpu
from jax.sharding import Mesh
from jax.sharding import PartitionSpec as P

bf16 = jnp.bfloat16
f32 = jnp.float32
noise_scale = 0.5
AXES = ("z", "l", "x", "h", "c")
RING = 4
VMEM = 58 * 1024 * 1024
HINT = 1
NT = (((1,), (1,)), ((), ()))
TN = (((0,), (0,)), ((), ()))


def _call(kernel, name, flops=0, moved=0, **kw):
    return pl.pallas_call(
        kernel,
        name=name,
        compiler_params=pltpu.CompilerParams(vmem_limit_bytes=VMEM),
        cost_estimate=pl.CostEstimate(flops=flops // HINT, bytes_accessed=moved // HINT, transcendentals=0),
        **kw,
    )


def _any(n):
    return [pl.BlockSpec(memory_space=pl.ANY)] * n


FULL = pl.BlockSpec(memory_space=pltpu.VMEM)
SCALARS = pl.BlockSpec(memory_space=pltpu.SMEM)


def swap(v, axis, shift=1):
    n = lax.axis_size(axis)
    return lax.ppermute(v, axis, [(i, (i + shift) % n) for i in range(n)])


def join(vs, *after):
    n = len(vs)
    return _call(
        lambda *refs: None,
        "join",
        in_specs=_any(n + len(after)),
        out_specs=_any(n),
        out_shape=[jax.ShapeDtypeStruct(v.shape, v.dtype) for v in vs],
        input_output_aliases={i: i for i in range(n)},
    )(*vs, *after)


def tie(v, *after):
    return join([v], *after)[0]


def _own_mask(members, tokens):
    m = lax.broadcasted_iota(jnp.int32, (members, tokens), 0)
    t = lax.broadcasted_iota(jnp.int32, (members, tokens), 1)
    return jnp.logical_or(t == 2 * m, t == 2 * m + 1)


def _pack_kernel(tok_ref, ag_ref, au_ref, fit_ref, sg_ref, su_ref, all_ref):
    rank, d, m = ag_ref.shape
    tok = tok_ref[...]
    t = tok.shape[1]
    fit = fit_ref[...]
    mask = _own_mask(m, t)
    rows = []
    for a_ref, s_refs in ((ag_ref, (sg_ref,)), (au_ref, (su_ref, all_ref))):
        for r in range(rank):
            a = a_ref[r]
            for s_ref in s_refs:
                s_ref[r * d : (r + 1) * d, :] = (a.astype(f32) * fit).astype(bf16)
            s = lax.dot_general(a, tok, TN, preferred_element_type=f32)
            rows.append(jnp.sum(jnp.where(mask, s, 0.0), axis=0, keepdims=True))
    part = jnp.concatenate(rows, axis=0)
    high = part.astype(bf16)
    low = (part - high.astype(f32)).astype(bf16)
    at = rank * d
    for v in (tok, jnp.concatenate([high, low], axis=0)):
        for lo in range(0, t, m):
            all_ref[at : at + v.shape[0], :] = v[:, lo : lo + m]
            at += v.shape[0]


def pack(tok_t, ag, au, fit):
    rank, d, m = ag.shape
    t = tok_t.shape[1]
    pay = (d + 4 * rank) * (t // m)
    return _call(
        _pack_kernel,
        "pack",
        flops=4 * rank * d * m * t,
        moved=8 * rank * d * m,
        in_specs=[FULL] * 4,
        out_specs=[FULL] * 3,
        out_shape=[jax.ShapeDtypeStruct((n, m), bf16) for n in (rank * d, rank * d, rank * d + pay)],
    )(tok_t, ag, au, fit)


def _pick_kernel(y_ref, s_ref, pa_ref, pb_ref, all_ref, *refs):
    out_ref = refs[-1]
    n = s_ref.shape[0]
    y = y_ref[0]
    for where, at, ref in (
        (y == 1, 0, pb_ref),
        (y == 2, 0, pa_ref),
        (jnp.logical_or(y == 0, y == 3), 0, s_ref),
        (y < 2, n, pa_ref),
        (y >= 2, n, pb_ref),
    ):

        @pl.when(where)
        def _():
            out_ref[at : at + n, :] = ref[...]

    out_ref[2 * n :, :] = all_ref[n:, :]


def pick(y, s, pa, pb, rest, *after):
    n, m = s.shape
    return _call(
        _pick_kernel,
        "pick",
        moved=8 * s.size,
        in_specs=[SCALARS, FULL, FULL, FULL, FULL] + _any(len(after)),
        out_specs=FULL,
        out_shape=jax.ShapeDtypeStruct((n + rest.shape[0], m), s.dtype),
    )(y, s, pa, pb, rest, *after)


def rows_of(refs, lo, hi):
    if len(refs) == 1:
        return refs[0][lo:hi, :]
    n = refs[0].shape[0]
    parts = []
    if lo < n:
        parts.append(refs[0][lo : min(hi, n), :])
    if hi > n:
        parts.append(refs[1][max(lo, n) - n : hi - n, :])
    return parts[0] if len(parts) == 1 else jnp.concatenate(parts, axis=0)


def blocks_of(refs):
    own, one, two_lo, two_hi, three = refs
    return [own], [one], [two_lo, two_hi], [three]


PIECES = 5


ORDER = (2, 1, 3, 0)


def _update_kernel(coeff, slabs, d, rest, nb, nafter, block_ref, *refs):
    blocks = blocks_of(refs[:PIECES])
    b_refs = refs[PIECES : PIECES + nb]
    pp_ref, pm_ref, rp_ref, rm_ref, own_ref, lhs_ref, rhs_ref = refs[PIECES + nb + nafter :]
    m = b_refs[0].shape[2]
    n = d // 2
    i = pl.program_id(0)

    @pl.when(i == 0)
    def _():
        for step in range(RING):
            for j, block in enumerate(blocks):

                @pl.when(block_ref[step] == j)
                def _():
                    for k in range(slabs):
                        lhs_ref[step * d : (step + 1) * d, k * m : (k + 1) * m] = rows_of(block, k * d, (k + 1) * d)

    def put(acc):
        acc = (acc * coeff).astype(bf16)
        two, one, back, own = (acc[k * d : (k + 1) * d] for k in range(RING))
        w = acc.shape[1]
        pp_ref[:n, :w] = two[:n]
        pm_ref[:n, :w] = two[n:]
        pp_ref[n:, :w] = one[n:]
        rp_ref[:, :w] = one[:n]
        pm_ref[n:, :w] = back[:n]
        rm_ref[:, :w] = back[n:]
        own_ref[:, :w] = own

    slab = [(first, r) for first in range(0, nb, 2) for r in range(b_refs[first].shape[0])]
    for side in range(2):

        @pl.when(i == side)
        def _():
            for k, (first, r) in enumerate(slab):
                rhs_ref[:, k * m : (k + 1) * m] = b_refs[first + side][r]

    @pl.when(i < 2)
    def _():
        put(lax.dot_general(lhs_ref[...], rhs_ref[...], NT, preferred_element_type=f32))

    @pl.when(i == 2)
    def _():
        for k, (first, r) in enumerate(slab):
            for side in range(2):
                rhs_ref[side * rest : (side + 1) * rest, k * m : (k + 1) * m] = b_refs[first + side][r, :rest, :]
        put(lax.dot_general(lhs_ref[...], rhs_ref[: 2 * rest, :], NT, preferred_element_type=f32))


CUT = 1152


def update(coeff, block, rows, factors, seconds, *after):
    _, q, m = seconds[0].shape
    slabs = sum(b.shape[0] for b in seconds[::2])
    d = rows
    wide = 2 * q

    def once(shape):
        return pl.BlockSpec(shape, lambda i, w: (0,) * len(shape), pipeline_mode=pl.Buffered(1))

    def cut(n):
        return pl.BlockSpec((n, CUT), lambda i, w: (0, i))

    def near(b):
        return pl.BlockSpec((b.shape[0], CUT, m), lambda i, w: (0, jnp.minimum(i, 1), 0))

    def far(b):
        return pl.BlockSpec((b.shape[0], CUT, m), lambda i, w: (0, jnp.maximum(i - 1, 0), 0))

    sizes = (d, d, d // 2, d // 2, d)
    return _call(
        functools.partial(_update_kernel, coeff, slabs, d, q - CUT, len(seconds), len(after)),
        "update",
        flops=2 * RING * d * slabs * m * wide,
        moved=2 * (RING * slabs * d * m + slabs * m * wide + RING * d * wide),
        grid_spec=pltpu.PrefetchScalarGridSpec(
            num_scalar_prefetch=1,
            grid=(3,),
            in_specs=[once(f.shape) for f in factors] + [(near, far)[i % 2](b) for i, b in enumerate(seconds)] + _any(len(after)),
            out_specs=[cut(n) for n in sizes],
            scratch_shapes=[pltpu.VMEM((RING * d, slabs * m), bf16), pltpu.VMEM((CUT, slabs * m), bf16)],
        ),
        out_shape=[jax.ShapeDtypeStruct((n, wide), bf16) for n in sizes],
    )(block, *factors, *seconds, *after)


def _at(shape, row=0):
    return pl.BlockSpec(shape, lambda i: (row, 0))


def _relay_kernel(gp_ref, gm_ref, rp_ref, rm_ref, *refs):
    ap_ref, am_ref = refs[-2:]
    ap_ref[...] = (rp_ref[...].astype(f32) + gp_ref[...].astype(f32)).astype(bf16)
    am_ref[...] = (rm_ref[...].astype(f32) + gm_ref[...].astype(f32)).astype(bf16)


def relay(gp, gm, rp, rm, *after):
    spec = _at(rp.shape)
    return _call(
        _relay_kernel,
        "relay",
        grid=(1,),
        moved=12 * rp.size,
        in_specs=[spec] * 4 + _any(len(after)),
        out_specs=[spec] * 2,
        out_shape=[jax.ShapeDtypeStruct(rp.shape, bf16)] * 2,
    )(gp, gm, rp, rm, *after)


def _halves_kernel(one_ref, three_ref, *refs):
    lo_ref, hi_ref = refs[-2:]
    lo_ref[...] = one_ref[...]
    hi_ref[...] = three_ref[...]


def halves(one, three, *after):
    n, m = one.shape[0] // 2, one.shape[1]
    return _call(
        _halves_kernel,
        "halves",
        grid=(1,),
        moved=8 * n * m,
        in_specs=[_at((n, m)), _at((n, m), 1)] + _any(len(after)),
        out_specs=[_at((n, m))] * 2,
        out_shape=[jax.ShapeDtypeStruct((n, m), bf16)] * 2,
    )(one, three, *after)


def _total(own_ref, gp_ref, gm_ref, fp_ref, fm_ref):
    n = fp_ref.shape[0]
    first = own_ref[:n, :].astype(f32) + gm_ref[n:, :].astype(f32) + fp_ref[...].astype(f32)
    second = own_ref[n:, :].astype(f32) + gp_ref[n:, :].astype(f32) + fm_ref[...].astype(f32)
    return jnp.concatenate([first, second], axis=0)


def _split(total, near_ref, far_ref):
    q, k = near_ref.shape[1], CUT
    near_ref[:, :k] = total[:, :k]
    near_ref[:, k:] = total[:, 2 * k : k + q]
    far_ref[:, :k] = total[:, k : 2 * k].astype(far_ref.dtype)
    far_ref[:, k:] = total[:, k + q :].astype(far_ref.dtype)


def _ends(shape):
    d, q = shape[0], shape[1] // 2
    return [jax.ShapeDtypeStruct((d, q), f32), jax.ShapeDtypeStruct((d, q), bf16)]


def _gate_early_kernel(c_ref, held_ref, own_ref, gp_ref, gm_ref, *refs):
    near_ref, far_ref = refs[-2:]
    d = own_ref.shape[0]
    n = d // 2
    first = own_ref[:n, :].astype(f32) + gm_ref[n:, :].astype(f32)
    second = own_ref[n:, :].astype(f32) + gp_ref[n:, :].astype(f32)
    _split(jnp.concatenate([first, second], axis=0), near_ref, far_ref)
    near_ref[...] += held_ref[pl.ds(pl.multiple_of(c_ref[0] * d, d), d), :].astype(f32)


def gate_early(c, held, own, gp, gm, *after):
    d, q = own.shape[0], own.shape[1] // 2
    return _call(
        _gate_early_kernel,
        "gate_early",
        in_specs=[SCALARS] + [FULL] * 4 + _any(len(after)),
        out_specs=[FULL] * 2,
        out_shape=[jax.ShapeDtypeStruct((d, q), f32)] * 2,
    )(c, held, own, gp, gm, *after)


def _gate_late_kernel(near_ref, far_ref, fp_ref, fm_ref, out_ref, send_ref):
    n = fp_ref.shape[0]
    q, k = near_ref.shape[1], CUT
    for ref, rows in ((fp_ref, slice(0, n)), (fm_ref, slice(n, 2 * n))):
        out_ref[rows, :k] = (near_ref[rows, :k] + ref[:, :k].astype(f32)).astype(bf16)
        out_ref[rows, k:] = (near_ref[rows, k:] + ref[:, 2 * k : k + q].astype(f32)).astype(bf16)
        send_ref[rows, :k] = (far_ref[rows, :k] + ref[:, k : 2 * k].astype(f32)).astype(bf16)
        send_ref[rows, k:] = (far_ref[rows, k:] + ref[:, k + q :].astype(f32)).astype(bf16)


def gate_late(near, far, fp, fm):
    return _call(
        _gate_late_kernel,
        "gate_late",
        in_specs=[FULL] * 4,
        out_specs=[FULL] * 2,
        out_shape=[jax.ShapeDtypeStruct(near.shape, bf16)] * 2,
    )(near, far, fp, fm)


def _gate_rows_kernel(c_ref, held_ref, near_ref, far_ref, out_ref):
    d = near_ref.shape[0]
    c = c_ref[0]
    mine, other = pl.ds(pl.multiple_of(c * d, d), d), pl.ds(pl.multiple_of((1 - c) * d, d), d)
    out_ref[mine, :] = near_ref[...]
    out_ref[other, :] = (held_ref[other, :].astype(f32) + far_ref[...].astype(f32)).astype(bf16)


def gate_rows(c, held, near, far):
    return _call(
        _gate_rows_kernel,
        "gate_rows",
        in_specs=[SCALARS] + [FULL] * 3,
        out_specs=FULL,
        out_shape=jax.ShapeDtypeStruct(held.shape, bf16),
    )(c, held, near, far)


def _up_sums_kernel(mine_ref, *refs):
    keep_ref, send_ref = refs[10:]
    a, b = _total(*refs[:5]), _total(*refs[5:10])
    mine = mine_ref[0] == 1
    keep_ref[...] = jnp.where(mine, a, b)
    send_ref[...] = jnp.where(mine, b, a).astype(bf16)


def up_sums(mine, parts_a, parts_b, *after):
    shape = parts_a[0].shape

    def kernel(mine_ref, *refs):
        _up_sums_kernel(mine_ref, *refs[:10], *refs[-2:])

    return _call(
        kernel,
        "up_sums",
        in_specs=[SCALARS] + [FULL] * 10 + _any(len(after)),
        out_specs=[FULL] * 2,
        out_shape=[jax.ShapeDtypeStruct(shape, f32), jax.ShapeDtypeStruct(shape, bf16)],
    )(mine, *parts_a, *parts_b, *after)


def up_sum(keep, sent):
    def kernel(keep_ref, sent_ref, near_ref, far_ref):
        _split(keep_ref[...] + sent_ref[...].astype(f32), near_ref, far_ref)

    return _call(
        kernel,
        "up_sum",
        in_specs=[FULL] * 2,
        out_specs=[FULL] * 2,
        out_shape=_ends(keep.shape),
    )(keep, sent)


def _renew_kernel(c_ref, held_ref, near_ref, far_ref, out_ref):
    d = near_ref.shape[0]
    near, far = near_ref[...], far_ref[...].astype(f32)

    def put(first, second):
        out_ref[:d, :] = (held_ref[:d, :].astype(f32) + first).astype(bf16)
        out_ref[d:, :] = (held_ref[d:, :].astype(f32) + second).astype(bf16)

    @pl.when(c_ref[0] == 0)
    def _():
        put(near, far)

    @pl.when(c_ref[0] == 1)
    def _():
        put(far, near)


def renew(c, held, near, far):
    return _call(
        _renew_kernel,
        "renew",
        in_specs=[SCALARS] + [FULL] * 3,
        out_specs=FULL,
        out_shape=jax.ShapeDtypeStruct(held.shape, bf16),
    )(c, held, near, far)


def _tokens_kernel(n, at_ref, *refs):
    tok_ref = refs[-1]
    t, m = tok_ref.shape[1], refs[0].shape[1]
    d = (tok_ref.shape[0] - 2 * n) // (2 * RING)
    x, h = at_ref[0], at_ref[1]
    wide = t // m
    total = None
    for s in range(2):
        gather = refs[s * PIECES : (s + 1) * PIECES]
        start = gather[0].shape[0] - wide * (d + 2 * n)
        for j, block in enumerate(blocks_of(gather)):
            rows = [rows_of(block, start + i * d, start + (i + 1) * d) for i in range(wide)]
            to = 2 * lax.rem(x + RING - j, RING) + (h if s == 0 else 1 - h)
            tok_ref[pl.ds(pl.multiple_of(to * d, d), d), :] = jnp.concatenate(rows, axis=1)
            at = start + wide * d
            terms = [rows_of(block, at + i * 2 * n, at + (i + 1) * 2 * n).astype(f32) for i in range(wide)]
            both = jnp.concatenate(terms, axis=1)
            value = both[:n] + both[n:]
            total = value if total is None else total + value
    high = total.astype(bf16)
    low = (total - high.astype(f32)).astype(bf16)
    tok_ref[2 * RING * d :, :] = jnp.concatenate([high, low], axis=0)


def tokens_of(at, own, other, d, t, probes, *after):
    return _call(
        functools.partial(_tokens_kernel, probes),
        "tokens",
        moved=8 * RING * 2 * d * t,
        in_specs=[SCALARS] + [FULL] * (2 * PIECES) + _any(len(after)),
        out_specs=FULL,
        out_shape=jax.ShapeDtypeStruct((2 * RING * d + 2 * probes, t), bf16),
    )(at, *own, *other, *after)


def _hidden_kernel(c_ref, mine_ref, other_ref, wg_ref, wu_ref, bg_ref, bu_ref, *refs):
    out_ref, tok_ref, p_ref = refs[-3:]
    rank, _, m = bg_ref.shape
    t = mine_ref.shape[1]
    n = 2 * rank
    d = (mine_ref.shape[0] - 2 * n) // (2 * RING)

    @pl.when(pl.program_id(0) == 0)
    def _():
        c = c_ref[0]
        for ref, core in ((mine_ref, c), (other_ref, 1 - c)):
            for i in range(2 * RING):
                tok_ref[pl.ds(pl.multiple_of((2 * i + core) * d, d), d), :] = ref[i * d : (i + 1) * d, :]
        mask = _own_mask(m, t)
        terms = mine_ref[2 * RING * d :, :].astype(f32) + other_ref[2 * RING * d :, :].astype(f32)
        probe = (terms[:n] + terms[n:]).astype(bf16).astype(f32) * noise_scale
        for i in range(2 * rank):
            row = jnp.broadcast_to(probe[i : i + 1, :], (m, t))
            p_ref[i * m : (i + 1) * m, :] = jnp.where(mask, row, 0.0).astype(bf16)

    pre = []
    for k, (w_ref, b_ref) in enumerate(((wg_ref, bg_ref), (wu_ref, bu_ref))):
        b = jnp.concatenate([b_ref[r] for r in range(rank)], axis=1)
        acc = jnp.dot(w_ref[...], tok_ref[...], preferred_element_type=f32)
        acc += jnp.dot(b, p_ref[k * rank * m : (k + 1) * rank * m, :], preferred_element_type=f32)
        pre.append(acc)
    g, u = pre
    out_ref[...] = (g / (1.0 + jnp.exp(-g)) * u).astype(out_ref.dtype)


def hidden_of(c, mine, other, wg, wu, bg, bu, *after):
    t = mine.shape[1]
    q, d = wg.shape
    rank, _, m = bg.shape
    block = 304
    w_spec = pl.BlockSpec((block, d), lambda i: (i, 0))
    b_spec = pl.BlockSpec((rank, block, m), lambda i: (0, i, 0))
    t_spec = pl.BlockSpec(mine.shape, lambda i: (0, 0), pipeline_mode=pl.Buffered(1))
    return _call(
        _hidden_kernel,
        "hidden",
        flops=4 * q * t * (d + rank * m),
        moved=2 * (2 * q * d + d * t + 2 * rank * q * m + q * t),
        grid=(pl.cdiv(q, block),),
        in_specs=[SCALARS, t_spec, t_spec, w_spec, w_spec, b_spec, b_spec] + _any(len(after)),
        out_specs=pl.BlockSpec((block, t), lambda i: (i, 0)),
        out_shape=jax.ShapeDtypeStruct((q, t), bf16),
        scratch_shapes=[pltpu.VMEM((d, t), bf16), pltpu.VMEM((2 * rank * m, t), bf16)],
    )(c, mine, other, wg, wu, bg, bu, *after)


def local(tokens, w_gate, w_up, a_gate, a_up, b_gate, b_up, fitness):
    members, rank, d = a_gate.shape
    q = w_gate.shape[1]
    coeff = 1.0 / (members * lax.axis_size("z") * lax.axis_size("l") * rank) ** 0.5
    z, l, x, h, c = (lax.axis_index(a) for a in AXES)
    tok_t = tokens.T
    ag_t, au_t = (a.transpose(1, 2, 0) for a in (a_gate, a_up))
    bg, bu = (b.transpose(1, 2, 0) for b in (b_gate, b_up))
    block = (x - z - jnp.array(ORDER, jnp.int32)) % RING

    sg, su, rest = pack(tok_t, ag_t, au_t, fitness[None, :])
    bu_c = swap(bu, "c")

    def hop(axis, first, second):
        return swap(first, axis, 1), swap(second, axis, -1)

    one, three = hop("x", su, su)
    first = (2 * z + l) * 2 * d
    held = [lax.dynamic_slice_in_dim(w, first, 2 * d, 0) for w in (w_gate, w_up)]
    so = swap(rest, "h")
    one, three, bu_c, *held = join([one, three, bu_c, *held])
    at_y = (0, 2, 1, 3)
    sg_y = tie(sg, so)
    pa, pb = (
        lax.ppermute(sg_y, ("l", "h"), [(at_y[i], at_y[j]) for i, j in pairs])
        for pairs in (((1, 0), (2, 1), (0, 2)), ((3, 1), (1, 2), (2, 3)))
    )
    lo, hi, so = join([*hop("x", *halves(one, three)), so])
    su_x = (su, one, lo, hi, three)
    so = tie(so, lo)
    one, three = hop("x", so, so)
    ua = update(coeff, block, d, su_x, [bu, bu_c], so)
    gp_a, gm_a = hop("z", *ua[:2])
    one, three, pb = join([one, three, pb], ua[-1])
    lo, hi = hop("x", *halves(one, three))
    both = pick((2 * h + l).reshape(1), sg_y, pa, pb, rest, one)
    far_0 = swap(tie(bg, both), "l")
    lo, hi = join([lo, hi], both)
    so_x = (so, one, lo, hi, three)
    both = tie(both, lo)
    one, three = hop("x", both, both)
    gp_a, gm_a = join([gp_a, gm_a], both)
    ap, am = relay(gp_a, gm_a, *ua[2:4])
    fp_a, fm_a = hop("z", ap, am)
    ub = update(coeff, block, d, so_x, [bu, bu_c], ap)
    one, three = join([one, three], ap, ub[-1])
    lo, hi = hop("x", *halves(one, three))
    fp_a, fm_a = join([fp_a, fm_a], one)
    gp_b, gm_b = hop("z", *join(ub[:2], fp_a))
    lo, hi = join([lo, hi], fp_a)
    sg_x = (both, one, lo, hi, three)
    bg_c = swap(tie(bg, lo), "c")
    tok = tokens_of(jnp.stack([x, h]), sg_x, so_x, d, tok_t.shape[1], 2 * rank)
    tok_c = swap(tok, "c")
    gp_b, gm_b, far_0 = join([gp_b, gm_b, far_0], tok)
    ap, am = relay(gp_b, gm_b, *ub[2:4])
    fp_b, fm_b = hop("z", ap, am)
    fars = [v for far in (far_0,) for v in (far, swap(far, "c"))]
    gg = update(coeff, block, d, sg_x, [bg, bg_c, *fars], ap)
    fp_b, fm_b = join([fp_b, fm_b], gg[-1])
    gp_g, gm_g = hop("z", *gg[:2])
    keep, send = up_sums(
        (l == h).astype(jnp.int32).reshape(1), (ua[4], gp_a, gm_a, fp_a, fm_a), (ub[4], gp_b, gm_b, fp_b, fm_b)
    )
    sent = swap(send, "l")
    hidden = hidden_of(c.reshape(1), tok, tok_c, w_gate.T, w_up.T, bg, bu, gg[-1])
    gp_g, gm_g = join([gp_g, gm_g], hidden)
    ap, am = relay(gp_g, gm_g, *gg[2:4])
    fp_g, fm_g = hop("z", ap, am)
    at_c = c.reshape(1)
    gate_near, gate_far = gate_early(at_c, held[0], gg[4], gp_g, gm_g, ap)
    up_near, up_far = up_sum(keep, tie(sent, gate_near))
    new_up = renew(at_c, held[1], up_near, swap(up_far, "c"))
    fp_g, fm_g = join([fp_g, fm_g], gate_near)
    gate_near, gate_far = gate_late(gate_near, gate_far, fp_g, fm_g)
    new_gate = gate_rows(at_c, held[0], gate_near, swap(gate_far, "c"))
    return hidden.T, new_gate, new_up


def solution(mesh):
    fine = Mesh(mesh.devices.reshape(4, 2, 4, 2, 2), AXES)
    pop, mp = ("z", "l"), ("x", "h", "c")
    return jax.shard_map(
        local,
        mesh=fine,
        in_specs=(
            P(pop, mp),
            P(None, mp),
            P(None, mp),
            P(pop, None, mp),
            P(pop, None, mp),
            P(pop, None, mp),
            P(pop, None, mp),
            P(pop),
        ),
        out_specs=(P(pop, mp), P(pop, mp), P(pop, mp)),
        check_vma=False,
    )
```

profile of v0, /device:TPU:1, one launch (start us, length us, event | category | flops | bytes accessed | tf_op | source)
XLA Modules:
  0.0 214.4 jit_solution(6926507339366001186)
XLA Ops:
  0.6 1.5 collective-permute-start.4
  2.1 3.1 %pack.1 = (bf16[896,256]{1,0:T(8,128)(2,1)}, bf16[896,256]{1,0:T(8,128)(2,1)}, bf16[1376,256]{1,0:T(8,128)(2,1)}) custom-call(bf16[224,512]{1,0:T(8,128)(2,1)} %bitcast.27, bf16[4,224,256]{2,1,0:T(8,128)(2,1)} %bitcast.25, bf16[4,224,256]{2,1,0:T(8,128)(2,1)} %bitcast.26, f32[1,256]{1,0:T(1,128)} %bitcast.28), custom_call_target="tpu_custom_call" | custom-call | flops 469762048 | bytes 1835008 | tf_op jit(solution)/shard_map/pack/pallas_call | solution.py:95
  5.2 3.0 %collective-permute-start = (bf16[1376,256]{1,0:T(8,128)(2,1)}, bf16[1376,256]{1,0:T(8,128)(2,1)S(1)}, u32[]{:S(2)}, u32[]{:S(2)}) collective-permute-start(bf16[1376,256]{1,0:T(8,128)(2,1)} %get-tuple-element.74.all_ref), channel_id=1, source_target_pairs={{0,2},{2,0},{1,3},{3,1},{4,6},{6,4},{5,7},{7,5},{8,10},{10,8},{9,1... | collective-permute-start | bytes 2113544 | tf_op jit(solution)/shard_map/ppermute | solution.py:42
  8.2 1.2 collective-permute-start.2
  9.4 1.5 collective-permute-start.3
  10.9 3.2 %constant_dynamic-slice_fusion = (bf16[448,1184]{0,1:T(8,128)(2,1)S(1)}, bf16[448,1184]{0,1:T(8,128)(2,1)S(1)}) fusion(bf16[3584,1184]{0,1:T(8,128)(2,1)} %param.11, s32[]{:T(128)S(6)} %select_n.11, bf16[3584,1184]{0,1:T(8,128)(2,1)} %param.10), kind=kLoop, calls=%fused_computation.5 | loop fusion | bytes 4243460 | tf_op jit(solution)/shard_map/dynamic_slice | solution.py:536
  14.1 1.6 copy.52.refs_3_
  15.7 1.5 copy.53.refs_4_
  17.2 4.4 %collective-permute-done.2.refs_0_ = bf16[896,256]{1,0:T(8,128)(2,1)} collective-permute-done((bf16[896,256]{1,0:T(8,128)(2,1)}, bf16[896,256]{1,0:T(8,128)(2,1)}, u32[]{:S(2)}, u32[]{:S(2)}) %collective-permute-start.2) | collective-permute-done | bytes 458784 | tf_op jit(solution)/shard_map/ppermute | solution.py:42
  21.6 1.8 halves.3
  23.4 0.9 collective-permute-start.5
  24.3 1.8 collective-permute-start.6
  26.1 0.9 copy-done.1
  27.8 3.0 %collective-permute-done.5.refs_0_ = bf16[448,256]{1,0:T(8,128)(2,1)S(1)} collective-permute-done((bf16[448,256]{1,0:T(8,128)(2,1)}, bf16[448,256]{1,0:T(8,128)(2,1)S(1)}, u32[]{:S(2)}, u32[]{:S(2)}) %collective-permute-start.5) | collective-permute-done | bytes 229408 | tf_op jit(solution)/shard_map/ppermute | solution.py:42
  32.2 2.7 %collective-permute-start.8 = (bf16[1376,256]{1,0:T(8,128)(2,1)}, bf16[1376,256]{1,0:T(8,128)(2,1)S(1)}, u32[]{:S(2)}, u32[]{:S(2)}) collective-permute-start(bf16[1376,256]{1,0:T(8,128)(2,1)} %join.22.refs_7_.refs_0_.refs_5_), channel_id=1, source_target_pairs={{0,12},{4,0},{8,4},{12,8},{1,13},{5,1},{9,5},{13,9},{2,14},{6,2},{... | collective-permute-start | bytes 2113544 | tf_op jit(solution)/shard_map/ppermute | solution.py:42
  35.4 2.4 %collective-permute-start.1 = (bf16[896,256]{1,0:T(8,128)(2,1)S(1)}, bf16[896,256]{1,0:T(8,128)(2,1)}, u32[]{:S(2)}, u32[]{:S(2)}) collective-permute-start(bf16[896,256]{1,0:T(8,128)(2,1)S(1)} %copy-done.22), channel_id=1, source_target_pairs={{16,0},{2,16},{0,2},{17,1},{3,17},{1,3},{20,4},{6,20},{4,6},{21,5}... | collective-permute-start | bytes 1376264 | tf_op jit(solution)/shard_map/ppermute | solution.py:542
  37.8 11.3 %update.3 = (bf16[224,2368]{1,0:T(8,128)(2,1)}, bf16[224,2368]{1,0:T(8,128)(2,1)}, bf16[112,2368]{1,0:T(8,128)(2,1)}, bf16[112,2368]{1,0:T(8,128)(2,1)}, bf16[224,2368]{1,0:T(8,128)(2,1)}) custom-call(s32[4]{0:T(128)} %and_select_fusion.block_ref, bf16[896,256]{1,0:T(8,128)(2,1)} %get-tuple-element.75.refs_0_, ...), custom_call_target="tpu_custom_call" | custom-call | flops 4345298944 | bytes 10928128 | tf_op jit(solution)/shard_map/update/pallas_call | solution.py:232
  49.0 1.7 collective-permute-start.14
  50.8 2.2 %collective-permute-start.15 = (bf16[224,2368]{1,0:T(8,128)(2,1)}, bf16[224,2368]{1,0:T(8,128)(2,1)S(1)}, u32[]{:S(2)}, u32[]{:S(2)}) collective-permute-start(bf16[224,2368]{1,0:T(8,128)(2,1)} %get-tuple-element.92), channel_id=1, source_target_pairs={{0,96},{32,0},{64,32},{96,64},{1,97},{33,1},{65,33},{97,65},{2,98}... | collective-permute-start | bytes 3182600 | tf_op jit(solution)/shard_map/ppermute | solution.py:42
  53.0 0.8 copy-done.2
  54.1 2.0 halves.4
  56.1 2.6 %collective-permute-start.11 = (bf16[688,256]{1,0:T(8,128)(2,1)}, bf16[688,256]{1,0:T(8,128)(2,1)S(1)}, u32[]{:S(2)}, u32[]{:S(2)}) collective-permute-start(bf16[688,256]{1,0:T(8,128)(2,1)} %get-tuple-element.89), channel_id=1, source_target_pairs={{0,12},{4,0},{8,4},{12,8},{1,13},{5,1},{9,5},{13,9},{2,14},{6,2},{... | collective-permute-start | bytes 1056776 | tf_op jit(solution)/shard_map/ppermute | solution.py:42
  58.8 3.3 %copy.81.refs_0_ = bf16[4,1184,256]{2,1,0:T(8,128)(2,1)} copy(bf16[4,1184,256]{2,1,0:T(8,128)(2,1)} %bitcast.14) | data formatting | bytes 4849664
  62.1 2.6 %pick.1.refs_2_.refs_0_.refs_1_ = bf16[2272,256]{1,0:T(8,128)(2,1)} custom-call(s32[1]{0:T(128)} %bitcast.3.y_ref, bf16[896,256]{1,0:T(8,128)(2,1)} %join.19.s_ref, bf16[896,256]{1,0:T(8,128)(2,1)} %collective-permute-done.1.pa_ref, bf16[896,256]{1,0:T(8,128)(2,1)} %get-tuple-element.85.pb_ref, bf16[1376,256]{1,0:T(8,128)(2,1)} %get-tuple-element.74.all_ref, ...), custom_call_target="tpu_custom_call" | custom-call | bytes 1835008 | tf_op jit(solution)/shard_map/pick/pallas_call | solution.py:127
  64.7 1.0 collective-permute-start.24
  67.2 2.7 %collective-permute-start.13 = (bf16[2272,256]{1,0:T(8,128)(2,1)}, bf16[2272,256]{1,0:T(8,128)(2,1)S(1)}, u32[]{:S(2)}, u32[]{:S(2)}) collective-permute-start(bf16[2272,256]{1,0:T(8,128)(2,1)} %join.25.refs_2_.refs_0_), channel_id=1, source_target_pairs={{0,12},{4,0},{8,4},{12,8},{1,13},{5,1},{9,5},{13,9},{2,14},{6,2},{... | collective-permute-start | bytes 3489800 | tf_op jit(solution)/shard_map/ppermute | solution.py:42
  69.9 5.0 %collective-permute-done.14.refs_0_ = bf16[224,2368]{1,0:T(8,128)(2,1)S(1)} collective-permute-done((bf16[224,2368]{1,0:T(8,128)(2,1)}, bf16[224,2368]{1,0:T(8,128)(2,1)S(1)}, u32[]{:S(2)}, u32[]{:S(2)}) %collective-permute-start.14) | collective-permute-done | bytes 1060896 | tf_op jit(solution)/shard_map/ppermute | solution.py:42
  74.9 1.0 copy-done.8
  75.9 1.0 copy-done.9
  76.9 2.7 %relay.3 = (bf16[112,2368]{1,0:T(8,128)(2,1)}, bf16[112,2368]{1,0:T(8,128)(2,1)}) custom-call(bf16[224,2368]{1,0:T(8,128)(2,1)} %get-tuple-element.93.gp_ref.refs_1_, bf16[224,2368]{1,0:T(8,128)(2,1)} %get-tuple-element.94.gm_ref.refs_2_, bf16[112,2368]{1,0:T(8,128)(2,1)} %get-tuple-element.95.rp_ref, bf16[112,2368]{1,0:T(8,128)(2,1)} %get-tuple-element.96.rm_ref), custom_call_target="tpu_custom_call" | custom-call | bytes 3182592 | tf_op jit(solution)/shard_map/relay/pallas_call | solution.py:260
  79.6 2.7 %collective-permute-start.19 = (bf16[112,2368]{1,0:T(8,128)(2,1)}, bf16[112,2368]{1,0:T(8,128)(2,1)S(1)}, u32[]{:S(2)}, u32[]{:S(2)}) collective-permute-start(bf16[112,2368]{1,0:T(8,128)(2,1)} %get-tuple-element.104), channel_id=1, source_target_pairs={{0,96},{32,0},{64,32},{96,64},{1,97},{33,1},{65,33},{97,65},{2,98}... | collective-permute-start | bytes 1591304 | tf_op jit(solution)/shard_map/ppermute | solution.py:42
  82.3 11.6 %update.4 = (bf16[224,2368]{1,0:T(8,128)(2,1)}, bf16[224,2368]{1,0:T(8,128)(2,1)}, bf16[112,2368]{1,0:T(8,128)(2,1)}, bf16[112,2368]{1,0:T(8,128)(2,1)}, bf16[224,2368]{1,0:T(8,128)(2,1)}) custom-call(s32[4]{0:T(128)} %and_select_fusion.block_ref, bf16[1376,256]{1,0:T(8,128)(2,1)} %join.22.refs_7_.refs_0_.refs_5_, ...), custom_call_target="tpu_custom_call" | custom-call | flops 4345298944 | bytes 10928128 | tf_op jit(solution)/shard_map/update/pallas_call | solution.py:232
  93.9 1.0 copy-done
  96.3 2.7 %collective-permute-start.23 = (bf16[224,2368]{1,0:T(8,128)(2,1)}, bf16[224,2368]{1,0:T(8,128)(2,1)S(1)}, u32[]{:S(2)}, u32[]{:S(2)}) collective-permute-start(bf16[224,2368]{1,0:T(8,128)(2,1)} %get-tuple-element.111), channel_id=1, source_target_pairs={{0,96},{32,0},{64,32},{96,64},{1,97},{33,1},{65,33},{97,65},{2,98}... | collective-permute-start | bytes 3182600 | tf_op jit(solution)/shard_map/ppermute | solution.py:42
  98.9 2.3 %halves.5 = (bf16[1136,256]{1,0:T(8,128)(2,1)}, bf16[1136,256]{1,0:T(8,128)(2,1)}) custom-call(bf16[2272,256]{1,0:T(8,128)(2,1)} %get-tuple-element.100.one_ref.refs_2_.refs_1_, bf16[2272,256]{1,0:T(8,128)(2,1)} %get-tuple-element.101.three_ref.refs_4_), custom_call_target="tpu_custom_call" | custom-call | bytes 2326528 | tf_op jit(solution)/shard_map/halves/pallas_call | solution.py:279
  101.8 2.1 collective-permute-start.17
  103.9 1.5 copy.78.refs_0_
  105.9 7.1 %collective-permute-done.16.refs_0_ = bf16[1136,256]{1,0:T(8,128)(2,1)S(1)} collective-permute-done((bf16[1136,256]{1,0:T(8,128)(2,1)}, bf16[1136,256]{1,0:T(8,128)(2,1)S(1)}, u32[]{:S(2)}, u32[]{:S(2)}) %collective-permute-start.16) | collective-permute-done | bytes 581664 | tf_op jit(solution)/shard_map/ppermute | solution.py:42
  113.1 0.8 copy-done.13
  113.9 0.8 copy-done.16
  114.7 5.2 %collective-permute-start.21 = (bf16[4,1184,256]{2,1,0:T(8,128)(2,1)}, bf16[4,1184,256]{2,1,0:T(8,128)(2,1)S(1)}, u32[]{:S(2)}, u32[]{:S(2)}) collective-permute-start(bf16[4,1184,256]{2,1,0:T(8,128)(2,1)} %join.30), channel_id=1, source_target_pairs={{0,1},{1,0},{2,3},{3,2},{4,5},{5,4},{6,7},{7,6},{8,9},{9,8},{10,11... | collective-permute-start | bytes 7274504 | tf_op jit(solution)/shard_map/ppermute | solution.py:42
  119.9 4.6 %tokens.1.refs_3_.mine_ref = bf16[1808,512]{1,0:T(8,128)(2,1)} custom-call(s32[2]{0:T(128)} %pad_add_fusion.at_ref, bf16[2272,256]{1,0:T(8,128)(2,1)} %join.25.refs_2_.refs_0_, bf16[2272,256]{1,0:T(8,128)(2,1)} %get-tuple-element.100.one_ref.refs_2_.refs_1_, bf16[1136,256]{1,0:T(8,128)(2,1)} %get-tuple-element.106.refs_2_.refs_1_, ...), custom_call_target="tpu_custom_call" | custom-call | bytes 7340032 | tf_op jit(solution)/shard_map/tokens/pallas_call | solution.py:457
  124.5 1.0 copy-done.6
  125.5 1.0 copy-done.7
  127.0 2.7 %relay.4 = (bf16[112,2368]{1,0:T(8,128)(2,1)}, bf16[112,2368]{1,0:T(8,128)(2,1)}) custom-call(bf16[224,2368]{1,0:T(8,128)(2,1)} %get-tuple-element.113.gp_ref.refs_6_, bf16[224,2368]{1,0:T(8,128)(2,1)} %get-tuple-element.114.gm_ref.refs_7_, bf16[112,2368]{1,0:T(8,128)(2,1)} %get-tuple-element.115.rp_ref, bf16[112,2368]{1,0:T(8,128)(2,1)} %get-tuple-element.116.rm_ref), custom_call_target="tpu_custom_call" | custom-call | bytes 3182592 | tf_op jit(solution)/shard_map/relay/pallas_call | solution.py:260
  129.7 2.7 %collective-permute-start.32 = (bf16[112,2368]{1,0:T(8,128)(2,1)}, bf16[112,2368]{1,0:T(8,128)(2,1)S(1)}, u32[]{:S(2)}, u32[]{:S(2)}) collective-permute-start(bf16[112,2368]{1,0:T(8,128)(2,1)} %get-tuple-element.136), channel_id=1, source_target_pairs={{0,96},{32,0},{64,32},{96,64},{1,97},{33,1},{65,33},{97,65},{2,98}... | collective-permute-start | bytes 1591304 | tf_op jit(solution)/shard_map/ppermute | solution.py:42
  132.4 1.5 copy-done.29
  133.8 19.6 %update.5 = (bf16[224,2368]{1,0:T(8,128)(2,1)}, bf16[224,2368]{1,0:T(8,128)(2,1)}, bf16[112,2368]{1,0:T(8,128)(2,1)}, bf16[112,2368]{1,0:T(8,128)(2,1)}, bf16[224,2368]{1,0:T(8,128)(2,1)}) custom-call(s32[4]{0:T(128)} %and_select_fusion.block_ref, bf16[2272,256]{1,0:T(8,128)(2,1)} %join.25.refs_2_.refs_0_, ...), custom_call_target="tpu_custom_call" | custom-call | flops 8690597888 | bytes 17612800 | tf_op jit(solution)/shard_map/update/pallas_call | solution.py:232
  153.5 2.7 %collective-permute-start.27 = (bf16[224,2368]{1,0:T(8,128)(2,1)}, bf16[224,2368]{1,0:T(8,128)(2,1)S(1)}, u32[]{:S(2)}, u32[]{:S(2)}) collective-permute-start(bf16[224,2368]{1,0:T(8,128)(2,1)} %get-tuple-element.121), channel_id=1, source_target_pairs={{0,96},{32,0},{64,32},{96,64},{1,97},{33,1},{65,33},{97,65},{2,98}... | collective-permute-start | bytes 3182600 | tf_op jit(solution)/shard_map/ppermute | solution.py:42
  157.2 5.9 %up_sums.1 = (f32[224,2368]{1,0:T(8,128)}, bf16[224,2368]{1,0:T(8,128)(2,1)}) custom-call(s32[1]{0:T(128)} %bitcast.13.mine_ref, bf16[224,2368]{1,0:T(8,128)(2,1)} %get-tuple-element.84.refs_3_.refs_0_, bf16[224,2368]{1,0:T(8,128)(2,1)} %get-tuple-element.93.gp_ref.refs_1_, bf16[224,2368]{1,0:T(8,128)(2,1)} %get-tuple-element.94.gm_ref.refs_2_, ...), custom_call_target="tpu_custom_call" | custom-call | tf_op jit(solution)/shard_map/up_sums/pallas_call | solution.py:383
  163.8 17.6 %hidden.1.refs_2_ = bf16[1184,512]{1,0:T(8,128)(2,1)} custom-call(s32[1]{0:T(128)} %bitcast.c_ref, bf16[1808,512]{1,0:T(8,128)(2,1)} %tokens.1.refs_3_.mine_ref, bf16[1808,512]{1,0:T(8,128)(2,1)} %collective-permute-done.20.other_ref, bf16[1184,3584]{1,0:T(8,128)(2,1)} %bitcast.20, bf16[1184,3584]{1,0:T(8,128)(2,1)} %bitcast.19, ...), custom_call_target="tpu_custom_call" | custom-call | flops 11173625856 | bytes 26705920 | tf_op jit(solution)/shard_map/hidden/pallas_call | solution.py:505
  181.4 1.0 copy-done.4
  182.3 1.0 copy-done.5
  183.3 2.6 %relay.5 = (bf16[112,2368]{1,0:T(8,128)(2,1)}, bf16[112,2368]{1,0:T(8,128)(2,1)}) custom-call(bf16[224,2368]{1,0:T(8,128)(2,1)} %get-tuple-element.122.gp_ref, bf16[224,2368]{1,0:T(8,128)(2,1)} %get-tuple-element.123.gm_ref, bf16[112,2368]{1,0:T(8,128)(2,1)} %get-tuple-element.124.rp_ref, bf16[112,2368]{1,0:T(8,128)(2,1)} %get-tuple-element.125.rm_ref), custom_call_target="tpu_custom_call" | custom-call | bytes 3182592 | tf_op jit(solution)/shard_map/relay/pallas_call | solution.py:260
  186.0 2.7 %collective-permute-start.29 = (bf16[112,2368]{1,0:T(8,128)(2,1)}, bf16[112,2368]{1,0:T(8,128)(2,1)S(1)}, u32[]{:S(2)}, u32[]{:S(2)}) collective-permute-start(bf16[112,2368]{1,0:T(8,128)(2,1)} %get-tuple-element.129), channel_id=1, source_target_pairs={{0,96},{32,0},{64,32},{96,64},{1,97},{33,1},{65,33},{97,65},{2,98}... | collective-permute-start | bytes 1591304 | tf_op jit(solution)/shard_map/ppermute | solution.py:42
  188.7 4.0 %gate_early.1 = (f32[224,1184]{1,0:T(8,128)}, f32[224,1184]{1,0:T(8,128)}) custom-call(s32[1]{0:T(128)} %bitcast.c_ref, bf16[448,1184]{1,0:T(8,128)(2,1)} %get-tuple-element.119.held_ref, bf16[224,2368]{1,0:T(8,128)(2,1)} %get-tuple-element.118.refs_0_.own_ref.refs_2_, bf16[224,2368]{1,0:T(8,128)(2,1)} %get-tuple-element.122.gp_ref, ...), custom_call_target="tpu_custom_call" | custom-call | tf_op jit(solution)/shard_map/gate_early/pallas_call | solution.py:322
  192.6 1.0 copy-done.14
  193.6 3.3 %up_sum.1 = (f32[224,1184]{1,0:T(8,128)}, bf16[224,1184]{1,0:T(8,128)(2,1)}) custom-call(f32[224,2368]{1,0:T(8,128)} %get-tuple-element.139.keep_ref, bf16[224,2368]{1,0:T(8,128)(2,1)} %join.37.sent_ref), custom_call_target="tpu_custom_call" | custom-call | tf_op jit(solution)/shard_map/up_sum/pallas_call | solution.py:396
  196.9 2.0 collective-permute-start.34
  198.9 1.0 collective-permute-done.28.refs_0_
  201.5 3.1 %gate_late.1 = (bf16[224,1184]{1,0:T(8,128)(2,1)}, bf16[224,1184]{1,0:T(8,128)(2,1)}) custom-call(f32[224,1184]{1,0:T(8,128)} %get-tuple-element.127.refs_2_.near_ref.refs_1_, f32[224,1184]{1,0:T(8,128)} %get-tuple-element.128.far_ref, bf16[112,2368]{1,0:T(8,128)(2,1)} %get-tuple-element.130.fp_ref, bf16[112,2368]{1,0:T(8,128)(2,1)} %get-tuple-element.131.fm_ref), custom_call_target="tpu_custom_call" | custom-call | tf_op jit(solution)/shard_map/gate_late/pallas_call | solution.py:342
  204.6 2.3 %collective-permute-start.30 = (bf16[224,1184]{1,0:T(8,128)(2,1)}, bf16[224,1184]{1,0:T(8,128)(2,1)S(1)}, u32[]{:S(2)}, u32[]{:S(2)}) collective-permute-start(bf16[224,1184]{1,0:T(8,128)(2,1)} %get-tuple-element.133), channel_id=1, source_target_pairs={{0,1},{1,0},{2,3},{3,2},{4,5},{5,4},{6,7},{7,6},{8,9},{9,8},{10,11... | collective-permute-start | bytes 1591304 | tf_op jit(solution)/shard_map/ppermute | solution.py:42
  207.8 3.1 %renew.1 = bf16[448,1184]{1,0:T(8,128)(2,1)} custom-call(s32[1]{0:T(128)} %bitcast.c_ref, bf16[448,1184]{1,0:T(8,128)(2,1)} %get-tuple-element.134.held_ref, f32[224,1184]{1,0:T(8,128)} %get-tuple-element.141.near_ref, bf16[224,1184]{1,0:T(8,128)(2,1)} %copy-done.27), custom_call_target="tpu_custom_call" | custom-call | tf_op jit(solution)/shard_map/renew/pallas_call | solution.py:423
  211.7 2.7 %gate_rows.1 = bf16[448,1184]{1,0:T(8,128)(2,1)} custom-call(s32[1]{0:T(128)} %bitcast.c_ref, bf16[448,1184]{1,0:T(8,128)(2,1)} %get-tuple-element.119.held_ref, bf16[224,1184]{1,0:T(8,128)(2,1)} %get-tuple-element.132.near_ref, bf16[224,1184]{1,0:T(8,128)(2,1)} %copy-done.26), custom_call_target="tpu_custom_call" | custom-call | tf_op jit(solution)/shard_map/gate_rows/pallas_call | solution.py:360
  (113 shorter events, 12.5 us)
Async XLA Ops:
  0.6 20.9 %collective-permute-start.4 = (bf16[4,1184,256]{2,1,0:T(8,128)(2,1)}, bf16[4,1184,256]{2,1,0:T(8,128)(2,1)}, u32[]{:S(2)}, u32[]{:S(2)}) collective-permute-start(bf16[4,1184,256]{2,1,0:T(8,128)(2,1)} %bitcast.21), channel_id=1, source_target_pairs={{0,1},{1,0},{2,3},{3,2},{4,5},{5,4},{6,7},{7,6},{8,9},{9,8},{10,11... | collective-permute-start | bytes 7274504 | tf_op jit(solution)/shard_map/ppermute | solution.py:42
  5.2 20.8 %collective-permute-start = (bf16[1376,256]{1,0:T(8,128)(2,1)}, bf16[1376,256]{1,0:T(8,128)(2,1)S(1)}, u32[]{:S(2)}, u32[]{:S(2)}) collective-permute-start(bf16[1376,256]{1,0:T(8,128)(2,1)} %get-tuple-element.74.all_ref), channel_id=1, source_target_pairs={{0,2},{2,0},{1,3},{3,1},{4,6},{6,4},{5,7},{7,5},{8,10},{10,8},{9,1... | collective-permute-start | bytes 2113544 | tf_op jit(solution)/shard_map/ppermute | solution.py:42
  8.2 13.3 %collective-permute-start.2 = (bf16[896,256]{1,0:T(8,128)(2,1)}, bf16[896,256]{1,0:T(8,128)(2,1)}, u32[]{:S(2)}, u32[]{:S(2)}) collective-permute-start(bf16[896,256]{1,0:T(8,128)(2,1)} %get-tuple-element.75.refs_0_), channel_id=1, source_target_pairs={{0,4},{4,8},{8,12},{12,0},{1,5},{5,9},{9,13},{13,1},{2,6},{6,10},{... | collective-permute-start | bytes 1376264 | tf_op jit(solution)/shard_map/ppermute | solution.py:42
  9.4 12.1 %collective-permute-start.3 = (bf16[896,256]{1,0:T(8,128)(2,1)}, bf16[896,256]{1,0:T(8,128)(2,1)}, u32[]{:S(2)}, u32[]{:S(2)}) collective-permute-start(bf16[896,256]{1,0:T(8,128)(2,1)} %get-tuple-element.75.refs_0_), channel_id=1, source_target_pairs={{0,12},{4,0},{8,4},{12,8},{1,13},{5,1},{9,5},{13,9},{2,14},{6,2},{... | collective-permute-start | bytes 1376264 | tf_op jit(solution)/shard_map/ppermute | solution.py:42
  23.4 7.4 %collective-permute-start.5 = (bf16[448,256]{1,0:T(8,128)(2,1)}, bf16[448,256]{1,0:T(8,128)(2,1)S(1)}, u32[]{:S(2)}, u32[]{:S(2)}) collective-permute-start(bf16[448,256]{1,0:T(8,128)(2,1)} %get-tuple-element.78), channel_id=1, source_target_pairs={{0,4},{4,8},{8,12},{12,0},{1,5},{5,9},{9,13},{13,1},{2,6},{6,10},{... | collective-permute-start | bytes 688136 | tf_op jit(solution)/shard_map/ppermute | solution.py:42
  24.3 6.5 %collective-permute-start.6 = (bf16[448,256]{1,0:T(8,128)(2,1)}, bf16[448,256]{1,0:T(8,128)(2,1)S(1)}, u32[]{:S(2)}, u32[]{:S(2)}) collective-permute-start(bf16[448,256]{1,0:T(8,128)(2,1)} %get-tuple-element.79), channel_id=1, source_target_pairs={{0,12},{4,0},{8,4},{12,8},{1,13},{5,1},{9,5},{13,9},{2,14},{6,2},{... | collective-permute-start | bytes 688136 | tf_op jit(solution)/shard_map/ppermute | solution.py:42
  26.1 0.9 copy-start.1
  26.9 7.9 %copy-start.30 = (s32[4]{0:T(128)S(1)}, s32[4]{0:T(128)}, u32[]{:S(2)}) copy-start(s32[4]{0:T(128)} %constant.45) | copy-start | bytes 52
  26.9 8.5 %copy-start.22 = (bf16[896,256]{1,0:T(8,128)(2,1)S(1)}, bf16[896,256]{1,0:T(8,128)(2,1)}, u32[]{:S(2)}) copy-start(bf16[896,256]{1,0:T(8,128)(2,1)} %join.19.s_ref) | copy-start | bytes 1376260
  26.9 23.8 %collective-permute-start.9 = (bf16[896,256]{1,0:T(8,128)(2,1)}, bf16[896,256]{1,0:T(8,128)(2,1)S(1)}, u32[]{:S(2)}, u32[]{:S(2)}) collective-permute-start(bf16[896,256]{1,0:T(8,128)(2,1)} %join.19.s_ref), channel_id=1, source_target_pairs={{18,16},{16,2},{2,18},{19,17},{17,3},{3,19},{22,20},{20,6},{6,22},... | collective-permute-start | bytes 1376264 | tf_op jit(solution)/shard_map/ppermute | solution.py:542
  32.2 20.8 %collective-permute-start.7 = (bf16[1376,256]{1,0:T(8,128)(2,1)}, bf16[1376,256]{1,0:T(8,128)(2,1)S(1)}, u32[]{:S(2)}, u32[]{:S(2)}) collective-permute-start(bf16[1376,256]{1,0:T(8,128)(2,1)} %join.22.refs_7_.refs_0_.refs_5_), channel_id=1, source_target_pairs={{0,4},{4,8},{8,12},{12,0},{1,5},{5,9},{9,13},{13,1},{2,6},{6,10},{... | collective-permute-start | bytes 2113544 | tf_op jit(solution)/shard_map/ppermute | solution.py:42
  32.2 20.8 %collective-permute-start.8 = (bf16[1376,256]{1,0:T(8,128)(2,1)}, bf16[1376,256]{1,0:T(8,128)(2,1)S(1)}, u32[]{:S(2)}, u32[]{:S(2)}) collective-permute-start(bf16[1376,256]{1,0:T(8,128)(2,1)} %join.22.refs_7_.refs_0_.refs_5_), channel_id=1, source_target_pairs={{0,12},{4,0},{8,4},{12,8},{1,13},{5,1},{9,5},{13,9},{2,14},{6,2},{... | collective-permute-start | bytes 2113544 | tf_op jit(solution)/shard_map/ppermute | solution.py:42
  35.4 26.7 %collective-permute-start.1 = (bf16[896,256]{1,0:T(8,128)(2,1)S(1)}, bf16[896,256]{1,0:T(8,128)(2,1)}, u32[]{:S(2)}, u32[]{:S(2)}) collective-permute-start(bf16[896,256]{1,0:T(8,128)(2,1)S(1)} %copy-done.22), channel_id=1, source_target_pairs={{16,0},{2,16},{0,2},{17,1},{3,17},{1,3},{20,4},{6,20},{4,6},{21,5}... | collective-permute-start | bytes 1376264 | tf_op jit(solution)/shard_map/ppermute | solution.py:542
  49.0 25.9 %collective-permute-start.14 = (bf16[224,2368]{1,0:T(8,128)(2,1)}, bf16[224,2368]{1,0:T(8,128)(2,1)S(1)}, u32[]{:S(2)}, u32[]{:S(2)}) collective-permute-start(bf16[224,2368]{1,0:T(8,128)(2,1)} %get-tuple-element.91), channel_id=1, source_target_pairs={{0,32},{32,64},{64,96},{96,0},{1,33},{33,65},{65,97},{97,1},{2,34}... | collective-permute-start | bytes 3182600 | tf_op jit(solution)/shard_map/ppermute | solution.py:42
  50.8 2.2 %copy-start.23 = (bf16[896,256]{1,0:T(8,128)(2,1)}, bf16[896,256]{1,0:T(8,128)(2,1)S(1)}, u32[]{:S(2)}) copy-start(bf16[896,256]{1,0:T(8,128)(2,1)S(1)} %collective-permute-done.9.refs_2_) | copy-start | bytes 1376260
  50.8 24.2 %collective-permute-start.15 = (bf16[224,2368]{1,0:T(8,128)(2,1)}, bf16[224,2368]{1,0:T(8,128)(2,1)S(1)}, u32[]{:S(2)}, u32[]{:S(2)}) collective-permute-start(bf16[224,2368]{1,0:T(8,128)(2,1)} %get-tuple-element.92), channel_id=1, source_target_pairs={{0,96},{32,0},{64,32},{96,64},{1,97},{33,1},{65,33},{97,65},{2,98}... | collective-permute-start | bytes 3182600 | tf_op jit(solution)/shard_map/ppermute | solution.py:42
  53.0 0.9 copy-start.2
  53.0 1.1 copy-start.12
  56.1 9.6 %collective-permute-start.10 = (bf16[688,256]{1,0:T(8,128)(2,1)}, bf16[688,256]{1,0:T(8,128)(2,1)S(1)}, u32[]{:S(2)}, u32[]{:S(2)}) collective-permute-start(bf16[688,256]{1,0:T(8,128)(2,1)} %get-tuple-element.88), channel_id=1, source_target_pairs={{0,4},{4,8},{8,12},{12,0},{1,5},{5,9},{9,13},{13,1},{2,6},{6,10},{... | collective-permute-start | bytes 1056776 | tf_op jit(solution)/shard_map/ppermute | solution.py:42
  56.1 9.6 %collective-permute-start.11 = (bf16[688,256]{1,0:T(8,128)(2,1)}, bf16[688,256]{1,0:T(8,128)(2,1)S(1)}, u32[]{:S(2)}, u32[]{:S(2)}) collective-permute-start(bf16[688,256]{1,0:T(8,128)(2,1)} %get-tuple-element.89), channel_id=1, source_target_pairs={{0,12},{4,0},{8,4},{12,8},{1,13},{5,1},{9,5},{13,9},{2,14},{6,2},{... | collective-permute-start | bytes 1056776 | tf_op jit(solution)/shard_map/ppermute | solution.py:42
  64.7 59.8 %collective-permute-start.24 = (bf16[4,1184,256]{2,1,0:T(8,128)(2,1)}, bf16[4,1184,256]{2,1,0:T(8,128)(2,1)}, u32[]{:S(2)}, u32[]{:S(2)}) collective-permute-start(bf16[4,1184,256]{2,1,0:T(8,128)(2,1)} %join.32), channel_id=1, source_target_pairs={{0,16},{16,0},{1,17},{17,1},{2,18},{18,2},{3,19},{19,3},{4,20},{20... | collective-permute-start | bytes 7274504 | tf_op jit(solution)/shard_map/ppermute | solution.py:42
  65.7 0.7 copy-start.15
  66.5 0.7 copy-start.24
  67.2 26.7 %collective-permute-start.12 = (bf16[2272,256]{1,0:T(8,128)(2,1)}, bf16[2272,256]{1,0:T(8,128)(2,1)S(1)}, u32[]{:S(2)}, u32[]{:S(2)}) collective-permute-start(bf16[2272,256]{1,0:T(8,128)(2,1)} %join.25.refs_2_.refs_0_), channel_id=1, source_target_pairs={{0,4},{4,8},{8,12},{12,0},{1,5},{5,9},{9,13},{13,1},{2,6},{6,10},{... | collective-permute-start | bytes 3489800 | tf_op jit(solution)/shard_map/ppermute | solution.py:42
  67.2 26.7 %collective-permute-start.13 = (bf16[2272,256]{1,0:T(8,128)(2,1)}, bf16[2272,256]{1,0:T(8,128)(2,1)S(1)}, u32[]{:S(2)}, u32[]{:S(2)}) collective-permute-start(bf16[2272,256]{1,0:T(8,128)(2,1)} %join.25.refs_2_.refs_0_), channel_id=1, source_target_pairs={{0,12},{4,0},{8,4},{12,8},{1,13},{5,1},{9,5},{13,9},{2,14},{6,2},{... | collective-permute-start | bytes 3489800 | tf_op jit(solution)/shard_map/ppermute | solution.py:42
  74.9 1.0 copy-start.8
  75.9 1.0 copy-start.9
  79.6 15.6 %collective-permute-start.18 = (bf16[112,2368]{1,0:T(8,128)(2,1)}, bf16[112,2368]{1,0:T(8,128)(2,1)S(1)}, u32[]{:S(2)}, u32[]{:S(2)}) collective-permute-start(bf16[112,2368]{1,0:T(8,128)(2,1)} %get-tuple-element.97.refs_7_.refs_2_), channel_id=1, source_target_pairs={{0,32},{32,64},{64,96},{96,0},{1,33},{33,65},{65,97},{97,1},{2,34}... | collective-permute-start | bytes 1591304 | tf_op jit(solution)/shard_map/ppermute | solution.py:42
  79.6 15.6 %collective-permute-start.19 = (bf16[112,2368]{1,0:T(8,128)(2,1)}, bf16[112,2368]{1,0:T(8,128)(2,1)S(1)}, u32[]{:S(2)}, u32[]{:S(2)}) collective-permute-start(bf16[112,2368]{1,0:T(8,128)(2,1)} %get-tuple-element.104), channel_id=1, source_target_pairs={{0,96},{32,0},{64,32},{96,64},{1,97},{33,1},{65,33},{97,65},{2,98}... | collective-permute-start | bytes 1591304 | tf_op jit(solution)/shard_map/ppermute | solution.py:42
  93.9 1.0 copy-start
  93.9 1.4 copy-start.3
  95.2 0.8 copy-start.11
  95.3 1.0 copy-start.21
  96.3 7.6 %copy-start.10 = (bf16[256,4,1184]{0,2,1:T(8,128)(2,1)S(1)}, bf16[256,4,1184]{0,2,1:T(8,128)(2,1)}, u32[]{:S(2)}) copy-start(bf16[256,4,1184]{0,2,1:T(8,128)(2,1)} %param.14) | copy-start | bytes 7274500
  96.3 28.2 %collective-permute-start.22 = (bf16[224,2368]{1,0:T(8,128)(2,1)}, bf16[224,2368]{1,0:T(8,128)(2,1)S(1)}, u32[]{:S(2)}, u32[]{:S(2)}) collective-permute-start(bf16[224,2368]{1,0:T(8,128)(2,1)} %get-tuple-element.110), channel_id=1, source_target_pairs={{0,32},{32,64},{64,96},{96,0},{1,33},{33,65},{65,97},{97,1},{2,34}... | collective-permute-start | bytes 3182600 | tf_op jit(solution)/shard_map/ppermute | solution.py:42
  96.3 28.2 %collective-permute-start.23 = (bf16[224,2368]{1,0:T(8,128)(2,1)}, bf16[224,2368]{1,0:T(8,128)(2,1)S(1)}, u32[]{:S(2)}, u32[]{:S(2)}) collective-permute-start(bf16[224,2368]{1,0:T(8,128)(2,1)} %get-tuple-element.111), channel_id=1, source_target_pairs={{0,96},{32,0},{64,32},{96,64},{1,97},{33,1},{65,33},{97,65},{2,98}... | collective-permute-start | bytes 3182600 | tf_op jit(solution)/shard_map/ppermute | solution.py:42
  101.2 11.8 %collective-permute-start.16 = (bf16[1136,256]{1,0:T(8,128)(2,1)}, bf16[1136,256]{1,0:T(8,128)(2,1)S(1)}, u32[]{:S(2)}, u32[]{:S(2)}) collective-permute-start(bf16[1136,256]{1,0:T(8,128)(2,1)} %get-tuple-element.102), channel_id=1, source_target_pairs={{0,4},{4,8},{8,12},{12,0},{1,5},{5,9},{9,13},{13,1},{2,6},{6,10},{... | collective-permute-start | bytes 1744904 | tf_op jit(solution)/shard_map/ppermute | solution.py:42
  101.8 11.2 %collective-permute-start.17 = (bf16[1136,256]{1,0:T(8,128)(2,1)}, bf16[1136,256]{1,0:T(8,128)(2,1)S(1)}, u32[]{:S(2)}, u32[]{:S(2)}) collective-permute-start(bf16[1136,256]{1,0:T(8,128)(2,1)} %get-tuple-element.103), channel_id=1, source_target_pairs={{0,12},{4,0},{8,4},{12,8},{1,13},{5,1},{9,5},{13,9},{2,14},{6,2},{... | collective-permute-start | bytes 1744904 | tf_op jit(solution)/shard_map/ppermute | solution.py:42
  113.0 0.9 copy-start.13
  113.9 0.8 copy-start.16
  114.7 17.6 %collective-permute-start.21 = (bf16[4,1184,256]{2,1,0:T(8,128)(2,1)}, bf16[4,1184,256]{2,1,0:T(8,128)(2,1)S(1)}, u32[]{:S(2)}, u32[]{:S(2)}) collective-permute-start(bf16[4,1184,256]{2,1,0:T(8,128)(2,1)} %join.30), channel_id=1, source_target_pairs={{0,1},{1,0},{2,3},{3,2},{4,5},{5,4},{6,7},{7,6},{8,9},{9,8},{10,11... | collective-permute-start | bytes 7274504 | tf_op jit(solution)/shard_map/ppermute | solution.py:42
  124.5 1.0 copy-start.6
  125.5 1.0 copy-start.7
  126.5 5.9 %collective-permute-start.25 = (bf16[4,1184,256]{2,1,0:T(8,128)(2,1)}, bf16[4,1184,256]{2,1,0:T(8,128)(2,1)}, u32[]{:S(2)}, u32[]{:S(2)}) collective-permute-start(bf16[4,1184,256]{2,1,0:T(8,128)(2,1)} %get-tuple-element.112.refs_7_), channel_id=1, source_target_pairs={{0,1},{1,0},{2,3},{3,2},{4,5},{5,4},{6,7},{7,6},{8,9},{9,8},{10,11... | collective-permute-start | bytes 7274504 | tf_op jit(solution)/shard_map/ppermute | solution.py:42
  126.5 37.3 %collective-permute-start.20 = (bf16[1808,512]{1,0:T(8,128)(2,1)}, bf16[1808,512]{1,0:T(8,128)(2,1)}, u32[]{:S(2)}, u32[]{:S(2)}) collective-permute-start(bf16[1808,512]{1,0:T(8,128)(2,1)} %tokens.1.refs_3_.mine_ref), channel_id=1, source_target_pairs={{0,1},{1,0},{2,3},{3,2},{4,5},{5,4},{6,7},{7,6},{8,9},{9,8},{10,11... | collective-permute-start | bytes 5554184 | tf_op jit(solution)/shard_map/ppermute | solution.py:42
  129.7 26.5 %collective-permute-start.31 = (bf16[112,2368]{1,0:T(8,128)(2,1)}, bf16[112,2368]{1,0:T(8,128)(2,1)S(1)}, u32[]{:S(2)}, u32[]{:S(2)}) collective-permute-start(bf16[112,2368]{1,0:T(8,128)(2,1)} %get-tuple-element.117.refs_9_), channel_id=1, source_target_pairs={{0,32},{32,64},{64,96},{96,0},{1,33},{33,65},{65,97},{97,1},{2,34}... | collective-permute-start | bytes 1591304 | tf_op jit(solution)/shard_map/ppermute | solution.py:42
  129.7 26.5 %collective-permute-start.32 = (bf16[112,2368]{1,0:T(8,128)(2,1)}, bf16[112,2368]{1,0:T(8,128)(2,1)S(1)}, u32[]{:S(2)}, u32[]{:S(2)}) collective-permute-start(bf16[112,2368]{1,0:T(8,128)(2,1)} %get-tuple-element.136), channel_id=1, source_target_pairs={{0,96},{32,0},{64,32},{96,64},{1,97},{33,1},{65,33},{97,65},{2,98}... | collective-permute-start | bytes 1591304 | tf_op jit(solution)/shard_map/ppermute | solution.py:42
  132.4 1.5 copy-start.29
  153.5 27.9 %collective-permute-start.26 = (bf16[224,2368]{1,0:T(8,128)(2,1)}, bf16[224,2368]{1,0:T(8,128)(2,1)S(1)}, u32[]{:S(2)}, u32[]{:S(2)}) collective-permute-start(bf16[224,2368]{1,0:T(8,128)(2,1)} %get-tuple-element.120), channel_id=1, source_target_pairs={{0,32},{32,64},{64,96},{96,0},{1,33},{33,65},{65,97},{97,1},{2,34}... | collective-permute-start | bytes 3182600 | tf_op jit(solution)/shard_map/ppermute | solution.py:42
  153.5 27.8 %collective-permute-start.27 = (bf16[224,2368]{1,0:T(8,128)(2,1)}, bf16[224,2368]{1,0:T(8,128)(2,1)S(1)}, u32[]{:S(2)}, u32[]{:S(2)}) collective-permute-start(bf16[224,2368]{1,0:T(8,128)(2,1)} %get-tuple-element.121), channel_id=1, source_target_pairs={{0,96},{32,0},{64,32},{96,64},{1,97},{33,1},{65,33},{97,65},{2,98}... | collective-permute-start | bytes 3182600 | tf_op jit(solution)/shard_map/ppermute | solution.py:42
  156.2 0.8 copy-start.17
  156.2 1.0 copy-start.18
  163.2 29.5 %collective-permute-start.33 = (bf16[224,2368]{1,0:T(8,128)(2,1)}, bf16[224,2368]{1,0:T(8,128)(2,1)S(1)}, u32[]{:S(2)}, u32[]{:S(2)}) collective-permute-start(bf16[224,2368]{1,0:T(8,128)(2,1)} %get-tuple-element.140), channel_id=1, source_target_pairs={{0,16},{16,0},{1,17},{17,1},{2,18},{18,2},{3,19},{19,3},{4,20},{20... | collective-permute-start | bytes 3182600 | tf_op jit(solution)/shard_map/ppermute | solution.py:42
  181.4 1.0 copy-start.4
  182.3 1.0 copy-start.5
  186.0 13.9 %collective-permute-start.28 = (bf16[112,2368]{1,0:T(8,128)(2,1)}, bf16[112,2368]{1,0:T(8,128)(2,1)S(1)}, u32[]{:S(2)}, u32[]{:S(2)}) collective-permute-start(bf16[112,2368]{1,0:T(8,128)(2,1)} %get-tuple-element.126.refs_0_), channel_id=1, source_target_pairs={{0,32},{32,64},{64,96},{96,0},{1,33},{33,65},{65,97},{97,1},{2,34}... | collective-permute-start | bytes 1591304 | tf_op jit(solution)/shard_map/ppermute | solution.py:42
  186.0 13.9 %collective-permute-start.29 = (bf16[112,2368]{1,0:T(8,128)(2,1)}, bf16[112,2368]{1,0:T(8,128)(2,1)S(1)}, u32[]{:S(2)}, u32[]{:S(2)}) collective-permute-start(bf16[112,2368]{1,0:T(8,128)(2,1)} %get-tuple-element.129), channel_id=1, source_target_pairs={{0,96},{32,0},{64,32},{96,64},{1,97},{33,1},{65,33},{97,65},{2,98}... | collective-permute-start | bytes 1591304 | tf_op jit(solution)/shard_map/ppermute | solution.py:42
  192.6 1.0 copy-start.14
  196.9 10.0 %collective-permute-start.34 = (bf16[224,1184]{1,0:T(8,128)(2,1)}, bf16[224,1184]{1,0:T(8,128)(2,1)S(1)}, u32[]{:S(2)}, u32[]{:S(2)}) collective-permute-start(bf16[224,1184]{1,0:T(8,128)(2,1)} %get-tuple-element.142), channel_id=1, source_target_pairs={{0,1},{1,0},{2,3},{3,2},{4,5},{5,4},{6,7},{7,6},{8,9},{9,8},{10,11... | collective-permute-start | bytes 1591304 | tf_op jit(solution)/shard_map/ppermute | solution.py:42
  199.9 0.8 copy-start.19
  200.7 0.8 copy-start.20
  204.6 6.2 %collective-permute-start.30 = (bf16[224,1184]{1,0:T(8,128)(2,1)}, bf16[224,1184]{1,0:T(8,128)(2,1)S(1)}, u32[]{:S(2)}, u32[]{:S(2)}) collective-permute-start(bf16[224,1184]{1,0:T(8,128)(2,1)} %get-tuple-element.133), channel_id=1, source_target_pairs={{0,1},{1,0},{2,3},{3,2},{4,5},{5,4},{6,7},{7,6},{8,9},{9,8},{10,11... | collective-permute-start | bytes 1591304 | tf_op jit(solution)/shard_map/ppermute | solution.py:42
  206.9 0.8 copy-start.27
  210.8 0.8 copy-start.26
  (2 other events, 1.4 us)
where the time goes:
time: 215 us; the launch traced here: 214 us
  Pallas kernels  107 us (50%)
  starting transfers between devices  52.7 us (25%)
  local copies, waits for them, and re-layouts  32.7 us (15%)
  waiting for transfers between devices  20.6 us (10%)
    ppermute x33, starting transfers between devices, swap(): return lax.ppermute(v, axis, [(i, (i + shift) % n) for i in range(n)])  49.5 us
    pallas_call x3, Pallas kernels, update(): _call(functools.partial(_update_kernel, coeff, slabs, d, q - CUT, len(sec...  42.5 us
    unnamed x66, local copies, waits for them, and re-layouts  29.5 us
    ppermute x33, waiting for transfers between devices, swap(): return lax.ppermute(v, axis, [(i, (i + shift) % n) for i in range(n)])  20.6 us
    pallas_call x1, Pallas kernels, hidden_of(): _call(_hidden_kernel, 'hidden', flops=4 * q * t * (d + rank * m), moved=2...  17.6 us
    pallas_call x3, Pallas kernels, relay(): _call(_relay_kernel, 'relay', grid=(1,), moved=12 * rp.size, in_specs=[sp...  7.98 us
    pallas_call x3, Pallas kernels, halves(): _call(_halves_kernel, 'halves', grid=(1,), moved=8 * n * m, in_specs=[_at...  6.09 us
    pallas_call x1, Pallas kernels, up_sums(): _call(kernel, 'up_sums', in_specs=[SCALARS] + [FULL] * 10 + _any(len(afte...  5.93 us
  transfers between devices with their start and end apart: 35, of which 5 were waited for; matrix products, arithmetic and copies ran while one was open for 6% of the time, Pallas kernels for 48%

commit v1 on v0

--- a/solution.py
+++ b/solution.py
@@ -249,6 +249,9 @@
     return pl.BlockSpec(shape, lambda i: (row, 0))
 
 
+WIDE = 1280
+
+
 def _relay_kernel(gp_ref, gm_ref, rp_ref, rm_ref, *refs):
     ap_ref, am_ref = refs[-2:]
     ap_ref[...] = (rp_ref[...].astype(f32) + gp_ref[...].astype(f32)).astype(bf16)
@@ -256,11 +259,11 @@
 
 
 def relay(gp, gm, rp, rm, *after):
-    spec = _at(rp.shape)
+    spec = pl.BlockSpec((rp.shape[0], WIDE), lambda i: (0, i))
     return _call(
         _relay_kernel,
         "relay",
-        grid=(1,),
+        grid=(2,),
         moved=12 * rp.size,
         in_specs=[spec] * 4 + _any(len(after)),
         out_specs=[spec] * 2,
@@ -383,8 +386,9 @@
     return _call(
         kernel,
         "up_sums",
-        in_specs=[SCALARS] + [FULL] * 10 + _any(len(after)),
-        out_specs=[FULL] * 2,
+        grid=(2,),
+        in_specs=[SCALARS] + [pl.BlockSpec((p.shape[0], WIDE), lambda i: (0, i)) for p in (*parts_a, *parts_b)] + _any(len(after)),
+        out_specs=[pl.BlockSpec((shape[0], WIDE), lambda i: (0, i))] * 2,
         out_shape=[jax.ShapeDtypeStruct(shape, f32), jax.ShapeDtypeStruct(shape, bf16)],
     )(mine, *parts_a, *parts_b, *after)
 
@@ -568,11 +572,12 @@
     sg_x = (both, one, lo, hi, three)
     bg_c = swap(tie(bg, lo), "c")
     tok = tokens_of(jnp.stack([x, h]), sg_x, so_x, d, tok_t.shape[1], 2 * rank)
-    tok_c = swap(tok, "c")
     gp_b, gm_b, far_0 = join([gp_b, gm_b, far_0], tok)
     ap, am = relay(gp_b, gm_b, *ub[2:4])
     fp_b, fm_b = hop("z", ap, am)
     fars = [v for far in (far_0,) for v in (far, swap(far, "c"))]
+    tok = tie(tok, am)
+    tok_c = swap(tok, "c")
     gg = update(coeff, block, d, sg_x, [bg, bg_c, *fars], ap)
     fp_b, fm_b = join([fp_b, fm_b], gg[-1])
     gp_g, gm_g = hop("z", *gg[:2])

time: 215 us -> 213 us (level)
  transfers between devices with their start and end apart: 35 -> 35, of which waited for: 5 -> 6; matrix products, arithmetic and copies ran while one was open for 6% -> 6% of each run, Pallas kernels for 48% -> 48%
where the time goes in v1:
time: 213 us; the launch traced here: 212 us
  Pallas kernels  105 us (49%)
  starting transfers between devices  51.7 us (24%)
  local copies, waits for them, and re-layouts  32.2 us (15%)
  waiting for transfers between devices  20.9 us (10%)
    ppermute x33, starting transfers between devices, swap(): return lax.ppermute(v, axis, [(i, (i + shift) % n) for i in range(n)])  48.5 us
    pallas_call x3, Pallas kernels, update(): _call(functools.partial(_update_kernel, coeff, slabs, d, q - CUT, len(sec...  42.5 us
    unnamed x66, local copies, waits for them, and re-layouts  29 us
    ppermute x33, waiting for transfers between devices, swap(): return lax.ppermute(v, axis, [(i, (i + shift) % n) for i in range(n)])  20.9 us
    pallas_call x1, Pallas kernels, hidden_of(): _call(_hidden_kernel, 'hidden', flops=4 * q * t * (d + rank * m), moved=2...  17.6 us
    pallas_call x3, Pallas kernels, relay(): _call(_relay_kernel, 'relay', grid=(2,), moved=12 * rp.size, in_specs=[sp...  7.56 us
    pallas_call x3, Pallas kernels, halves(): _call(_halves_kernel, 'halves', grid=(1,), moved=8 * n * m, in_specs=[_at...  6.09 us
    pallas_call x1, Pallas kernels, up_sums(): _call(kernel, 'up_sums', grid=(2,), in_specs=[SCALARS] + [pl.BlockSpec((p...  5.25 us
  transfers between devices with their start and end apart: 35, of which 6 were waited for; matrix products, arithmetic and copies ran while one was open for 6% of the time, Pallas kernels for 48%

profile of v1, /device:TPU:1, one launch (start us, length us, event | category | flops | bytes accessed | tf_op | source)
XLA Modules:
  0.0 212.1 jit_solution(8684744114491312353)
XLA Ops:
  0.6 1.5 collective-permute-start.4
  2.1 3.1 %pack.1 = (bf16[896,256]{1,0:T(8,128)(2,1)}, bf16[896,256]{1,0:T(8,128)(2,1)}, bf16[1376,256]{1,0:T(8,128)(2,1)}) custom-call(bf16[224,512]{1,0:T(8,128)(2,1)} %bitcast.27, bf16[4,224,256]{2,1,0:T(8,128)(2,1)} %bitcast.25, bf16[4,224,256]{2,1,0:T(8,128)(2,1)} %bitcast.26, f32[1,256]{1,0:T(1,128)} %bitcast.28), custom_call_target="tpu_custom_call" | custom-call | flops 469762048 | bytes 1835008 | tf_op jit(solution)/shard_map/pack/pallas_call | solution.py:95
  5.2 3.0 %collective-permute-start = (bf16[1376,256]{1,0:T(8,128)(2,1)}, bf16[1376,256]{1,0:T(8,128)(2,1)S(1)}, u32[]{:S(2)}, u32[]{:S(2)}) collective-permute-start(bf16[1376,256]{1,0:T(8,128)(2,1)} %get-tuple-element.74.all_ref), channel_id=1, source_target_pairs={{0,2},{2,0},{1,3},{3,1},{4,6},{6,4},{5,7},{7,5},{8,10},{10,8},{9,1... | collective-permute-start | bytes 2113544 | tf_op jit(solution)/shard_map/ppermute | solution.py:42
  8.2 1.2 collective-permute-start.2
  9.4 1.5 collective-permute-start.3
  10.9 3.2 %constant_dynamic-slice_fusion = (bf16[448,1184]{0,1:T(8,128)(2,1)S(1)}, bf16[448,1184]{0,1:T(8,128)(2,1)S(1)}) fusion(bf16[3584,1184]{0,1:T(8,128)(2,1)} %param.11, s32[]{:T(128)S(6)} %select_n.11, bf16[3584,1184]{0,1:T(8,128)(2,1)} %param.10), kind=kLoop, calls=%fused_computation.5 | loop fusion | bytes 4243460 | tf_op jit(solution)/shard_map/dynamic_slice | solution.py:540
  14.1 1.6 copy.53.refs_3_
  15.7 1.5 copy.54.refs_4_
  17.2 4.4 %collective-permute-done.2.refs_0_ = bf16[896,256]{1,0:T(8,128)(2,1)} collective-permute-done((bf16[896,256]{1,0:T(8,128)(2,1)}, bf16[896,256]{1,0:T(8,128)(2,1)}, u32[]{:S(2)}, u32[]{:S(2)}) %collective-permute-start.2) | collective-permute-done | bytes 458784 | tf_op jit(solution)/shard_map/ppermute | solution.py:42
  21.6 1.8 halves.3
  23.4 0.9 collective-permute-start.5
  24.3 1.8 collective-permute-start.6
  26.1 0.9 copy-done.1
  27.8 3.0 %collective-permute-done.5.refs_0_ = bf16[448,256]{1,0:T(8,128)(2,1)S(1)} collective-permute-done((bf16[448,256]{1,0:T(8,128)(2,1)}, bf16[448,256]{1,0:T(8,128)(2,1)S(1)}, u32[]{:S(2)}, u32[]{:S(2)}) %collective-permute-start.5) | collective-permute-done | bytes 229408 | tf_op jit(solution)/shard_map/ppermute | solution.py:42
  32.2 2.7 %collective-permute-start.8 = (bf16[1376,256]{1,0:T(8,128)(2,1)}, bf16[1376,256]{1,0:T(8,128)(2,1)S(1)}, u32[]{:S(2)}, u32[]{:S(2)}) collective-permute-start(bf16[1376,256]{1,0:T(8,128)(2,1)} %join.23.refs_7_.refs_0_.refs_5_), channel_id=1, source_target_pairs={{0,12},{4,0},{8,4},{12,8},{1,13},{5,1},{9,5},{13,9},{2,14},{6,2},{... | collective-permute-start | bytes 2113544 | tf_op jit(solution)/shard_map/ppermute | solution.py:42
  35.4 2.4 %collective-permute-start.1 = (bf16[896,256]{1,0:T(8,128)(2,1)S(1)}, bf16[896,256]{1,0:T(8,128)(2,1)}, u32[]{:S(2)}, u32[]{:S(2)}) collective-permute-start(bf16[896,256]{1,0:T(8,128)(2,1)S(1)} %copy-done.22), channel_id=1, source_target_pairs={{16,0},{2,16},{0,2},{17,1},{3,17},{1,3},{20,4},{6,20},{4,6},{21,5}... | collective-permute-start | bytes 1376264 | tf_op jit(solution)/shard_map/ppermute | solution.py:546
  37.8 11.3 %update.3 = (bf16[224,2368]{1,0:T(8,128)(2,1)}, bf16[224,2368]{1,0:T(8,128)(2,1)}, bf16[112,2368]{1,0:T(8,128)(2,1)}, bf16[112,2368]{1,0:T(8,128)(2,1)}, bf16[224,2368]{1,0:T(8,128)(2,1)}) custom-call(s32[4]{0:T(128)} %and_select_fusion.block_ref, bf16[896,256]{1,0:T(8,128)(2,1)} %get-tuple-element.75.refs_0_, ...), custom_call_target="tpu_custom_call" | custom-call | flops 4345298944 | bytes 10928128 | tf_op jit(solution)/shard_map/update/pallas_call | solution.py:232
  49.0 1.7 collective-permute-start.14
  50.8 2.2 %collective-permute-start.15 = (bf16[224,2368]{1,0:T(8,128)(2,1)}, bf16[224,2368]{1,0:T(8,128)(2,1)S(1)}, u32[]{:S(2)}, u32[]{:S(2)}) collective-permute-start(bf16[224,2368]{1,0:T(8,128)(2,1)} %get-tuple-element.92), channel_id=1, source_target_pairs={{0,96},{32,0},{64,32},{96,64},{1,97},{33,1},{65,33},{97,65},{2,98}... | collective-permute-start | bytes 3182600 | tf_op jit(solution)/shard_map/ppermute | solution.py:42
  53.0 0.8 copy-done.2
  54.1 2.0 halves.4
  56.1 2.6 %collective-permute-start.11 = (bf16[688,256]{1,0:T(8,128)(2,1)}, bf16[688,256]{1,0:T(8,128)(2,1)S(1)}, u32[]{:S(2)}, u32[]{:S(2)}) collective-permute-start(bf16[688,256]{1,0:T(8,128)(2,1)} %get-tuple-element.89), channel_id=1, source_target_pairs={{0,12},{4,0},{8,4},{12,8},{1,13},{5,1},{9,5},{13,9},{2,14},{6,2},{... | collective-permute-start | bytes 1056776 | tf_op jit(solution)/shard_map/ppermute | solution.py:42
  58.8 3.3 %copy.81.refs_0_ = bf16[4,1184,256]{2,1,0:T(8,128)(2,1)} copy(bf16[4,1184,256]{2,1,0:T(8,128)(2,1)} %bitcast.14) | data formatting | bytes 4849664
  62.1 2.6 %pick.1.refs_2_.refs_0_.refs_1_ = bf16[2272,256]{1,0:T(8,128)(2,1)} custom-call(s32[1]{0:T(128)} %bitcast.3.y_ref, bf16[896,256]{1,0:T(8,128)(2,1)} %join.20.s_ref, bf16[896,256]{1,0:T(8,128)(2,1)} %collective-permute-done.1.pa_ref, bf16[896,256]{1,0:T(8,128)(2,1)} %get-tuple-element.85.pb_ref, bf16[1376,256]{1,0:T(8,128)(2,1)} %get-tuple-element.74.all_ref, ...), custom_call_target="tpu_custom_call" | custom-call | bytes 1835008 | tf_op jit(solution)/shard_map/pick/pallas_call | solution.py:127
  64.7 1.0 collective-permute-start.22
  67.2 2.7 %collective-permute-start.13 = (bf16[2272,256]{1,0:T(8,128)(2,1)}, bf16[2272,256]{1,0:T(8,128)(2,1)S(1)}, u32[]{:S(2)}, u32[]{:S(2)}) collective-permute-start(bf16[2272,256]{1,0:T(8,128)(2,1)} %join.26.refs_2_.refs_0_), channel_id=1, source_target_pairs={{0,12},{4,0},{8,4},{12,8},{1,13},{5,1},{9,5},{13,9},{2,14},{6,2},{... | collective-permute-start | bytes 3489800 | tf_op jit(solution)/shard_map/ppermute | solution.py:42
  69.9 5.0 %collective-permute-done.14.refs_0_ = bf16[224,2368]{1,0:T(8,128)(2,1)S(1)} collective-permute-done((bf16[224,2368]{1,0:T(8,128)(2,1)}, bf16[224,2368]{1,0:T(8,128)(2,1)S(1)}, u32[]{:S(2)}, u32[]{:S(2)}) %collective-permute-start.14) | collective-permute-done | bytes 1060896 | tf_op jit(solution)/shard_map/ppermute | solution.py:42
  74.9 1.0 copy-done.8
  75.9 1.0 copy-done.9
  76.9 2.5 %relay.3 = (bf16[112,2368]{1,0:T(8,128)(2,1)}, bf16[112,2368]{1,0:T(8,128)(2,1)}) custom-call(bf16[224,2368]{1,0:T(8,128)(2,1)} %get-tuple-element.93.gp_ref.refs_1_, bf16[224,2368]{1,0:T(8,128)(2,1)} %get-tuple-element.94.gm_ref.refs_2_, bf16[112,2368]{1,0:T(8,128)(2,1)} %get-tuple-element.95.rp_ref, bf16[112,2368]{1,0:T(8,128)(2,1)} %get-tuple-element.96.rm_ref), custom_call_target="tpu_custom_call" | custom-call | bytes 3182592 | tf_op jit(solution)/shard_map/relay/pallas_call | solution.py:263
  79.5 2.7 %collective-permute-start.19 = (bf16[112,2368]{1,0:T(8,128)(2,1)}, bf16[112,2368]{1,0:T(8,128)(2,1)S(1)}, u32[]{:S(2)}, u32[]{:S(2)}) collective-permute-start(bf16[112,2368]{1,0:T(8,128)(2,1)} %get-tuple-element.104), channel_id=1, source_target_pairs={{0,96},{32,0},{64,32},{96,64},{1,97},{33,1},{65,33},{97,65},{2,98}... | collective-permute-start | bytes 1591304 | tf_op jit(solution)/shard_map/ppermute | solution.py:42
  82.1 11.6 %update.4 = (bf16[224,2368]{1,0:T(8,128)(2,1)}, bf16[224,2368]{1,0:T(8,128)(2,1)}, bf16[112,2368]{1,0:T(8,128)(2,1)}, bf16[112,2368]{1,0:T(8,128)(2,1)}, bf16[224,2368]{1,0:T(8,128)(2,1)}) custom-call(s32[4]{0:T(128)} %and_select_fusion.block_ref, bf16[1376,256]{1,0:T(8,128)(2,1)} %join.23.refs_7_.refs_0_.refs_5_, ...), custom_call_target="tpu_custom_call" | custom-call | flops 4345298944 | bytes 10928128 | tf_op jit(solution)/shard_map/update/pallas_call | solution.py:232
  93.7 1.0 copy-done
  96.1 2.7 %collective-permute-start.21 = (bf16[224,2368]{1,0:T(8,128)(2,1)}, bf16[224,2368]{1,0:T(8,128)(2,1)S(1)}, u32[]{:S(2)}, u32[]{:S(2)}) collective-permute-start(bf16[224,2368]{1,0:T(8,128)(2,1)} %get-tuple-element.111), channel_id=1, source_target_pairs={{0,96},{32,0},{64,32},{96,64},{1,97},{33,1},{65,33},{97,65},{2,98}... | collective-permute-start | bytes 3182600 | tf_op jit(solution)/shard_map/ppermute | solution.py:42
  98.8 2.3 %halves.5 = (bf16[1136,256]{1,0:T(8,128)(2,1)}, bf16[1136,256]{1,0:T(8,128)(2,1)}) custom-call(bf16[2272,256]{1,0:T(8,128)(2,1)} %get-tuple-element.100.one_ref.refs_2_.refs_1_, bf16[2272,256]{1,0:T(8,128)(2,1)} %get-tuple-element.101.three_ref.refs_4_), custom_call_target="tpu_custom_call" | custom-call | bytes 2326528 | tf_op jit(solution)/shard_map/halves/pallas_call | solution.py:282
  101.7 2.1 collective-permute-start.17
  103.8 1.5 copy.86.refs_0_
  105.8 7.1 %collective-permute-done.16.refs_0_ = bf16[1136,256]{1,0:T(8,128)(2,1)S(1)} collective-permute-done((bf16[1136,256]{1,0:T(8,128)(2,1)}, bf16[1136,256]{1,0:T(8,128)(2,1)S(1)}, u32[]{:S(2)}, u32[]{:S(2)}) %collective-permute-start.16) | collective-permute-done | bytes 581664 | tf_op jit(solution)/shard_map/ppermute | solution.py:42
  112.9 0.8 copy-done.13
  113.8 0.8 copy-done.16
  114.6 5.2 %collective-permute-start.24 = (bf16[4,1184,256]{2,1,0:T(8,128)(2,1)}, bf16[4,1184,256]{2,1,0:T(8,128)(2,1)S(1)}, u32[]{:S(2)}, u32[]{:S(2)}) collective-permute-start(bf16[4,1184,256]{2,1,0:T(8,128)(2,1)} %join.35), channel_id=1, source_target_pairs={{0,1},{1,0},{2,3},{3,2},{4,5},{5,4},{6,7},{7,6},{8,9},{9,8},{10,11... | collective-permute-start | bytes 7274504 | tf_op jit(solution)/shard_map/ppermute | solution.py:42
  119.8 4.6 %tokens.1.refs_3_.refs_0_ = bf16[1808,512]{1,0:T(8,128)(2,1)} custom-call(s32[2]{0:T(128)} %pad_add_fusion.at_ref, bf16[2272,256]{1,0:T(8,128)(2,1)} %join.26.refs_2_.refs_0_, bf16[2272,256]{1,0:T(8,128)(2,1)} %get-tuple-element.100.one_ref.refs_2_.refs_1_, bf16[1136,256]{1,0:T(8,128)(2,1)} %get-tuple-element.106.refs_2_.refs_1_, ...), custom_call_target="tpu_custom_call" | custom-call | bytes 7340032 | tf_op jit(solution)/shard_map/tokens/pallas_call | solution.py:461
  124.3 1.0 copy-done.6
  125.3 1.0 copy-done.7
  126.4 2.5 %relay.4 = (bf16[112,2368]{1,0:T(8,128)(2,1)}, bf16[112,2368]{1,0:T(8,128)(2,1)}) custom-call(bf16[224,2368]{1,0:T(8,128)(2,1)} %get-tuple-element.112.gp_ref.refs_6_, bf16[224,2368]{1,0:T(8,128)(2,1)} %get-tuple-element.113.gm_ref.refs_7_, bf16[112,2368]{1,0:T(8,128)(2,1)} %get-tuple-element.114.rp_ref, bf16[112,2368]{1,0:T(8,128)(2,1)} %get-tuple-element.115.rm_ref), custom_call_target="tpu_custom_call" | custom-call | bytes 3182592 | tf_op jit(solution)/shard_map/relay/pallas_call | solution.py:263
  129.4 0.9 collective-permute-start.32
  131.3 1.0 copy-done.29
  132.3 19.6 %update.5 = (bf16[224,2368]{1,0:T(8,128)(2,1)}, bf16[224,2368]{1,0:T(8,128)(2,1)}, bf16[112,2368]{1,0:T(8,128)(2,1)}, bf16[112,2368]{1,0:T(8,128)(2,1)}, bf16[224,2368]{1,0:T(8,128)(2,1)}) custom-call(s32[4]{0:T(128)} %and_select_fusion.block_ref, bf16[2272,256]{1,0:T(8,128)(2,1)} %join.26.refs_2_.refs_0_, ...), custom_call_target="tpu_custom_call" | custom-call | flops 8690597888 | bytes 17612800 | tf_op jit(solution)/shard_map/update/pallas_call | solution.py:232
  152.0 2.7 %collective-permute-start.27 = (bf16[224,2368]{1,0:T(8,128)(2,1)}, bf16[224,2368]{1,0:T(8,128)(2,1)S(1)}, u32[]{:S(2)}, u32[]{:S(2)}) collective-permute-start(bf16[224,2368]{1,0:T(8,128)(2,1)} %get-tuple-element.122), channel_id=1, source_target_pairs={{0,96},{32,0},{64,32},{96,64},{1,97},{33,1},{65,33},{97,65},{2,98}... | collective-permute-start | bytes 3182600 | tf_op jit(solution)/shard_map/ppermute | solution.py:42
  155.7 5.2 %up_sums.1 = (f32[224,2368]{1,0:T(8,128)}, bf16[224,2368]{1,0:T(8,128)(2,1)}) custom-call(s32[1]{0:T(128)} %bitcast.13.mine_ref, bf16[224,2368]{1,0:T(8,128)(2,1)} %get-tuple-element.84.refs_3_.refs_0_, bf16[224,2368]{1,0:T(8,128)(2,1)} %get-tuple-element.93.gp_ref.refs_1_, bf16[224,2368]{1,0:T(8,128)(2,1)} %get-tuple-element.94.gm_ref.refs_2_, ...), custom_call_target="tpu_custom_call" | custom-call | tf_op jit(solution)/shard_map/up_sums/pallas_call | solution.py:386
  161.6 17.6 %hidden.1.refs_2_ = bf16[1184,512]{1,0:T(8,128)(2,1)} custom-call(s32[1]{0:T(128)} %bitcast.c_ref, bf16[1808,512]{1,0:T(8,128)(2,1)} %join.34.mine_ref, bf16[1808,512]{1,0:T(8,128)(2,1)} %collective-permute-done.23.other_ref, bf16[1184,3584]{1,0:T(8,128)(2,1)} %bitcast.20, bf16[1184,3584]{1,0:T(8,128)(2,1)} %bitcast.19, bf16[4,1184,256]{2,1,0:T(8,128)(2,1)} %bitcast.16, ...), custom_call_target="tpu_custom_call" | custom-call | flops 11173625856 | bytes 26705920 | tf_op jit(solution)/shard_map/hidden/pallas_call | solution.py:509
  179.2 1.0 copy-done.4
  180.2 1.0 copy-done.5
  181.2 2.5 %relay.5 = (bf16[112,2368]{1,0:T(8,128)(2,1)}, bf16[112,2368]{1,0:T(8,128)(2,1)}) custom-call(bf16[224,2368]{1,0:T(8,128)(2,1)} %get-tuple-element.123.gp_ref, bf16[224,2368]{1,0:T(8,128)(2,1)} %get-tuple-element.124.gm_ref, bf16[112,2368]{1,0:T(8,128)(2,1)} %get-tuple-element.125.rp_ref, bf16[112,2368]{1,0:T(8,128)(2,1)} %get-tuple-element.126.rm_ref), custom_call_target="tpu_custom_call" | custom-call | bytes 3182592 | tf_op jit(solution)/shard_map/relay/pallas_call | solution.py:263
  183.7 2.7 %collective-permute-start.29 = (bf16[112,2368]{1,0:T(8,128)(2,1)}, bf16[112,2368]{1,0:T(8,128)(2,1)S(1)}, u32[]{:S(2)}, u32[]{:S(2)}) collective-permute-start(bf16[112,2368]{1,0:T(8,128)(2,1)} %get-tuple-element.130), channel_id=1, source_target_pairs={{0,96},{32,0},{64,32},{96,64},{1,97},{33,1},{65,33},{97,65},{2,98}... | collective-permute-start | bytes 1591304 | tf_op jit(solution)/shard_map/ppermute | solution.py:42
  186.4 4.0 %gate_early.1 = (f32[224,1184]{1,0:T(8,128)}, f32[224,1184]{1,0:T(8,128)}) custom-call(s32[1]{0:T(128)} %bitcast.c_ref, bf16[448,1184]{1,0:T(8,128)(2,1)} %get-tuple-element.120.held_ref, bf16[224,2368]{1,0:T(8,128)(2,1)} %get-tuple-element.119.refs_0_.own_ref.refs_2_, bf16[224,2368]{1,0:T(8,128)(2,1)} %get-tuple-element.123.gp_ref, ...), custom_call_target="tpu_custom_call" | custom-call | tf_op jit(solution)/shard_map/gate_early/pallas_call | solution.py:325
  190.4 1.0 copy-done.14
  191.4 3.3 %up_sum.1 = (f32[224,1184]{1,0:T(8,128)}, bf16[224,1184]{1,0:T(8,128)(2,1)}) custom-call(f32[224,2368]{1,0:T(8,128)} %get-tuple-element.139.keep_ref, bf16[224,2368]{1,0:T(8,128)(2,1)} %join.39.sent_ref), custom_call_target="tpu_custom_call" | custom-call | tf_op jit(solution)/shard_map/up_sum/pallas_call | solution.py:400
  194.6 2.0 collective-permute-start.34
  196.7 0.8 collective-permute-done.28.refs_0_
  199.1 3.1 %gate_late.1 = (bf16[224,1184]{1,0:T(8,128)(2,1)}, bf16[224,1184]{1,0:T(8,128)(2,1)}) custom-call(f32[224,1184]{1,0:T(8,128)} %get-tuple-element.128.refs_2_.near_ref.refs_1_, f32[224,1184]{1,0:T(8,128)} %get-tuple-element.129.far_ref, bf16[112,2368]{1,0:T(8,128)(2,1)} %get-tuple-element.131.fp_ref, bf16[112,2368]{1,0:T(8,128)(2,1)} %get-tuple-element.132.fm_ref), custom_call_target="tpu_custom_call" | custom-call | tf_op jit(solution)/shard_map/gate_late/pallas_call | solution.py:345
  202.3 2.4 %collective-permute-start.30 = (bf16[224,1184]{1,0:T(8,128)(2,1)}, bf16[224,1184]{1,0:T(8,128)(2,1)S(1)}, u32[]{:S(2)}, u32[]{:S(2)}) collective-permute-start(bf16[224,1184]{1,0:T(8,128)(2,1)} %get-tuple-element.134), channel_id=1, source_target_pairs={{0,1},{1,0},{2,3},{3,2},{4,5},{5,4},{6,7},{7,6},{8,9},{9,8},{10,11... | collective-permute-start | bytes 1591304 | tf_op jit(solution)/shard_map/ppermute | solution.py:42
  205.5 3.1 %renew.1 = bf16[448,1184]{1,0:T(8,128)(2,1)} custom-call(s32[1]{0:T(128)} %bitcast.c_ref, bf16[448,1184]{1,0:T(8,128)(2,1)} %get-tuple-element.135.held_ref, f32[224,1184]{1,0:T(8,128)} %get-tuple-element.141.near_ref, bf16[224,1184]{1,0:T(8,128)(2,1)} %copy-done.27), custom_call_target="tpu_custom_call" | custom-call | tf_op jit(solution)/shard_map/renew/pallas_call | solution.py:427
  209.4 2.7 %gate_rows.1 = bf16[448,1184]{1,0:T(8,128)(2,1)} custom-call(s32[1]{0:T(128)} %bitcast.c_ref, bf16[448,1184]{1,0:T(8,128)(2,1)} %get-tuple-element.120.held_ref, bf16[224,1184]{1,0:T(8,128)(2,1)} %get-tuple-element.133.near_ref, bf16[224,1184]{1,0:T(8,128)(2,1)} %copy-done.26), custom_call_target="tpu_custom_call" | custom-call | tf_op jit(solution)/shard_map/gate_rows/pallas_call | solution.py:363
  (114 shorter events, 13.6 us)
Async XLA Ops:
  0.6 20.9 %collective-permute-start.4 = (bf16[4,1184,256]{2,1,0:T(8,128)(2,1)}, bf16[4,1184,256]{2,1,0:T(8,128)(2,1)}, u32[]{:S(2)}, u32[]{:S(2)}) collective-permute-start(bf16[4,1184,256]{2,1,0:T(8,128)(2,1)} %bitcast.21), channel_id=1, source_target_pairs={{0,1},{1,0},{2,3},{3,2},{4,5},{5,4},{6,7},{7,6},{8,9},{9,8},{10,11... | collective-permute-start | bytes 7274504 | tf_op jit(solution)/shard_map/ppermute | solution.py:42
  5.2 20.8 %collective-permute-start = (bf16[1376,256]{1,0:T(8,128)(2,1)}, bf16[1376,256]{1,0:T(8,128)(2,1)S(1)}, u32[]{:S(2)}, u32[]{:S(2)}) collective-permute-start(bf16[1376,256]{1,0:T(8,128)(2,1)} %get-tuple-element.74.all_ref), channel_id=1, source_target_pairs={{0,2},{2,0},{1,3},{3,1},{4,6},{6,4},{5,7},{7,5},{8,10},{10,8},{9,1... | collective-permute-start | bytes 2113544 | tf_op jit(solution)/shard_map/ppermute | solution.py:42
  8.2 13.3 %collective-permute-start.2 = (bf16[896,256]{1,0:T(8,128)(2,1)}, bf16[896,256]{1,0:T(8,128)(2,1)}, u32[]{:S(2)}, u32[]{:S(2)}) collective-permute-start(bf16[896,256]{1,0:T(8,128)(2,1)} %get-tuple-element.75.refs_0_), channel_id=1, source_target_pairs={{0,4},{4,8},{8,12},{12,0},{1,5},{5,9},{9,13},{13,1},{2,6},{6,10},{... | collective-permute-start | bytes 1376264 | tf_op jit(solution)/shard_map/ppermute | solution.py:42
  9.4 12.1 %collective-permute-start.3 = (bf16[896,256]{1,0:T(8,128)(2,1)}, bf16[896,256]{1,0:T(8,128)(2,1)}, u32[]{:S(2)}, u32[]{:S(2)}) collective-permute-start(bf16[896,256]{1,0:T(8,128)(2,1)} %get-tuple-element.75.refs_0_), channel_id=1, source_target_pairs={{0,12},{4,0},{8,4},{12,8},{1,13},{5,1},{9,5},{13,9},{2,14},{6,2},{... | collective-permute-start | bytes 1376264 | tf_op jit(solution)/shard_map/ppermute | solution.py:42
  23.4 7.4 %collective-permute-start.5 = (bf16[448,256]{1,0:T(8,128)(2,1)}, bf16[448,256]{1,0:T(8,128)(2,1)S(1)}, u32[]{:S(2)}, u32[]{:S(2)}) collective-permute-start(bf16[448,256]{1,0:T(8,128)(2,1)} %get-tuple-element.78), channel_id=1, source_target_pairs={{0,4},{4,8},{8,12},{12,0},{1,5},{5,9},{9,13},{13,1},{2,6},{6,10},{... | collective-permute-start | bytes 688136 | tf_op jit(solution)/shard_map/ppermute | solution.py:42
  24.3 6.5 %collective-permute-start.6 = (bf16[448,256]{1,0:T(8,128)(2,1)}, bf16[448,256]{1,0:T(8,128)(2,1)S(1)}, u32[]{:S(2)}, u32[]{:S(2)}) collective-permute-start(bf16[448,256]{1,0:T(8,128)(2,1)} %get-tuple-element.79), channel_id=1, source_target_pairs={{0,12},{4,0},{8,4},{12,8},{1,13},{5,1},{9,5},{13,9},{2,14},{6,2},{... | collective-permute-start | bytes 688136 | tf_op jit(solution)/shard_map/ppermute | solution.py:42
  26.1 0.9 copy-start.1
  26.9 7.9 %copy-start.30 = (s32[4]{0:T(128)S(1)}, s32[4]{0:T(128)}, u32[]{:S(2)}) copy-start(s32[4]{0:T(128)} %constant.45) | copy-start | bytes 52
  26.9 8.5 %copy-start.22 = (bf16[896,256]{1,0:T(8,128)(2,1)S(1)}, bf16[896,256]{1,0:T(8,128)(2,1)}, u32[]{:S(2)}) copy-start(bf16[896,256]{1,0:T(8,128)(2,1)} %join.20.s_ref) | copy-start | bytes 1376260
  26.9 23.8 %collective-permute-start.9 = (bf16[896,256]{1,0:T(8,128)(2,1)}, bf16[896,256]{1,0:T(8,128)(2,1)S(1)}, u32[]{:S(2)}, u32[]{:S(2)}) collective-permute-start(bf16[896,256]{1,0:T(8,128)(2,1)} %join.20.s_ref), channel_id=1, source_target_pairs={{18,16},{16,2},{2,18},{19,17},{17,3},{3,19},{22,20},{20,6},{6,22},... | collective-permute-start | bytes 1376264 | tf_op jit(solution)/shard_map/ppermute | solution.py:546
  32.2 20.8 %collective-permute-start.7 = (bf16[1376,256]{1,0:T(8,128)(2,1)}, bf16[1376,256]{1,0:T(8,128)(2,1)S(1)}, u32[]{:S(2)}, u32[]{:S(2)}) collective-permute-start(bf16[1376,256]{1,0:T(8,128)(2,1)} %join.23.refs_7_.refs_0_.refs_5_), channel_id=1, source_target_pairs={{0,4},{4,8},{8,12},{12,0},{1,5},{5,9},{9,13},{13,1},{2,6},{6,10},{... | collective-permute-start | bytes 2113544 | tf_op jit(solution)/shard_map/ppermute | solution.py:42
  32.2 20.8 %collective-permute-start.8 = (bf16[1376,256]{1,0:T(8,128)(2,1)}, bf16[1376,256]{1,0:T(8,128)(2,1)S(1)}, u32[]{:S(2)}, u32[]{:S(2)}) collective-permute-start(bf16[1376,256]{1,0:T(8,128)(2,1)} %join.23.refs_7_.refs_0_.refs_5_), channel_id=1, source_target_pairs={{0,12},{4,0},{8,4},{12,8},{1,13},{5,1},{9,5},{13,9},{2,14},{6,2},{... | collective-permute-start | bytes 2113544 | tf_op jit(solution)/shard_map/ppermute | solution.py:42
  35.4 26.7 %collective-permute-start.1 = (bf16[896,256]{1,0:T(8,128)(2,1)S(1)}, bf16[896,256]{1,0:T(8,128)(2,1)}, u32[]{:S(2)}, u32[]{:S(2)}) collective-permute-start(bf16[896,256]{1,0:T(8,128)(2,1)S(1)} %copy-done.22), channel_id=1, source_target_pairs={{16,0},{2,16},{0,2},{17,1},{3,17},{1,3},{20,4},{6,20},{4,6},{21,5}... | collective-permute-start | bytes 1376264 | tf_op jit(solution)/shard_map/ppermute | solution.py:546
  49.0 25.9 %collective-permute-start.14 = (bf16[224,2368]{1,0:T(8,128)(2,1)}, bf16[224,2368]{1,0:T(8,128)(2,1)S(1)}, u32[]{:S(2)}, u32[]{:S(2)}) collective-permute-start(bf16[224,2368]{1,0:T(8,128)(2,1)} %get-tuple-element.91), channel_id=1, source_target_pairs={{0,32},{32,64},{64,96},{96,0},{1,33},{33,65},{65,97},{97,1},{2,34}... | collective-permute-start | bytes 3182600 | tf_op jit(solution)/shard_map/ppermute | solution.py:42
  50.8 2.2 %copy-start.23 = (bf16[896,256]{1,0:T(8,128)(2,1)}, bf16[896,256]{1,0:T(8,128)(2,1)S(1)}, u32[]{:S(2)}) copy-start(bf16[896,256]{1,0:T(8,128)(2,1)S(1)} %collective-permute-done.9.refs_2_) | copy-start | bytes 1376260
  50.8 24.2 %collective-permute-start.15 = (bf16[224,2368]{1,0:T(8,128)(2,1)}, bf16[224,2368]{1,0:T(8,128)(2,1)S(1)}, u32[]{:S(2)}, u32[]{:S(2)}) collective-permute-start(bf16[224,2368]{1,0:T(8,128)(2,1)} %get-tuple-element.92), channel_id=1, source_target_pairs={{0,96},{32,0},{64,32},{96,64},{1,97},{33,1},{65,33},{97,65},{2,98}... | collective-permute-start | bytes 3182600 | tf_op jit(solution)/shard_map/ppermute | solution.py:42
  53.0 0.9 copy-start.2
  53.0 1.1 copy-start.12
  56.1 9.6 %collective-permute-start.10 = (bf16[688,256]{1,0:T(8,128)(2,1)}, bf16[688,256]{1,0:T(8,128)(2,1)S(1)}, u32[]{:S(2)}, u32[]{:S(2)}) collective-permute-start(bf16[688,256]{1,0:T(8,128)(2,1)} %get-tuple-element.88), channel_id=1, source_target_pairs={{0,4},{4,8},{8,12},{12,0},{1,5},{5,9},{9,13},{13,1},{2,6},{6,10},{... | collective-permute-start | bytes 1056776 | tf_op jit(solution)/shard_map/ppermute | solution.py:42
  56.1 9.6 %collective-permute-start.11 = (bf16[688,256]{1,0:T(8,128)(2,1)}, bf16[688,256]{1,0:T(8,128)(2,1)S(1)}, u32[]{:S(2)}, u32[]{:S(2)}) collective-permute-start(bf16[688,256]{1,0:T(8,128)(2,1)} %get-tuple-element.89), channel_id=1, source_target_pairs={{0,12},{4,0},{8,4},{12,8},{1,13},{5,1},{9,5},{13,9},{2,14},{6,2},{... | collective-permute-start | bytes 1056776 | tf_op jit(solution)/shard_map/ppermute | solution.py:42
  64.7 59.6 %collective-permute-start.22 = (bf16[4,1184,256]{2,1,0:T(8,128)(2,1)}, bf16[4,1184,256]{2,1,0:T(8,128)(2,1)}, u32[]{:S(2)}, u32[]{:S(2)}) collective-permute-start(bf16[4,1184,256]{2,1,0:T(8,128)(2,1)} %join.32), channel_id=1, source_target_pairs={{0,16},{16,0},{1,17},{17,1},{2,18},{18,2},{3,19},{19,3},{4,20},{20... | collective-permute-start | bytes 7274504 | tf_op jit(solution)/shard_map/ppermute | solution.py:42
  65.7 0.7 copy-start.15
  66.5 0.7 copy-start.24
  67.2 26.5 %collective-permute-start.12 = (bf16[2272,256]{1,0:T(8,128)(2,1)}, bf16[2272,256]{1,0:T(8,128)(2,1)S(1)}, u32[]{:S(2)}, u32[]{:S(2)}) collective-permute-start(bf16[2272,256]{1,0:T(8,128)(2,1)} %join.26.refs_2_.refs_0_), channel_id=1, source_target_pairs={{0,4},{4,8},{8,12},{12,0},{1,5},{5,9},{9,13},{13,1},{2,6},{6,10},{... | collective-permute-start | bytes 3489800 | tf_op jit(solution)/shard_map/ppermute | solution.py:42
  67.2 26.5 %collective-permute-start.13 = (bf16[2272,256]{1,0:T(8,128)(2,1)}, bf16[2272,256]{1,0:T(8,128)(2,1)S(1)}, u32[]{:S(2)}, u32[]{:S(2)}) collective-permute-start(bf16[2272,256]{1,0:T(8,128)(2,1)} %join.26.refs_2_.refs_0_), channel_id=1, source_target_pairs={{0,12},{4,0},{8,4},{12,8},{1,13},{5,1},{9,5},{13,9},{2,14},{6,2},{... | collective-permute-start | bytes 3489800 | tf_op jit(solution)/shard_map/ppermute | solution.py:42
  74.9 1.0 copy-start.8
  75.9 1.0 copy-start.9
  79.5 15.6 %collective-permute-start.18 = (bf16[112,2368]{1,0:T(8,128)(2,1)}, bf16[112,2368]{1,0:T(8,128)(2,1)S(1)}, u32[]{:S(2)}, u32[]{:S(2)}) collective-permute-start(bf16[112,2368]{1,0:T(8,128)(2,1)} %get-tuple-element.97.refs_7_.refs_2_), channel_id=1, source_target_pairs={{0,32},{32,64},{64,96},{96,0},{1,33},{33,65},{65,97},{97,1},{2,34}... | collective-permute-start | bytes 1591304 | tf_op jit(solution)/shard_map/ppermute | solution.py:42
  79.5 15.6 %collective-permute-start.19 = (bf16[112,2368]{1,0:T(8,128)(2,1)}, bf16[112,2368]{1,0:T(8,128)(2,1)S(1)}, u32[]{:S(2)}, u32[]{:S(2)}) collective-permute-start(bf16[112,2368]{1,0:T(8,128)(2,1)} %get-tuple-element.104), channel_id=1, source_target_pairs={{0,96},{32,0},{64,32},{96,64},{1,97},{33,1},{65,33},{97,65},{2,98}... | collective-permute-start | bytes 1591304 | tf_op jit(solution)/shard_map/ppermute | solution.py:42
  93.7 1.0 copy-start
  93.7 1.4 copy-start.3
  95.1 0.8 copy-start.11
  95.1 1.0 copy-start.21
  96.1 7.6 %copy-start.10 = (bf16[256,4,1184]{0,2,1:T(8,128)(2,1)S(1)}, bf16[256,4,1184]{0,2,1:T(8,128)(2,1)}, u32[]{:S(2)}) copy-start(bf16[256,4,1184]{0,2,1:T(8,128)(2,1)} %param.14) | copy-start | bytes 7274500
  96.1 28.2 %collective-permute-start.20 = (bf16[224,2368]{1,0:T(8,128)(2,1)}, bf16[224,2368]{1,0:T(8,128)(2,1)S(1)}, u32[]{:S(2)}, u32[]{:S(2)}) collective-permute-start(bf16[224,2368]{1,0:T(8,128)(2,1)} %get-tuple-element.110), channel_id=1, source_target_pairs={{0,32},{32,64},{64,96},{96,0},{1,33},{33,65},{65,97},{97,1},{2,34}... | collective-permute-start | bytes 3182600 | tf_op jit(solution)/shard_map/ppermute | solution.py:42
  96.1 28.2 %collective-permute-start.21 = (bf16[224,2368]{1,0:T(8,128)(2,1)}, bf16[224,2368]{1,0:T(8,128)(2,1)S(1)}, u32[]{:S(2)}, u32[]{:S(2)}) collective-permute-start(bf16[224,2368]{1,0:T(8,128)(2,1)} %get-tuple-element.111), channel_id=1, source_target_pairs={{0,96},{32,0},{64,32},{96,64},{1,97},{33,1},{65,33},{97,65},{2,98}... | collective-permute-start | bytes 3182600 | tf_op jit(solution)/shard_map/ppermute | solution.py:42
  101.1 11.8 %collective-permute-start.16 = (bf16[1136,256]{1,0:T(8,128)(2,1)}, bf16[1136,256]{1,0:T(8,128)(2,1)S(1)}, u32[]{:S(2)}, u32[]{:S(2)}) collective-permute-start(bf16[1136,256]{1,0:T(8,128)(2,1)} %get-tuple-element.102), channel_id=1, source_target_pairs={{0,4},{4,8},{8,12},{12,0},{1,5},{5,9},{9,13},{13,1},{2,6},{6,10},{... | collective-permute-start | bytes 1744904 | tf_op jit(solution)/shard_map/ppermute | solution.py:42
  101.7 11.2 %collective-permute-start.17 = (bf16[1136,256]{1,0:T(8,128)(2,1)}, bf16[1136,256]{1,0:T(8,128)(2,1)S(1)}, u32[]{:S(2)}, u32[]{:S(2)}) collective-permute-start(bf16[1136,256]{1,0:T(8,128)(2,1)} %get-tuple-element.103), channel_id=1, source_target_pairs={{0,12},{4,0},{8,4},{12,8},{1,13},{5,1},{9,5},{13,9},{2,14},{6,2},{... | collective-permute-start | bytes 1744904 | tf_op jit(solution)/shard_map/ppermute | solution.py:42
  112.9 0.9 copy-start.13
  113.7 0.8 copy-start.16
  114.6 16.3 %collective-permute-start.24 = (bf16[4,1184,256]{2,1,0:T(8,128)(2,1)}, bf16[4,1184,256]{2,1,0:T(8,128)(2,1)S(1)}, u32[]{:S(2)}, u32[]{:S(2)}) collective-permute-start(bf16[4,1184,256]{2,1,0:T(8,128)(2,1)} %join.35), channel_id=1, source_target_pairs={{0,1},{1,0},{2,3},{3,2},{4,5},{5,4},{6,7},{7,6},{8,9},{9,8},{10,11... | collective-permute-start | bytes 7274504 | tf_op jit(solution)/shard_map/ppermute | solution.py:42
  124.3 1.0 copy-start.6
  125.3 1.0 copy-start.7
  126.3 5.0 %collective-permute-start.25 = (bf16[4,1184,256]{2,1,0:T(8,128)(2,1)}, bf16[4,1184,256]{2,1,0:T(8,128)(2,1)}, u32[]{:S(2)}, u32[]{:S(2)}) collective-permute-start(bf16[4,1184,256]{2,1,0:T(8,128)(2,1)} %get-tuple-element.117.refs_7_), channel_id=1, source_target_pairs={{0,1},{1,0},{2,3},{3,2},{4,5},{5,4},{6,7},{7,6},{8,9},{9,8},{10,11... | collective-permute-start | bytes 7274504 | tf_op jit(solution)/shard_map/ppermute | solution.py:42
  128.9 32.8 %collective-permute-start.23 = (bf16[1808,512]{1,0:T(8,128)(2,1)}, bf16[1808,512]{1,0:T(8,128)(2,1)}, u32[]{:S(2)}, u32[]{:S(2)}) collective-permute-start(bf16[1808,512]{1,0:T(8,128)(2,1)} %join.34.mine_ref), channel_id=1, source_target_pairs={{0,1},{1,0},{2,3},{3,2},{4,5},{5,4},{6,7},{7,6},{8,9},{9,8},{10,11... | collective-permute-start | bytes 5554184 | tf_op jit(solution)/shard_map/ppermute | solution.py:42
  129.4 25.3 %collective-permute-start.32 = (bf16[112,2368]{1,0:T(8,128)(2,1)}, bf16[112,2368]{1,0:T(8,128)(2,1)S(1)}, u32[]{:S(2)}, u32[]{:S(2)}) collective-permute-start(bf16[112,2368]{1,0:T(8,128)(2,1)} %get-tuple-element.116.refs_1_), channel_id=1, source_target_pairs={{0,96},{32,0},{64,32},{96,64},{1,97},{33,1},{65,33},{97,65},{2,98}... | collective-permute-start | bytes 1591304 | tf_op jit(solution)/shard_map/ppermute | solution.py:42
  130.3 24.4 %collective-permute-start.31 = (bf16[112,2368]{1,0:T(8,128)(2,1)}, bf16[112,2368]{1,0:T(8,128)(2,1)S(1)}, u32[]{:S(2)}, u32[]{:S(2)}) collective-permute-start(bf16[112,2368]{1,0:T(8,128)(2,1)} %get-tuple-element.118.refs_9_), channel_id=1, source_target_pairs={{0,32},{32,64},{64,96},{96,0},{1,33},{33,65},{65,97},{97,1},{2,34}... | collective-permute-start | bytes 1591304 | tf_op jit(solution)/shard_map/ppermute | solution.py:42
  130.8 1.5 copy-start.29
  152.0 27.3 %collective-permute-start.26 = (bf16[224,2368]{1,0:T(8,128)(2,1)}, bf16[224,2368]{1,0:T(8,128)(2,1)S(1)}, u32[]{:S(2)}, u32[]{:S(2)}) collective-permute-start(bf16[224,2368]{1,0:T(8,128)(2,1)} %get-tuple-element.121), channel_id=1, source_target_pairs={{0,32},{32,64},{64,96},{96,0},{1,33},{33,65},{65,97},{97,1},{2,34}... | collective-permute-start | bytes 3182600 | tf_op jit(solution)/shard_map/ppermute | solution.py:42
  152.0 27.2 %collective-permute-start.27 = (bf16[224,2368]{1,0:T(8,128)(2,1)}, bf16[224,2368]{1,0:T(8,128)(2,1)S(1)}, u32[]{:S(2)}, u32[]{:S(2)}) collective-permute-start(bf16[224,2368]{1,0:T(8,128)(2,1)} %get-tuple-element.122), channel_id=1, source_target_pairs={{0,96},{32,0},{64,32},{96,64},{1,97},{33,1},{65,33},{97,65},{2,98}... | collective-permute-start | bytes 3182600 | tf_op jit(solution)/shard_map/ppermute | solution.py:42
  154.7 0.8 copy-start.18
  154.7 1.0 copy-start.17
  161.0 29.4 %collective-permute-start.33 = (bf16[224,2368]{1,0:T(8,128)(2,1)}, bf16[224,2368]{1,0:T(8,128)(2,1)S(1)}, u32[]{:S(2)}, u32[]{:S(2)}) collective-permute-start(bf16[224,2368]{1,0:T(8,128)(2,1)} %get-tuple-element.140), channel_id=1, source_target_pairs={{0,16},{16,0},{1,17},{17,1},{2,18},{18,2},{3,19},{19,3},{4,20},{20... | collective-permute-start | bytes 3182600 | tf_op jit(solution)/shard_map/ppermute | solution.py:42
  179.2 1.0 copy-start.4
  180.2 1.0 copy-start.5
  183.7 13.8 %collective-permute-start.28 = (bf16[112,2368]{1,0:T(8,128)(2,1)}, bf16[112,2368]{1,0:T(8,128)(2,1)S(1)}, u32[]{:S(2)}, u32[]{:S(2)}) collective-permute-start(bf16[112,2368]{1,0:T(8,128)(2,1)} %get-tuple-element.127.refs_0_), channel_id=1, source_target_pairs={{0,32},{32,64},{64,96},{96,0},{1,33},{33,65},{65,97},{97,1},{2,34}... | collective-permute-start | bytes 1591304 | tf_op jit(solution)/shard_map/ppermute | solution.py:42
  183.7 13.8 %collective-permute-start.29 = (bf16[112,2368]{1,0:T(8,128)(2,1)}, bf16[112,2368]{1,0:T(8,128)(2,1)S(1)}, u32[]{:S(2)}, u32[]{:S(2)}) collective-permute-start(bf16[112,2368]{1,0:T(8,128)(2,1)} %get-tuple-element.130), channel_id=1, source_target_pairs={{0,96},{32,0},{64,32},{96,64},{1,97},{33,1},{65,33},{97,65},{2,98}... | collective-permute-start | bytes 1591304 | tf_op jit(solution)/shard_map/ppermute | solution.py:42
  190.4 1.0 copy-start.14
  194.6 10.0 %collective-permute-start.34 = (bf16[224,1184]{1,0:T(8,128)(2,1)}, bf16[224,1184]{1,0:T(8,128)(2,1)S(1)}, u32[]{:S(2)}, u32[]{:S(2)}) collective-permute-start(bf16[224,1184]{1,0:T(8,128)(2,1)} %get-tuple-element.142), channel_id=1, source_target_pairs={{0,1},{1,0},{2,3},{3,2},{4,5},{5,4},{6,7},{7,6},{8,9},{9,8},{10,11... | collective-permute-start | bytes 1591304 | tf_op jit(solution)/shard_map/ppermute | solution.py:42
  197.5 0.8 copy-start.19
  198.3 0.8 copy-start.20
  202.3 6.3 %collective-permute-start.30 = (bf16[224,1184]{1,0:T(8,128)(2,1)}, bf16[224,1184]{1,0:T(8,128)(2,1)S(1)}, u32[]{:S(2)}, u32[]{:S(2)}) collective-permute-start(bf16[224,1184]{1,0:T(8,128)(2,1)} %get-tuple-element.134), channel_id=1, source_target_pairs={{0,1},{1,0},{2,3},{3,2},{4,5},{5,4},{6,7},{7,6},{8,9},{9,8},{10,11... | collective-permute-start | bytes 1591304 | tf_op jit(solution)/shard_map/ppermute | solution.py:42
  204.7 0.8 copy-start.27
  208.6 0.8 copy-start.26
  (2 other events, 1.4 us)

commit v2 on v1

--- a/solution.py
+++ b/solution.py
@@ -332,39 +332,52 @@
 
 
 def _gate_late_kernel(near_ref, far_ref, fp_ref, fm_ref, out_ref, send_ref):
-    n = fp_ref.shape[0]
     q, k = near_ref.shape[1], CUT
-    for ref, rows in ((fp_ref, slice(0, n)), (fm_ref, slice(n, 2 * n))):
-        out_ref[rows, :k] = (near_ref[rows, :k] + ref[:, :k].astype(f32)).astype(bf16)
-        out_ref[rows, k:] = (near_ref[rows, k:] + ref[:, 2 * k : k + q].astype(f32)).astype(bf16)
-        send_ref[rows, :k] = (far_ref[rows, :k] + ref[:, k : 2 * k].astype(f32)).astype(bf16)
-        send_ref[rows, k:] = (far_ref[rows, k:] + ref[:, k + q :].astype(f32)).astype(bf16)
+    for i, ref in enumerate((fp_ref, fm_ref)):
+
+        @pl.when(pl.program_id(0) == i)
+        def _():
+            out_ref[:, :k] = (near_ref[:, :k] + ref[:, :k].astype(f32)).astype(bf16)
+            out_ref[:, k:] = (near_ref[:, k:] + ref[:, 2 * k : k + q].astype(f32)).astype(bf16)
+            send_ref[:, :k] = (far_ref[:, :k] + ref[:, k : 2 * k].astype(f32)).astype(bf16)
+            send_ref[:, k:] = (far_ref[:, k:] + ref[:, k + q :].astype(f32)).astype(bf16)
 
 
 def gate_late(near, far, fp, fm):
+    n, wide = fp.shape
+    half = pl.BlockSpec((n, near.shape[1]), lambda i: (i, 0))
+    whole = pl.BlockSpec((n, wide), lambda i: (0, 0))
     return _call(
         _gate_late_kernel,
         "gate_late",
-        in_specs=[FULL] * 4,
-        out_specs=[FULL] * 2,
+        grid=(2,),
+        in_specs=[half, half, whole, whole],
+        out_specs=[half, half],
         out_shape=[jax.ShapeDtypeStruct(near.shape, bf16)] * 2,
     )(near, far, fp, fm)
 
 
 def _gate_rows_kernel(c_ref, held_ref, near_ref, far_ref, out_ref):
-    d = near_ref.shape[0]
-    c = c_ref[0]
-    mine, other = pl.ds(pl.multiple_of(c * d, d), d), pl.ds(pl.multiple_of((1 - c) * d, d), d)
-    out_ref[mine, :] = near_ref[...]
-    out_ref[other, :] = (held_ref[other, :].astype(f32) + far_ref[...].astype(f32)).astype(bf16)
+    mine = pl.program_id(0) == c_ref[0]
+
+    @pl.when(mine)
+    def _():
+        out_ref[...] = near_ref[...]
+
+    @pl.when(jnp.logical_not(mine))
+    def _():
+        out_ref[...] = (held_ref[...].astype(f32) + far_ref[...].astype(f32)).astype(bf16)
 
 
 def gate_rows(c, held, near, far):
+    part = pl.BlockSpec(near.shape, lambda i: (i, 0))
+    all_of = pl.BlockSpec(near.shape, lambda i: (0, 0))
     return _call(
         _gate_rows_kernel,
         "gate_rows",
-        in_specs=[SCALARS] + [FULL] * 3,
-        out_specs=FULL,
+        grid=(2,),
+        in_specs=[SCALARS, part, all_of, all_of],
+        out_specs=part,
         out_shape=jax.ShapeDtypeStruct(held.shape, bf16),
     )(c, held, near, far)
 

time: 213 us -> 212 us (level)
  no operation moved by 1% of the time
where the time goes in v2:
time: 212 us
  Pallas kernels  105 us (50%)
  starting transfers between devices  51.7 us (24%)
  local copies, waits for them, and re-layouts  32.2 us (15%)
  waiting for transfers between devices  20.9 us (10%)
    ppermute x33, starting transfers between devices, swap(): return lax.ppermute(v, axis, [(i, (i + shift) % n) for i in range(n)])  48.5 us
    pallas_call x3, Pallas kernels, update(): _call(functools.partial(_update_kernel, coeff, slabs, d, q - CUT, len(sec...  42.5 us
    unnamed x66, local copies, waits for them, and re-layouts  29 us
    ppermute x33, waiting for transfers between devices, swap(): return lax.ppermute(v, axis, [(i, (i + shift) % n) for i in range(n)])  20.9 us
    pallas_call x1, Pallas kernels, hidden_of(): _call(_hidden_kernel, 'hidden', flops=4 * q * t * (d + rank * m), moved=2...  17.6 us
    pallas_call x3, Pallas kernels, relay(): _call(_relay_kernel, 'relay', grid=(2,), moved=12 * rp.size, in_specs=[sp...  7.56 us
    pallas_call x3, Pallas kernels, halves(): _call(_halves_kernel, 'halves', grid=(1,), moved=8 * n * m, in_specs=[_at...  6.09 us
    pallas_call x1, Pallas kernels, up_sums(): _call(kernel, 'up_sums', grid=(2,), in_specs=[SCALARS] + [pl.BlockSpec((p...  5.25 us
  transfers between devices with their start and end apart: 35, of which 6 were waited for; matrix products, arithmetic and copies ran while one was open for 6% of the time, Pallas kernels for 48%

profile of v2, /device:TPU:1, one launch (start us, length us, event | category | flops | bytes accessed | tf_op | source)
XLA Modules:
  0.0 211.7 jit_solution(1054770784489565516)
XLA Ops:
  0.6 1.5 collective-permute-start.4
  2.1 3.1 %pack.1 = (bf16[896,256]{1,0:T(8,128)(2,1)}, bf16[896,256]{1,0:T(8,128)(2,1)}, bf16[1376,256]{1,0:T(8,128)(2,1)}) custom-call(bf16[224,512]{1,0:T(8,128)(2,1)} %bitcast.27, bf16[4,224,256]{2,1,0:T(8,128)(2,1)} %bitcast.25, bf16[4,224,256]{2,1,0:T(8,128)(2,1)} %bitcast.26, f32[1,256]{1,0:T(1,128)} %bitcast.28), custom_call_target="tpu_custom_call" | custom-call | flops 469762048 | bytes 1835008 | tf_op jit(solution)/shard_map/pack/pallas_call | solution.py:95
  5.2 3.0 %collective-permute-start = (bf16[1376,256]{1,0:T(8,128)(2,1)}, bf16[1376,256]{1,0:T(8,128)(2,1)S(1)}, u32[]{:S(2)}, u32[]{:S(2)}) collective-permute-start(bf16[1376,256]{1,0:T(8,128)(2,1)} %get-tuple-element.74.all_ref), channel_id=1, source_target_pairs={{0,2},{2,0},{1,3},{3,1},{4,6},{6,4},{5,7},{7,5},{8,10},{10,8},{9,1... | collective-permute-start | bytes 2113544 | tf_op jit(solution)/shard_map/ppermute | solution.py:42
  8.2 1.2 collective-permute-start.2
  9.4 1.5 collective-permute-start.3
  10.9 3.2 %constant_dynamic-slice_fusion = (bf16[448,1184]{0,1:T(8,128)(2,1)S(1)}, bf16[448,1184]{0,1:T(8,128)(2,1)S(1)}) fusion(bf16[3584,1184]{0,1:T(8,128)(2,1)} %param.11, s32[]{:T(128)S(6)} %select_n.11, bf16[3584,1184]{0,1:T(8,128)(2,1)} %param.10), kind=kLoop, calls=%fused_computation.5 | loop fusion | bytes 4243460 | tf_op jit(solution)/shard_map/dynamic_slice | solution.py:553
  14.1 1.6 copy.53.refs_3_
  15.7 1.5 copy.54.refs_4_
  17.2 4.4 %collective-permute-done.2.refs_0_ = bf16[896,256]{1,0:T(8,128)(2,1)} collective-permute-done((bf16[896,256]{1,0:T(8,128)(2,1)}, bf16[896,256]{1,0:T(8,128)(2,1)}, u32[]{:S(2)}, u32[]{:S(2)}) %collective-permute-start.2) | collective-permute-done | bytes 458784 | tf_op jit(solution)/shard_map/ppermute | solution.py:42
  21.6 1.8 halves.3
  23.4 0.9 collective-permute-start.5
  24.3 1.8 collective-permute-start.6
  26.1 0.9 copy-done.1
  27.8 3.0 %collective-permute-done.5.refs_0_ = bf16[448,256]{1,0:T(8,128)(2,1)S(1)} collective-permute-done((bf16[448,256]{1,0:T(8,128)(2,1)}, bf16[448,256]{1,0:T(8,128)(2,1)S(1)}, u32[]{:S(2)}, u32[]{:S(2)}) %collective-permute-start.5) | collective-permute-done | bytes 229408 | tf_op jit(solution)/shard_map/ppermute | solution.py:42
  32.2 2.7 %collective-permute-start.8 = (bf16[1376,256]{1,0:T(8,128)(2,1)}, bf16[1376,256]{1,0:T(8,128)(2,1)S(1)}, u32[]{:S(2)}, u32[]{:S(2)}) collective-permute-start(bf16[1376,256]{1,0:T(8,128)(2,1)} %join.23.refs_7_.refs_0_.refs_5_), channel_id=1, source_target_pairs={{0,12},{4,0},{8,4},{12,8},{1,13},{5,1},{9,5},{13,9},{2,14},{6,2},{... | collective-permute-start | bytes 2113544 | tf_op jit(solution)/shard_map/ppermute | solution.py:42
  35.4 2.4 %collective-permute-start.1 = (bf16[896,256]{1,0:T(8,128)(2,1)S(1)}, bf16[896,256]{1,0:T(8,128)(2,1)}, u32[]{:S(2)}, u32[]{:S(2)}) collective-permute-start(bf16[896,256]{1,0:T(8,128)(2,1)S(1)} %copy-done.22), channel_id=1, source_target_pairs={{16,0},{2,16},{0,2},{17,1},{3,17},{1,3},{20,4},{6,20},{4,6},{21,5}... | collective-permute-start | bytes 1376264 | tf_op jit(solution)/shard_map/ppermute | solution.py:559
  37.8 11.3 %update.3 = (bf16[224,2368]{1,0:T(8,128)(2,1)}, bf16[224,2368]{1,0:T(8,128)(2,1)}, bf16[112,2368]{1,0:T(8,128)(2,1)}, bf16[112,2368]{1,0:T(8,128)(2,1)}, bf16[224,2368]{1,0:T(8,128)(2,1)}) custom-call(s32[4]{0:T(128)} %and_select_fusion.block_ref, bf16[896,256]{1,0:T(8,128)(2,1)} %get-tuple-element.75.refs_0_, ...), custom_call_target="tpu_custom_call" | custom-call | flops 4345298944 | bytes 10928128 | tf_op jit(solution)/shard_map/update/pallas_call | solution.py:232
  49.0 1.7 collective-permute-start.14
  50.8 2.2 %collective-permute-start.15 = (bf16[224,2368]{1,0:T(8,128)(2,1)}, bf16[224,2368]{1,0:T(8,128)(2,1)S(1)}, u32[]{:S(2)}, u32[]{:S(2)}) collective-permute-start(bf16[224,2368]{1,0:T(8,128)(2,1)} %get-tuple-element.92), channel_id=1, source_target_pairs={{0,96},{32,0},{64,32},{96,64},{1,97},{33,1},{65,33},{97,65},{2,98}... | collective-permute-start | bytes 3182600 | tf_op jit(solution)/shard_map/ppermute | solution.py:42
  53.0 0.8 copy-done.2
  54.1 2.0 halves.4
  56.1 2.6 %collective-permute-start.11 = (bf16[688,256]{1,0:T(8,128)(2,1)}, bf16[688,256]{1,0:T(8,128)(2,1)S(1)}, u32[]{:S(2)}, u32[]{:S(2)}) collective-permute-start(bf16[688,256]{1,0:T(8,128)(2,1)} %get-tuple-element.89), channel_id=1, source_target_pairs={{0,12},{4,0},{8,4},{12,8},{1,13},{5,1},{9,5},{13,9},{2,14},{6,2},{... | collective-permute-start | bytes 1056776 | tf_op jit(solution)/shard_map/ppermute | solution.py:42
  58.8 3.3 %copy.81.refs_0_ = bf16[4,1184,256]{2,1,0:T(8,128)(2,1)} copy(bf16[4,1184,256]{2,1,0:T(8,128)(2,1)} %bitcast.14) | data formatting | bytes 4849664
  62.1 2.6 %pick.1.refs_2_.refs_0_.refs_1_ = bf16[2272,256]{1,0:T(8,128)(2,1)} custom-call(s32[1]{0:T(128)} %bitcast.3.y_ref, bf16[896,256]{1,0:T(8,128)(2,1)} %join.20.s_ref, bf16[896,256]{1,0:T(8,128)(2,1)} %collective-permute-done.1.pa_ref, bf16[896,256]{1,0:T(8,128)(2,1)} %get-tuple-element.85.pb_ref, bf16[1376,256]{1,0:T(8,128)(2,1)} %get-tuple-element.74.all_ref, ...), custom_call_target="tpu_custom_call" | custom-call | bytes 1835008 | tf_op jit(solution)/shard_map/pick/pallas_call | solution.py:127
  64.7 1.0 collective-permute-start.22
  67.2 2.7 %collective-permute-start.13 = (bf16[2272,256]{1,0:T(8,128)(2,1)}, bf16[2272,256]{1,0:T(8,128)(2,1)S(1)}, u32[]{:S(2)}, u32[]{:S(2)}) collective-permute-start(bf16[2272,256]{1,0:T(8,128)(2,1)} %join.26.refs_2_.refs_0_), channel_id=1, source_target_pairs={{0,12},{4,0},{8,4},{12,8},{1,13},{5,1},{9,5},{13,9},{2,14},{6,2},{... | collective-permute-start | bytes 3489800 | tf_op jit(solution)/shard_map/ppermute | solution.py:42
  69.9 5.0 %collective-permute-done.14.refs_0_ = bf16[224,2368]{1,0:T(8,128)(2,1)S(1)} collective-permute-done((bf16[224,2368]{1,0:T(8,128)(2,1)}, bf16[224,2368]{1,0:T(8,128)(2,1)S(1)}, u32[]{:S(2)}, u32[]{:S(2)}) %collective-permute-start.14) | collective-permute-done | bytes 1060896 | tf_op jit(solution)/shard_map/ppermute | solution.py:42
  74.9 1.0 copy-done.8
  75.9 1.0 copy-done.9
  76.9 2.5 %relay.3 = (bf16[112,2368]{1,0:T(8,128)(2,1)}, bf16[112,2368]{1,0:T(8,128)(2,1)}) custom-call(bf16[224,2368]{1,0:T(8,128)(2,1)} %get-tuple-element.93.gp_ref.refs_1_, bf16[224,2368]{1,0:T(8,128)(2,1)} %get-tuple-element.94.gm_ref.refs_2_, bf16[112,2368]{1,0:T(8,128)(2,1)} %get-tuple-element.95.rp_ref, bf16[112,2368]{1,0:T(8,128)(2,1)} %get-tuple-element.96.rm_ref), custom_call_target="tpu_custom_call" | custom-call | bytes 3182592 | tf_op jit(solution)/shard_map/relay/pallas_call | solution.py:263
  79.5 2.7 %collective-permute-start.19 = (bf16[112,2368]{1,0:T(8,128)(2,1)}, bf16[112,2368]{1,0:T(8,128)(2,1)S(1)}, u32[]{:S(2)}, u32[]{:S(2)}) collective-permute-start(bf16[112,2368]{1,0:T(8,128)(2,1)} %get-tuple-element.104), channel_id=1, source_target_pairs={{0,96},{32,0},{64,32},{96,64},{1,97},{33,1},{65,33},{97,65},{2,98}... | collective-permute-start | bytes 1591304 | tf_op jit(solution)/shard_map/ppermute | solution.py:42
  82.1 11.6 %update.4 = (bf16[224,2368]{1,0:T(8,128)(2,1)}, bf16[224,2368]{1,0:T(8,128)(2,1)}, bf16[112,2368]{1,0:T(8,128)(2,1)}, bf16[112,2368]{1,0:T(8,128)(2,1)}, bf16[224,2368]{1,0:T(8,128)(2,1)}) custom-call(s32[4]{0:T(128)} %and_select_fusion.block_ref, bf16[1376,256]{1,0:T(8,128)(2,1)} %join.23.refs_7_.refs_0_.refs_5_, ...), custom_call_target="tpu_custom_call" | custom-call | flops 4345298944 | bytes 10928128 | tf_op jit(solution)/shard_map/update/pallas_call | solution.py:232
  93.7 1.0 copy-done
  96.1 2.7 %collective-permute-start.21 = (bf16[224,2368]{1,0:T(8,128)(2,1)}, bf16[224,2368]{1,0:T(8,128)(2,1)S(1)}, u32[]{:S(2)}, u32[]{:S(2)}) collective-permute-start(bf16[224,2368]{1,0:T(8,128)(2,1)} %get-tuple-element.111), channel_id=1, source_target_pairs={{0,96},{32,0},{64,32},{96,64},{1,97},{33,1},{65,33},{97,65},{2,98}... | collective-permute-start | bytes 3182600 | tf_op jit(solution)/shard_map/ppermute | solution.py:42
  98.8 2.3 %halves.5 = (bf16[1136,256]{1,0:T(8,128)(2,1)}, bf16[1136,256]{1,0:T(8,128)(2,1)}) custom-call(bf16[2272,256]{1,0:T(8,128)(2,1)} %get-tuple-element.100.one_ref.refs_2_.refs_1_, bf16[2272,256]{1,0:T(8,128)(2,1)} %get-tuple-element.101.three_ref.refs_4_), custom_call_target="tpu_custom_call" | custom-call | bytes 2326528 | tf_op jit(solution)/shard_map/halves/pallas_call | solution.py:282
  101.7 2.1 collective-permute-start.17
  103.8 1.5 copy.86.refs_0_
  105.8 7.1 %collective-permute-done.16.refs_0_ = bf16[1136,256]{1,0:T(8,128)(2,1)S(1)} collective-permute-done((bf16[1136,256]{1,0:T(8,128)(2,1)}, bf16[1136,256]{1,0:T(8,128)(2,1)S(1)}, u32[]{:S(2)}, u32[]{:S(2)}) %collective-permute-start.16) | collective-permute-done | bytes 581664 | tf_op jit(solution)/shard_map/ppermute | solution.py:42
  112.9 0.8 copy-done.13
  113.8 0.8 copy-done.16
  114.6 5.2 %collective-permute-start.24 = (bf16[4,1184,256]{2,1,0:T(8,128)(2,1)}, bf16[4,1184,256]{2,1,0:T(8,128)(2,1)S(1)}, u32[]{:S(2)}, u32[]{:S(2)}) collective-permute-start(bf16[4,1184,256]{2,1,0:T(8,128)(2,1)} %join.35), channel_id=1, source_target_pairs={{0,1},{1,0},{2,3},{3,2},{4,5},{5,4},{6,7},{7,6},{8,9},{9,8},{10,11... | collective-permute-start | bytes 7274504 | tf_op jit(solution)/shard_map/ppermute | solution.py:42
  119.8 4.6 %tokens.1.refs_3_.refs_0_ = bf16[1808,512]{1,0:T(8,128)(2,1)} custom-call(s32[2]{0:T(128)} %pad_add_fusion.at_ref, bf16[2272,256]{1,0:T(8,128)(2,1)} %join.26.refs_2_.refs_0_, bf16[2272,256]{1,0:T(8,128)(2,1)} %get-tuple-element.100.one_ref.refs_2_.refs_1_, bf16[1136,256]{1,0:T(8,128)(2,1)} %get-tuple-element.106.refs_2_.refs_1_, ...), custom_call_target="tpu_custom_call" | custom-call | bytes 7340032 | tf_op jit(solution)/shard_map/tokens/pallas_call | solution.py:474
  124.3 1.0 copy-done.6
  125.3 1.0 copy-done.7
  126.4 2.5 %relay.4 = (bf16[112,2368]{1,0:T(8,128)(2,1)}, bf16[112,2368]{1,0:T(8,128)(2,1)}) custom-call(bf16[224,2368]{1,0:T(8,128)(2,1)} %get-tuple-element.112.gp_ref.refs_6_, bf16[224,2368]{1,0:T(8,128)(2,1)} %get-tuple-element.113.gm_ref.refs_7_, bf16[112,2368]{1,0:T(8,128)(2,1)} %get-tuple-element.114.rp_ref, bf16[112,2368]{1,0:T(8,128)(2,1)} %get-tuple-element.115.rm_ref), custom_call_target="tpu_custom_call" | custom-call | bytes 3182592 | tf_op jit(solution)/shard_map/relay/pallas_call | solution.py:263
  129.4 0.9 collective-permute-start.32
  131.3 1.0 copy-done.29
  132.3 19.6 %update.5 = (bf16[224,2368]{1,0:T(8,128)(2,1)}, bf16[224,2368]{1,0:T(8,128)(2,1)}, bf16[112,2368]{1,0:T(8,128)(2,1)}, bf16[112,2368]{1,0:T(8,128)(2,1)}, bf16[224,2368]{1,0:T(8,128)(2,1)}) custom-call(s32[4]{0:T(128)} %and_select_fusion.block_ref, bf16[2272,256]{1,0:T(8,128)(2,1)} %join.26.refs_2_.refs_0_, ...), custom_call_target="tpu_custom_call" | custom-call | flops 8690597888 | bytes 17612800 | tf_op jit(solution)/shard_map/update/pallas_call | solution.py:232
  152.0 2.7 %collective-permute-start.27 = (bf16[224,2368]{1,0:T(8,128)(2,1)}, bf16[224,2368]{1,0:T(8,128)(2,1)S(1)}, u32[]{:S(2)}, u32[]{:S(2)}) collective-permute-start(bf16[224,2368]{1,0:T(8,128)(2,1)} %get-tuple-element.122), channel_id=1, source_target_pairs={{0,96},{32,0},{64,32},{96,64},{1,97},{33,1},{65,33},{97,65},{2,98}... | collective-permute-start | bytes 3182600 | tf_op jit(solution)/shard_map/ppermute | solution.py:42
  155.7 5.2 %up_sums.1 = (f32[224,2368]{1,0:T(8,128)}, bf16[224,2368]{1,0:T(8,128)(2,1)}) custom-call(s32[1]{0:T(128)} %bitcast.13.mine_ref, bf16[224,2368]{1,0:T(8,128)(2,1)} %get-tuple-element.84.refs_3_.refs_0_, bf16[224,2368]{1,0:T(8,128)(2,1)} %get-tuple-element.93.gp_ref.refs_1_, bf16[224,2368]{1,0:T(8,128)(2,1)} %get-tuple-element.94.gm_ref.refs_2_, ...), custom_call_target="tpu_custom_call" | custom-call | tf_op jit(solution)/shard_map/up_sums/pallas_call | solution.py:399
  161.6 17.6 %hidden.1.refs_2_ = bf16[1184,512]{1,0:T(8,128)(2,1)} custom-call(s32[1]{0:T(128)} %bitcast.c_ref, bf16[1808,512]{1,0:T(8,128)(2,1)} %join.34.mine_ref, bf16[1808,512]{1,0:T(8,128)(2,1)} %collective-permute-done.23.other_ref, bf16[1184,3584]{1,0:T(8,128)(2,1)} %bitcast.20, bf16[1184,3584]{1,0:T(8,128)(2,1)} %bitcast.19, bf16[4,1184,256]{2,1,0:T(8,128)(2,1)} %bitcast.16, ...), custom_call_target="tpu_custom_call" | custom-call | flops 11173625856 | bytes 26705920 | tf_op jit(solution)/shard_map/hidden/pallas_call | solution.py:522
  179.2 1.0 copy-done.4
  180.2 1.0 copy-done.5
  181.2 2.5 %relay.5 = (bf16[112,2368]{1,0:T(8,128)(2,1)}, bf16[112,2368]{1,0:T(8,128)(2,1)}) custom-call(bf16[224,2368]{1,0:T(8,128)(2,1)} %get-tuple-element.123.gp_ref, bf16[224,2368]{1,0:T(8,128)(2,1)} %get-tuple-element.124.gm_ref, bf16[112,2368]{1,0:T(8,128)(2,1)} %get-tuple-element.125.rp_ref, bf16[112,2368]{1,0:T(8,128)(2,1)} %get-tuple-element.126.rm_ref), custom_call_target="tpu_custom_call" | custom-call | bytes 3182592 | tf_op jit(solution)/shard_map/relay/pallas_call | solution.py:263
  183.7 2.7 %collective-permute-start.29 = (bf16[112,2368]{1,0:T(8,128)(2,1)}, bf16[112,2368]{1,0:T(8,128)(2,1)S(1)}, u32[]{:S(2)}, u32[]{:S(2)}) collective-permute-start(bf16[112,2368]{1,0:T(8,128)(2,1)} %get-tuple-element.130), channel_id=1, source_target_pairs={{0,96},{32,0},{64,32},{96,64},{1,97},{33,1},{65,33},{97,65},{2,98}... | collective-permute-start | bytes 1591304 | tf_op jit(solution)/shard_map/ppermute | solution.py:42
  186.4 4.0 %gate_early.1 = (f32[224,1184]{1,0:T(8,128)}, f32[224,1184]{1,0:T(8,128)}) custom-call(s32[1]{0:T(128)} %bitcast.c_ref, bf16[448,1184]{1,0:T(8,128)(2,1)} %get-tuple-element.120.held_ref, bf16[224,2368]{1,0:T(8,128)(2,1)} %get-tuple-element.119.refs_0_.own_ref.refs_2_, bf16[224,2368]{1,0:T(8,128)(2,1)} %get-tuple-element.123.gp_ref, ...), custom_call_target="tpu_custom_call" | custom-call | tf_op jit(solution)/shard_map/gate_early/pallas_call | solution.py:325
  190.4 1.0 copy-done.14
  191.4 3.3 %up_sum.1 = (f32[224,1184]{1,0:T(8,128)}, bf16[224,1184]{1,0:T(8,128)(2,1)}) custom-call(f32[224,2368]{1,0:T(8,128)} %get-tuple-element.139.keep_ref, bf16[224,2368]{1,0:T(8,128)(2,1)} %join.39.sent_ref), custom_call_target="tpu_custom_call" | custom-call | tf_op jit(solution)/shard_map/up_sum/pallas_call | solution.py:413
  194.6 2.0 collective-permute-start.34
  196.7 0.8 collective-permute-done.28.refs_0_
  199.1 2.9 %gate_late.1 = (bf16[224,1184]{1,0:T(8,128)(2,1)}, bf16[224,1184]{1,0:T(8,128)(2,1)}) custom-call(f32[224,1184]{1,0:T(8,128)} %get-tuple-element.128.refs_2_.near_ref.refs_1_, f32[224,1184]{1,0:T(8,128)} %get-tuple-element.129.far_ref, bf16[112,2368]{1,0:T(8,128)(2,1)} %get-tuple-element.131.fp_ref, bf16[112,2368]{1,0:T(8,128)(2,1)} %get-tuple-element.132.fm_ref), custom_call_target="tpu_custom_call" | custom-call | tf_op jit(solution)/shard_map/gate_late/pallas_call | solution.py:350
  202.0 2.4 %collective-permute-start.30 = (bf16[224,1184]{1,0:T(8,128)(2,1)}, bf16[224,1184]{1,0:T(8,128)(2,1)S(1)}, u32[]{:S(2)}, u32[]{:S(2)}) collective-permute-start(bf16[224,1184]{1,0:T(8,128)(2,1)} %get-tuple-element.134), channel_id=1, source_target_pairs={{0,1},{1,0},{2,3},{3,2},{4,5},{5,4},{6,7},{7,6},{8,9},{9,8},{10,11... | collective-permute-start | bytes 1591304 | tf_op jit(solution)/shard_map/ppermute | solution.py:42
  205.3 3.1 %renew.1 = bf16[448,1184]{1,0:T(8,128)(2,1)} custom-call(s32[1]{0:T(128)} %bitcast.c_ref, bf16[448,1184]{1,0:T(8,128)(2,1)} %get-tuple-element.135.held_ref, f32[224,1184]{1,0:T(8,128)} %get-tuple-element.141.near_ref, bf16[224,1184]{1,0:T(8,128)(2,1)} %copy-done.27), custom_call_target="tpu_custom_call" | custom-call | tf_op jit(solution)/shard_map/renew/pallas_call | solution.py:440
  209.2 2.5 %gate_rows.1 = bf16[448,1184]{1,0:T(8,128)(2,1)} custom-call(s32[1]{0:T(128)} %bitcast.c_ref, bf16[448,1184]{1,0:T(8,128)(2,1)} %get-tuple-element.120.held_ref, bf16[224,1184]{1,0:T(8,128)(2,1)} %get-tuple-element.133.near_ref, bf16[224,1184]{1,0:T(8,128)(2,1)} %copy-done.26), custom_call_target="tpu_custom_call" | custom-call | tf_op jit(solution)/shard_map/gate_rows/pallas_call | solution.py:375
  (114 shorter events, 13.6 us)
Async XLA Ops:
  0.6 20.9 %collective-permute-start.4 = (bf16[4,1184,256]{2,1,0:T(8,128)(2,1)}, bf16[4,1184,256]{2,1,0:T(8,128)(2,1)}, u32[]{:S(2)}, u32[]{:S(2)}) collective-permute-start(bf16[4,1184,256]{2,1,0:T(8,128)(2,1)} %bitcast.21), channel_id=1, source_target_pairs={{0,1},{1,0},{2,3},{3,2},{4,5},{5,4},{6,7},{7,6},{8,9},{9,8},{10,11... | collective-permute-start | bytes 7274504 | tf_op jit(solution)/shard_map/ppermute | solution.py:42
  5.2 20.8 %collective-permute-start = (bf16[1376,256]{1,0:T(8,128)(2,1)}, bf16[1376,256]{1,0:T(8,128)(2,1)S(1)}, u32[]{:S(2)}, u32[]{:S(2)}) collective-permute-start(bf16[1376,256]{1,0:T(8,128)(2,1)} %get-tuple-element.74.all_ref), channel_id=1, source_target_pairs={{0,2},{2,0},{1,3},{3,1},{4,6},{6,4},{5,7},{7,5},{8,10},{10,8},{9,1... | collective-permute-start | bytes 2113544 | tf_op jit(solution)/shard_map/ppermute | solution.py:42
  8.2 13.3 %collective-permute-start.2 = (bf16[896,256]{1,0:T(8,128)(2,1)}, bf16[896,256]{1,0:T(8,128)(2,1)}, u32[]{:S(2)}, u32[]{:S(2)}) collective-permute-start(bf16[896,256]{1,0:T(8,128)(2,1)} %get-tuple-element.75.refs_0_), channel_id=1, source_target_pairs={{0,4},{4,8},{8,12},{12,0},{1,5},{5,9},{9,13},{13,1},{2,6},{6,10},{... | collective-permute-start | bytes 1376264 | tf_op jit(solution)/shard_map/ppermute | solution.py:42
  9.4 12.1 %collective-permute-start.3 = (bf16[896,256]{1,0:T(8,128)(2,1)}, bf16[896,256]{1,0:T(8,128)(2,1)}, u32[]{:S(2)}, u32[]{:S(2)}) collective-permute-start(bf16[896,256]{1,0:T(8,128)(2,1)} %get-tuple-element.75.refs_0_), channel_id=1, source_target_pairs={{0,12},{4,0},{8,4},{12,8},{1,13},{5,1},{9,5},{13,9},{2,14},{6,2},{... | collective-permute-start | bytes 1376264 | tf_op jit(solution)/shard_map/ppermute | solution.py:42
  23.4 7.4 %collective-permute-start.5 = (bf16[448,256]{1,0:T(8,128)(2,1)}, bf16[448,256]{1,0:T(8,128)(2,1)S(1)}, u32[]{:S(2)}, u32[]{:S(2)}) collective-permute-start(bf16[448,256]{1,0:T(8,128)(2,1)} %get-tuple-element.78), channel_id=1, source_target_pairs={{0,4},{4,8},{8,12},{12,0},{1,5},{5,9},{9,13},{13,1},{2,6},{6,10},{... | collective-permute-start | bytes 688136 | tf_op jit(solution)/shard_map/ppermute | solution.py:42
  24.3 6.5 %collective-permute-start.6 = (bf16[448,256]{1,0:T(8,128)(2,1)}, bf16[448,256]{1,0:T(8,128)(2,1)S(1)}, u32[]{:S(2)}, u32[]{:S(2)}) collective-permute-start(bf16[448,256]{1,0:T(8,128)(2,1)} %get-tuple-element.79), channel_id=1, source_target_pairs={{0,12},{4,0},{8,4},{12,8},{1,13},{5,1},{9,5},{13,9},{2,14},{6,2},{... | collective-permute-start | bytes 688136 | tf_op jit(solution)/shard_map/ppermute | solution.py:42
  26.1 0.9 copy-start.1
  26.9 7.9 %copy-start.30 = (s32[4]{0:T(128)S(1)}, s32[4]{0:T(128)}, u32[]{:S(2)}) copy-start(s32[4]{0:T(128)} %constant.45) | copy-start | bytes 52
  26.9 8.5 %copy-start.22 = (bf16[896,256]{1,0:T(8,128)(2,1)S(1)}, bf16[896,256]{1,0:T(8,128)(2,1)}, u32[]{:S(2)}) copy-start(bf16[896,256]{1,0:T(8,128)(2,1)} %join.20.s_ref) | copy-start | bytes 1376260
  26.9 23.8 %collective-permute-start.9 = (bf16[896,256]{1,0:T(8,128)(2,1)}, bf16[896,256]{1,0:T(8,128)(2,1)S(1)}, u32[]{:S(2)}, u32[]{:S(2)}) collective-permute-start(bf16[896,256]{1,0:T(8,128)(2,1)} %join.20.s_ref), channel_id=1, source_target_pairs={{18,16},{16,2},{2,18},{19,17},{17,3},{3,19},{22,20},{20,6},{6,22},... | collective-permute-start | bytes 1376264 | tf_op jit(solution)/shard_map/ppermute | solution.py:559
  32.2 20.8 %collective-permute-start.7 = (bf16[1376,256]{1,0:T(8,128)(2,1)}, bf16[1376,256]{1,0:T(8,128)(2,1)S(1)}, u32[]{:S(2)}, u32[]{:S(2)}) collective-permute-start(bf16[1376,256]{1,0:T(8,128)(2,1)} %join.23.refs_7_.refs_0_.refs_5_), channel_id=1, source_target_pairs={{0,4},{4,8},{8,12},{12,0},{1,5},{5,9},{9,13},{13,1},{2,6},{6,10},{... | collective-permute-start | bytes 2113544 | tf_op jit(solution)/shard_map/ppermute | solution.py:42
  32.2 20.8 %collective-permute-start.8 = (bf16[1376,256]{1,0:T(8,128)(2,1)}, bf16[1376,256]{1,0:T(8,128)(2,1)S(1)}, u32[]{:S(2)}, u32[]{:S(2)}) collective-permute-start(bf16[1376,256]{1,0:T(8,128)(2,1)} %join.23.refs_7_.refs_0_.refs_5_), channel_id=1, source_target_pairs={{0,12},{4,0},{8,4},{12,8},{1,13},{5,1},{9,5},{13,9},{2,14},{6,2},{... | collective-permute-start | bytes 2113544 | tf_op jit(solution)/shard_map/ppermute | solution.py:42
  35.4 26.7 %collective-permute-start.1 = (bf16[896,256]{1,0:T(8,128)(2,1)S(1)}, bf16[896,256]{1,0:T(8,128)(2,1)}, u32[]{:S(2)}, u32[]{:S(2)}) collective-permute-start(bf16[896,256]{1,0:T(8,128)(2,1)S(1)} %copy-done.22), channel_id=1, source_target_pairs={{16,0},{2,16},{0,2},{17,1},{3,17},{1,3},{20,4},{6,20},{4,6},{21,5}... | collective-permute-start | bytes 1376264 | tf_op jit(solution)/shard_map/ppermute | solution.py:559
  49.0 25.9 %collective-permute-start.14 = (bf16[224,2368]{1,0:T(8,128)(2,1)}, bf16[224,2368]{1,0:T(8,128)(2,1)S(1)}, u32[]{:S(2)}, u32[]{:S(2)}) collective-permute-start(bf16[224,2368]{1,0:T(8,128)(2,1)} %get-tuple-element.91), channel_id=1, source_target_pairs={{0,32},{32,64},{64,96},{96,0},{1,33},{33,65},{65,97},{97,1},{2,34}... | collective-permute-start | bytes 3182600 | tf_op jit(solution)/shard_map/ppermute | solution.py:42
  50.8 2.2 %copy-start.23 = (bf16[896,256]{1,0:T(8,128)(2,1)}, bf16[896,256]{1,0:T(8,128)(2,1)S(1)}, u32[]{:S(2)}) copy-start(bf16[896,256]{1,0:T(8,128)(2,1)S(1)} %collective-permute-done.9.refs_2_) | copy-start | bytes 1376260
  50.8 24.2 %collective-permute-start.15 = (bf16[224,2368]{1,0:T(8,128)(2,1)}, bf16[224,2368]{1,0:T(8,128)(2,1)S(1)}, u32[]{:S(2)}, u32[]{:S(2)}) collective-permute-start(bf16[224,2368]{1,0:T(8,128)(2,1)} %get-tuple-element.92), channel_id=1, source_target_pairs={{0,96},{32,0},{64,32},{96,64},{1,97},{33,1},{65,33},{97,65},{2,98}... | collective-permute-start | bytes 3182600 | tf_op jit(solution)/shard_map/ppermute | solution.py:42
  53.0 0.9 copy-start.2
  53.0 1.1 copy-start.12
  56.1 9.6 %collective-permute-start.10 = (bf16[688,256]{1,0:T(8,128)(2,1)}, bf16[688,256]{1,0:T(8,128)(2,1)S(1)}, u32[]{:S(2)}, u32[]{:S(2)}) collective-permute-start(bf16[688,256]{1,0:T(8,128)(2,1)} %get-tuple-element.88), channel_id=1, source_target_pairs={{0,4},{4,8},{8,12},{12,0},{1,5},{5,9},{9,13},{13,1},{2,6},{6,10},{... | collective-permute-start | bytes 1056776 | tf_op jit(solution)/shard_map/ppermute | solution.py:42
  56.1 9.6 %collective-permute-start.11 = (bf16[688,256]{1,0:T(8,128)(2,1)}, bf16[688,256]{1,0:T(8,128)(2,1)S(1)}, u32[]{:S(2)}, u32[]{:S(2)}) collective-permute-start(bf16[688,256]{1,0:T(8,128)(2,1)} %get-tuple-element.89), channel_id=1, source_target_pairs={{0,12},{4,0},{8,4},{12,8},{1,13},{5,1},{9,5},{13,9},{2,14},{6,2},{... | collective-permute-start | bytes 1056776 | tf_op jit(solution)/shard_map/ppermute | solution.py:42
  64.7 59.6 %collective-permute-start.22 = (bf16[4,1184,256]{2,1,0:T(8,128)(2,1)}, bf16[4,1184,256]{2,1,0:T(8,128)(2,1)}, u32[]{:S(2)}, u32[]{:S(2)}) collective-permute-start(bf16[4,1184,256]{2,1,0:T(8,128)(2,1)} %join.32), channel_id=1, source_target_pairs={{0,16},{16,0},{1,17},{17,1},{2,18},{18,2},{3,19},{19,3},{4,20},{20... | collective-permute-start | bytes 7274504 | tf_op jit(solution)/shard_map/ppermute | solution.py:42
  65.7 0.7 copy-start.15
  66.5 0.7 copy-start.24
  67.2 26.5 %collective-permute-start.12 = (bf16[2272,256]{1,0:T(8,128)(2,1)}, bf16[2272,256]{1,0:T(8,128)(2,1)S(1)}, u32[]{:S(2)}, u32[]{:S(2)}) collective-permute-start(bf16[2272,256]{1,0:T(8,128)(2,1)} %join.26.refs_2_.refs_0_), channel_id=1, source_target_pairs={{0,4},{4,8},{8,12},{12,0},{1,5},{5,9},{9,13},{13,1},{2,6},{6,10},{... | collective-permute-start | bytes 3489800 | tf_op jit(solution)/shard_map/ppermute | solution.py:42
  67.2 26.5 %collective-permute-start.13 = (bf16[2272,256]{1,0:T(8,128)(2,1)}, bf16[2272,256]{1,0:T(8,128)(2,1)S(1)}, u32[]{:S(2)}, u32[]{:S(2)}) collective-permute-start(bf16[2272,256]{1,0:T(8,128)(2,1)} %join.26.refs_2_.refs_0_), channel_id=1, source_target_pairs={{0,12},{4,0},{8,4},{12,8},{1,13},{5,1},{9,5},{13,9},{2,14},{6,2},{... | collective-permute-start | bytes 3489800 | tf_op jit(solution)/shard_map/ppermute | solution.py:42
  74.9 1.0 copy-start.8
  75.9 1.0 copy-start.9
  79.5 15.6 %collective-permute-start.18 = (bf16[112,2368]{1,0:T(8,128)(2,1)}, bf16[112,2368]{1,0:T(8,128)(2,1)S(1)}, u32[]{:S(2)}, u32[]{:S(2)}) collective-permute-start(bf16[112,2368]{1,0:T(8,128)(2,1)} %get-tuple-element.97.refs_7_.refs_2_), channel_id=1, source_target_pairs={{0,32},{32,64},{64,96},{96,0},{1,33},{33,65},{65,97},{97,1},{2,34}... | collective-permute-start | bytes 1591304 | tf_op jit(solution)/shard_map/ppermute | solution.py:42
  79.5 15.6 %collective-permute-start.19 = (bf16[112,2368]{1,0:T(8,128)(2,1)}, bf16[112,2368]{1,0:T(8,128)(2,1)S(1)}, u32[]{:S(2)}, u32[]{:S(2)}) collective-permute-start(bf16[112,2368]{1,0:T(8,128)(2,1)} %get-tuple-element.104), channel_id=1, source_target_pairs={{0,96},{32,0},{64,32},{96,64},{1,97},{33,1},{65,33},{97,65},{2,98}... | collective-permute-start | bytes 1591304 | tf_op jit(solution)/shard_map/ppermute | solution.py:42
  93.7 1.0 copy-start
  93.7 1.4 copy-start.3
  95.1 0.8 copy-start.11
  95.1 1.0 copy-start.21
  96.1 7.6 %copy-start.10 = (bf16[256,4,1184]{0,2,1:T(8,128)(2,1)S(1)}, bf16[256,4,1184]{0,2,1:T(8,128)(2,1)}, u32[]{:S(2)}) copy-start(bf16[256,4,1184]{0,2,1:T(8,128)(2,1)} %param.14) | copy-start | bytes 7274500
  96.1 28.2 %collective-permute-start.20 = (bf16[224,2368]{1,0:T(8,128)(2,1)}, bf16[224,2368]{1,0:T(8,128)(2,1)S(1)}, u32[]{:S(2)}, u32[]{:S(2)}) collective-permute-start(bf16[224,2368]{1,0:T(8,128)(2,1)} %get-tuple-element.110), channel_id=1, source_target_pairs={{0,32},{32,64},{64,96},{96,0},{1,33},{33,65},{65,97},{97,1},{2,34}... | collective-permute-start | bytes 3182600 | tf_op jit(solution)/shard_map/ppermute | solution.py:42
  96.1 28.2 %collective-permute-start.21 = (bf16[224,2368]{1,0:T(8,128)(2,1)}, bf16[224,2368]{1,0:T(8,128)(2,1)S(1)}, u32[]{:S(2)}, u32[]{:S(2)}) collective-permute-start(bf16[224,2368]{1,0:T(8,128)(2,1)} %get-tuple-element.111), channel_id=1, source_target_pairs={{0,96},{32,0},{64,32},{96,64},{1,97},{33,1},{65,33},{97,65},{2,98}... | collective-permute-start | bytes 3182600 | tf_op jit(solution)/shard_map/ppermute | solution.py:42
  101.1 11.8 %collective-permute-start.16 = (bf16[1136,256]{1,0:T(8,128)(2,1)}, bf16[1136,256]{1,0:T(8,128)(2,1)S(1)}, u32[]{:S(2)}, u32[]{:S(2)}) collective-permute-start(bf16[1136,256]{1,0:T(8,128)(2,1)} %get-tuple-element.102), channel_id=1, source_target_pairs={{0,4},{4,8},{8,12},{12,0},{1,5},{5,9},{9,13},{13,1},{2,6},{6,10},{... | collective-permute-start | bytes 1744904 | tf_op jit(solution)/shard_map/ppermute | solution.py:42
  101.7 11.2 %collective-permute-start.17 = (bf16[1136,256]{1,0:T(8,128)(2,1)}, bf16[1136,256]{1,0:T(8,128)(2,1)S(1)}, u32[]{:S(2)}, u32[]{:S(2)}) collective-permute-start(bf16[1136,256]{1,0:T(8,128)(2,1)} %get-tuple-element.103), channel_id=1, source_target_pairs={{0,12},{4,0},{8,4},{12,8},{1,13},{5,1},{9,5},{13,9},{2,14},{6,2},{... | collective-permute-start | bytes 1744904 | tf_op jit(solution)/shard_map/ppermute | solution.py:42
  112.9 0.9 copy-start.13
  113.7 0.8 copy-start.16
  114.6 16.3 %collective-permute-start.24 = (bf16[4,1184,256]{2,1,0:T(8,128)(2,1)}, bf16[4,1184,256]{2,1,0:T(8,128)(2,1)S(1)}, u32[]{:S(2)}, u32[]{:S(2)}) collective-permute-start(bf16[4,1184,256]{2,1,0:T(8,128)(2,1)} %join.35), channel_id=1, source_target_pairs={{0,1},{1,0},{2,3},{3,2},{4,5},{5,4},{6,7},{7,6},{8,9},{9,8},{10,11... | collective-permute-start | bytes 7274504 | tf_op jit(solution)/shard_map/ppermute | solution.py:42
  124.3 1.0 copy-start.6
  125.3 1.0 copy-start.7
  126.3 5.0 %collective-permute-start.25 = (bf16[4,1184,256]{2,1,0:T(8,128)(2,1)}, bf16[4,1184,256]{2,1,0:T(8,128)(2,1)}, u32[]{:S(2)}, u32[]{:S(2)}) collective-permute-start(bf16[4,1184,256]{2,1,0:T(8,128)(2,1)} %get-tuple-element.117.refs_7_), channel_id=1, source_target_pairs={{0,1},{1,0},{2,3},{3,2},{4,5},{5,4},{6,7},{7,6},{8,9},{9,8},{10,11... | collective-permute-start | bytes 7274504 | tf_op jit(solution)/shard_map/ppermute | solution.py:42
  128.9 32.8 %collective-permute-start.23 = (bf16[1808,512]{1,0:T(8,128)(2,1)}, bf16[1808,512]{1,0:T(8,128)(2,1)}, u32[]{:S(2)}, u32[]{:S(2)}) collective-permute-start(bf16[1808,512]{1,0:T(8,128)(2,1)} %join.34.mine_ref), channel_id=1, source_target_pairs={{0,1},{1,0},{2,3},{3,2},{4,5},{5,4},{6,7},{7,6},{8,9},{9,8},{10,11... | collective-permute-start | bytes 5554184 | tf_op jit(solution)/shard_map/ppermute | solution.py:42
  129.4 25.3 %collective-permute-start.32 = (bf16[112,2368]{1,0:T(8,128)(2,1)}, bf16[112,2368]{1,0:T(8,128)(2,1)S(1)}, u32[]{:S(2)}, u32[]{:S(2)}) collective-permute-start(bf16[112,2368]{1,0:T(8,128)(2,1)} %get-tuple-element.116.refs_1_), channel_id=1, source_target_pairs={{0,96},{32,0},{64,32},{96,64},{1,97},{33,1},{65,33},{97,65},{2,98}... | collective-permute-start | bytes 1591304 | tf_op jit(solution)/shard_map/ppermute | solution.py:42
  130.3 24.4 %collective-permute-start.31 = (bf16[112,2368]{1,0:T(8,128)(2,1)}, bf16[112,2368]{1,0:T(8,128)(2,1)S(1)}, u32[]{:S(2)}, u32[]{:S(2)}) collective-permute-start(bf16[112,2368]{1,0:T(8,128)(2,1)} %get-tuple-element.118.refs_9_), channel_id=1, source_target_pairs={{0,32},{32,64},{64,96},{96,0},{1,33},{33,65},{65,97},{97,1},{2,34}... | collective-permute-start | bytes 1591304 | tf_op jit(solution)/shard_map/ppermute | solution.py:42
  130.8 1.5 copy-start.29
  152.0 27.3 %collective-permute-start.26 = (bf16[224,2368]{1,0:T(8,128)(2,1)}, bf16[224,2368]{1,0:T(8,128)(2,1)S(1)}, u32[]{:S(2)}, u32[]{:S(2)}) collective-permute-start(bf16[224,2368]{1,0:T(8,128)(2,1)} %get-tuple-element.121), channel_id=1, source_target_pairs={{0,32},{32,64},{64,96},{96,0},{1,33},{33,65},{65,97},{97,1},{2,34}... | collective-permute-start | bytes 3182600 | tf_op jit(solution)/shard_map/ppermute | solution.py:42
  152.0 27.2 %collective-permute-start.27 = (bf16[224,2368]{1,0:T(8,128)(2,1)}, bf16[224,2368]{1,0:T(8,128)(2,1)S(1)}, u32[]{:S(2)}, u32[]{:S(2)}) collective-permute-start(bf16[224,2368]{1,0:T(8,128)(2,1)} %get-tuple-element.122), channel_id=1, source_target_pairs={{0,96},{32,0},{64,32},{96,64},{1,97},{33,1},{65,33},{97,65},{2,98}... | collective-permute-start | bytes 3182600 | tf_op jit(solution)/shard_map/ppermute | solution.py:42
  154.7 0.8 copy-start.18
  154.7 1.0 copy-start.17
  161.0 29.4 %collective-permute-start.33 = (bf16[224,2368]{1,0:T(8,128)(2,1)}, bf16[224,2368]{1,0:T(8,128)(2,1)S(1)}, u32[]{:S(2)}, u32[]{:S(2)}) collective-permute-start(bf16[224,2368]{1,0:T(8,128)(2,1)} %get-tuple-element.140), channel_id=1, source_target_pairs={{0,16},{16,0},{1,17},{17,1},{2,18},{18,2},{3,19},{19,3},{4,20},{20... | collective-permute-start | bytes 3182600 | tf_op jit(solution)/shard_map/ppermute | solution.py:42
  179.2 1.0 copy-start.4
  180.2 1.0 copy-start.5
  183.7 13.8 %collective-permute-start.28 = (bf16[112,2368]{1,0:T(8,128)(2,1)}, bf16[112,2368]{1,0:T(8,128)(2,1)S(1)}, u32[]{:S(2)}, u32[]{:S(2)}) collective-permute-start(bf16[112,2368]{1,0:T(8,128)(2,1)} %get-tuple-element.127.refs_0_), channel_id=1, source_target_pairs={{0,32},{32,64},{64,96},{96,0},{1,33},{33,65},{65,97},{97,1},{2,34}... | collective-permute-start | bytes 1591304 | tf_op jit(solution)/shard_map/ppermute | solution.py:42
  183.7 13.8 %collective-permute-start.29 = (bf16[112,2368]{1,0:T(8,128)(2,1)}, bf16[112,2368]{1,0:T(8,128)(2,1)S(1)}, u32[]{:S(2)}, u32[]{:S(2)}) collective-permute-start(bf16[112,2368]{1,0:T(8,128)(2,1)} %get-tuple-element.130), channel_id=1, source_target_pairs={{0,96},{32,0},{64,32},{96,64},{1,97},{33,1},{65,33},{97,65},{2,98}... | collective-permute-start | bytes 1591304 | tf_op jit(solution)/shard_map/ppermute | solution.py:42
  190.4 1.0 copy-start.14
  194.6 9.8 %collective-permute-start.34 = (bf16[224,1184]{1,0:T(8,128)(2,1)}, bf16[224,1184]{1,0:T(8,128)(2,1)S(1)}, u32[]{:S(2)}, u32[]{:S(2)}) collective-permute-start(bf16[224,1184]{1,0:T(8,128)(2,1)} %get-tuple-element.142), channel_id=1, source_target_pairs={{0,1},{1,0},{2,3},{3,2},{4,5},{5,4},{6,7},{7,6},{8,9},{9,8},{10,11... | collective-permute-start | bytes 1591304 | tf_op jit(solution)/shard_map/ppermute | solution.py:42
  197.5 0.8 copy-start.19
  198.3 0.8 copy-start.20
  202.0 6.3 %collective-permute-start.30 = (bf16[224,1184]{1,0:T(8,128)(2,1)}, bf16[224,1184]{1,0:T(8,128)(2,1)S(1)}, u32[]{:S(2)}, u32[]{:S(2)}) collective-permute-start(bf16[224,1184]{1,0:T(8,128)(2,1)} %get-tuple-element.134), channel_id=1, source_target_pairs={{0,1},{1,0},{2,3},{3,2},{4,5},{5,4},{6,7},{7,6},{8,9},{9,8},{10,11... | collective-permute-start | bytes 1591304 | tf_op jit(solution)/shard_map/ppermute | solution.py:42
  204.4 0.8 copy-start.27
  208.3 0.8 copy-start.26
  (2 other events, 1.4 us)

commit v3 on v2

--- a/solution.py
+++ b/solution.py
@@ -515,7 +515,7 @@
     t = mine.shape[1]
     q, d = wg.shape
     rank, _, m = bg.shape
-    block = 304
+    block = 240
     w_spec = pl.BlockSpec((block, d), lambda i: (i, 0))
     b_spec = pl.BlockSpec((rank, block, m), lambda i: (0, i, 0))
     t_spec = pl.BlockSpec(mine.shape, lambda i: (0, 0), pipeline_mode=pl.Buffered(1))

time: 212 us -> 212 us (level)
  no operation moved by 1% of the time
where the time goes in v3:
time: 212 us; the launch traced here: 211 us
  Pallas kernels  105 us (50%)
  starting transfers between devices  51.7 us (24%)
  local copies, waits for them, and re-layouts  32.2 us (15%)
  waiting for transfers between devices  20.9 us (10%)
    ppermute x33, starting transfers between devices, swap(): return lax.ppermute(v, axis, [(i, (i + shift) % n) for i in range(n)])  48.5 us
    pallas_call x3, Pallas kernels, update(): _call(functools.partial(_update_kernel, coeff, slabs, d, q - CUT, len(sec...  42.5 us
    unnamed x66, local copies, waits for them, and re-layouts  29 us
    ppermute x33, waiting for transfers between devices, swap(): return lax.ppermute(v, axis, [(i, (i + shift) % n) for i in range(n)])  20.9 us
    pallas_call x1, Pallas kernels, hidden_of(): _call(_hidden_kernel, 'hidden', flops=4 * q * t * (d + rank * m), moved=2...  17.3 us
    pallas_call x3, Pallas kernels, relay(): _call(_relay_kernel, 'relay', grid=(2,), moved=12 * rp.size, in_specs=[sp...  7.56 us
    pallas_call x3, Pallas kernels, halves(): _call(_halves_kernel, 'halves', grid=(1,), moved=8 * n * m, in_specs=[_at...  6.09 us
    pallas_call x1, Pallas kernels, up_sums(): _call(kernel, 'up_sums', grid=(2,), in_specs=[SCALARS] + [pl.BlockSpec((p...  5.25 us
  transfers between devices with their start and end apart: 35, of which 6 were waited for; matrix products, arithmetic and copies ran while one was open for 6% of the time, Pallas kernels for 48%

profile of v3, /device:TPU:1, one launch (start us, length us, event | category | flops | bytes accessed | tf_op | source)
XLA Modules:
  0.0 211.4 jit_solution(14742378966418263700)
XLA Ops:
  0.6 1.5 collective-permute-start.4
  2.1 3.1 %pack.1 = (bf16[896,256]{1,0:T(8,128)(2,1)}, bf16[896,256]{1,0:T(8,128)(2,1)}, bf16[1376,256]{1,0:T(8,128)(2,1)}) custom-call(bf16[224,512]{1,0:T(8,128)(2,1)} %bitcast.27, bf16[4,224,256]{2,1,0:T(8,128)(2,1)} %bitcast.25, bf16[4,224,256]{2,1,0:T(8,128)(2,1)} %bitcast.26, f32[1,256]{1,0:T(1,128)} %bitcast.28), custom_call_target="tpu_custom_call" | custom-call | flops 469762048 | bytes 1835008 | tf_op jit(solution)/shard_map/pack/pallas_call | solution.py:95
  5.2 3.0 %collective-permute-start = (bf16[1376,256]{1,0:T(8,128)(2,1)}, bf16[1376,256]{1,0:T(8,128)(2,1)S(1)}, u32[]{:S(2)}, u32[]{:S(2)}) collective-permute-start(bf16[1376,256]{1,0:T(8,128)(2,1)} %get-tuple-element.74.all_ref), channel_id=1, source_target_pairs={{0,2},{2,0},{1,3},{3,1},{4,6},{6,4},{5,7},{7,5},{8,10},{10,8},{9,1... | collective-permute-start | bytes 2113544 | tf_op jit(solution)/shard_map/ppermute | solution.py:42
  8.2 1.2 collective-permute-start.2
  9.4 1.5 collective-permute-start.3
  10.9 3.2 %constant_dynamic-slice_fusion = (bf16[448,1184]{0,1:T(8,128)(2,1)S(1)}, bf16[448,1184]{0,1:T(8,128)(2,1)S(1)}) fusion(bf16[3584,1184]{0,1:T(8,128)(2,1)} %param.11, s32[]{:T(128)S(6)} %select_n.11, bf16[3584,1184]{0,1:T(8,128)(2,1)} %param.10), kind=kLoop, calls=%fused_computation.5 | loop fusion | bytes 4243460 | tf_op jit(solution)/shard_map/dynamic_slice | solution.py:553
  14.1 1.6 copy.53.refs_3_
  15.7 1.5 copy.54.refs_4_
  17.2 4.4 %collective-permute-done.2.refs_0_ = bf16[896,256]{1,0:T(8,128)(2,1)} collective-permute-done((bf16[896,256]{1,0:T(8,128)(2,1)}, bf16[896,256]{1,0:T(8,128)(2,1)}, u32[]{:S(2)}, u32[]{:S(2)}) %collective-permute-start.2) | collective-permute-done | bytes 458784 | tf_op jit(solution)/shard_map/ppermute | solution.py:42
  21.6 1.8 halves.3
  23.4 0.9 collective-permute-start.5
  24.3 1.8 collective-permute-start.6
  26.1 0.9 copy-done.1
  27.8 3.0 %collective-permute-done.5.refs_0_ = bf16[448,256]{1,0:T(8,128)(2,1)S(1)} collective-permute-done((bf16[448,256]{1,0:T(8,128)(2,1)}, bf16[448,256]{1,0:T(8,128)(2,1)S(1)}, u32[]{:S(2)}, u32[]{:S(2)}) %collective-permute-start.5) | collective-permute-done | bytes 229408 | tf_op jit(solution)/shard_map/ppermute | solution.py:42
  32.2 2.7 %collective-permute-start.8 = (bf16[1376,256]{1,0:T(8,128)(2,1)}, bf16[1376,256]{1,0:T(8,128)(2,1)S(1)}, u32[]{:S(2)}, u32[]{:S(2)}) collective-permute-start(bf16[1376,256]{1,0:T(8,128)(2,1)} %join.23.refs_7_.refs_0_.refs_5_), channel_id=1, source_target_pairs={{0,12},{4,0},{8,4},{12,8},{1,13},{5,1},{9,5},{13,9},{2,14},{6,2},{... | collective-permute-start | bytes 2113544 | tf_op jit(solution)/shard_map/ppermute | solution.py:42
  35.4 2.4 %collective-permute-start.1 = (bf16[896,256]{1,0:T(8,128)(2,1)S(1)}, bf16[896,256]{1,0:T(8,128)(2,1)}, u32[]{:S(2)}, u32[]{:S(2)}) collective-permute-start(bf16[896,256]{1,0:T(8,128)(2,1)S(1)} %copy-done.22), channel_id=1, source_target_pairs={{16,0},{2,16},{0,2},{17,1},{3,17},{1,3},{20,4},{6,20},{4,6},{21,5}... | collective-permute-start | bytes 1376264 | tf_op jit(solution)/shard_map/ppermute | solution.py:559
  37.8 11.3 %update.3 = (bf16[224,2368]{1,0:T(8,128)(2,1)}, bf16[224,2368]{1,0:T(8,128)(2,1)}, bf16[112,2368]{1,0:T(8,128)(2,1)}, bf16[112,2368]{1,0:T(8,128)(2,1)}, bf16[224,2368]{1,0:T(8,128)(2,1)}) custom-call(s32[4]{0:T(128)} %and_select_fusion.block_ref, bf16[896,256]{1,0:T(8,128)(2,1)} %get-tuple-element.75.refs_0_, ...), custom_call_target="tpu_custom_call" | custom-call | flops 4345298944 | bytes 10928128 | tf_op jit(solution)/shard_map/update/pallas_call | solution.py:232
  49.0 1.7 collective-permute-start.14
  50.8 2.2 %collective-permute-start.15 = (bf16[224,2368]{1,0:T(8,128)(2,1)}, bf16[224,2368]{1,0:T(8,128)(2,1)S(1)}, u32[]{:S(2)}, u32[]{:S(2)}) collective-permute-start(bf16[224,2368]{1,0:T(8,128)(2,1)} %get-tuple-element.92), channel_id=1, source_target_pairs={{0,96},{32,0},{64,32},{96,64},{1,97},{33,1},{65,33},{97,65},{2,98}... | collective-permute-start | bytes 3182600 | tf_op jit(solution)/shard_map/ppermute | solution.py:42
  53.0 0.8 copy-done.2
  54.1 2.0 halves.4
  56.1 2.6 %collective-permute-start.11 = (bf16[688,256]{1,0:T(8,128)(2,1)}, bf16[688,256]{1,0:T(8,128)(2,1)S(1)}, u32[]{:S(2)}, u32[]{:S(2)}) collective-permute-start(bf16[688,256]{1,0:T(8,128)(2,1)} %get-tuple-element.89), channel_id=1, source_target_pairs={{0,12},{4,0},{8,4},{12,8},{1,13},{5,1},{9,5},{13,9},{2,14},{6,2},{... | collective-permute-start | bytes 1056776 | tf_op jit(solution)/shard_map/ppermute | solution.py:42
  58.8 3.3 %copy.81.refs_0_ = bf16[4,1184,256]{2,1,0:T(8,128)(2,1)} copy(bf16[4,1184,256]{2,1,0:T(8,128)(2,1)} %bitcast.14) | data formatting | bytes 4849664
  62.1 2.6 %pick.1.refs_2_.refs_0_.refs_1_ = bf16[2272,256]{1,0:T(8,128)(2,1)} custom-call(s32[1]{0:T(128)} %bitcast.3.y_ref, bf16[896,256]{1,0:T(8,128)(2,1)} %join.20.s_ref, bf16[896,256]{1,0:T(8,128)(2,1)} %collective-permute-done.1.pa_ref, bf16[896,256]{1,0:T(8,128)(2,1)} %get-tuple-element.85.pb_ref, bf16[1376,256]{1,0:T(8,128)(2,1)} %get-tuple-element.74.all_ref, ...), custom_call_target="tpu_custom_call" | custom-call | bytes 1835008 | tf_op jit(solution)/shard_map/pick/pallas_call | solution.py:127
  64.7 1.0 collective-permute-start.22
  67.2 2.7 %collective-permute-start.13 = (bf16[2272,256]{1,0:T(8,128)(2,1)}, bf16[2272,256]{1,0:T(8,128)(2,1)S(1)}, u32[]{:S(2)}, u32[]{:S(2)}) collective-permute-start(bf16[2272,256]{1,0:T(8,128)(2,1)} %join.26.refs_2_.refs_0_), channel_id=1, source_target_pairs={{0,12},{4,0},{8,4},{12,8},{1,13},{5,1},{9,5},{13,9},{2,14},{6,2},{... | collective-permute-start | bytes 3489800 | tf_op jit(solution)/shard_map/ppermute | solution.py:42
  69.9 5.0 %collective-permute-done.14.refs_0_ = bf16[224,2368]{1,0:T(8,128)(2,1)S(1)} collective-permute-done((bf16[224,2368]{1,0:T(8,128)(2,1)}, bf16[224,2368]{1,0:T(8,128)(2,1)S(1)}, u32[]{:S(2)}, u32[]{:S(2)}) %collective-permute-start.14) | collective-permute-done | bytes 1060896 | tf_op jit(solution)/shard_map/ppermute | solution.py:42
  74.9 1.0 copy-done.8
  75.9 1.0 copy-done.9
  76.9 2.5 %relay.3 = (bf16[112,2368]{1,0:T(8,128)(2,1)}, bf16[112,2368]{1,0:T(8,128)(2,1)}) custom-call(bf16[224,2368]{1,0:T(8,128)(2,1)} %get-tuple-element.93.gp_ref.refs_1_, bf16[224,2368]{1,0:T(8,128)(2,1)} %get-tuple-element.94.gm_ref.refs_2_, bf16[112,2368]{1,0:T(8,128)(2,1)} %get-tuple-element.95.rp_ref, bf16[112,2368]{1,0:T(8,128)(2,1)} %get-tuple-element.96.rm_ref), custom_call_target="tpu_custom_call" | custom-call | bytes 3182592 | tf_op jit(solution)/shard_map/relay/pallas_call | solution.py:263
  79.5 2.7 %collective-permute-start.19 = (bf16[112,2368]{1,0:T(8,128)(2,1)}, bf16[112,2368]{1,0:T(8,128)(2,1)S(1)}, u32[]{:S(2)}, u32[]{:S(2)}) collective-permute-start(bf16[112,2368]{1,0:T(8,128)(2,1)} %get-tuple-element.104), channel_id=1, source_target_pairs={{0,96},{32,0},{64,32},{96,64},{1,97},{33,1},{65,33},{97,65},{2,98}... | collective-permute-start | bytes 1591304 | tf_op jit(solution)/shard_map/ppermute | solution.py:42
  82.1 11.6 %update.4 = (bf16[224,2368]{1,0:T(8,128)(2,1)}, bf16[224,2368]{1,0:T(8,128)(2,1)}, bf16[112,2368]{1,0:T(8,128)(2,1)}, bf16[112,2368]{1,0:T(8,128)(2,1)}, bf16[224,2368]{1,0:T(8,128)(2,1)}) custom-call(s32[4]{0:T(128)} %and_select_fusion.block_ref, bf16[1376,256]{1,0:T(8,128)(2,1)} %join.23.refs_7_.refs_0_.refs_5_, ...), custom_call_target="tpu_custom_call" | custom-call | flops 4345298944 | bytes 10928128 | tf_op jit(solution)/shard_map/update/pallas_call | solution.py:232
  93.7 1.0 copy-done
  96.1 2.7 %collective-permute-start.21 = (bf16[224,2368]{1,0:T(8,128)(2,1)}, bf16[224,2368]{1,0:T(8,128)(2,1)S(1)}, u32[]{:S(2)}, u32[]{:S(2)}) collective-permute-start(bf16[224,2368]{1,0:T(8,128)(2,1)} %get-tuple-element.111), channel_id=1, source_target_pairs={{0,96},{32,0},{64,32},{96,64},{1,97},{33,1},{65,33},{97,65},{2,98}... | collective-permute-start | bytes 3182600 | tf_op jit(solution)/shard_map/ppermute | solution.py:42
  98.8 2.3 %halves.5 = (bf16[1136,256]{1,0:T(8,128)(2,1)}, bf16[1136,256]{1,0:T(8,128)(2,1)}) custom-call(bf16[2272,256]{1,0:T(8,128)(2,1)} %get-tuple-element.100.one_ref.refs_2_.refs_1_, bf16[2272,256]{1,0:T(8,128)(2,1)} %get-tuple-element.101.three_ref.refs_4_), custom_call_target="tpu_custom_call" | custom-call | bytes 2326528 | tf_op jit(solution)/shard_map/halves/pallas_call | solution.py:282
  101.7 2.1 collective-permute-start.17
  103.8 1.5 copy.86.refs_0_
  105.8 7.1 %collective-permute-done.16.refs_0_ = bf16[1136,256]{1,0:T(8,128)(2,1)S(1)} collective-permute-done((bf16[1136,256]{1,0:T(8,128)(2,1)}, bf16[1136,256]{1,0:T(8,128)(2,1)S(1)}, u32[]{:S(2)}, u32[]{:S(2)}) %collective-permute-start.16) | collective-permute-done | bytes 581664 | tf_op jit(solution)/shard_map/ppermute | solution.py:42
  112.9 0.8 copy-done.13
  113.8 0.8 copy-done.16
  114.6 5.2 %collective-permute-start.24 = (bf16[4,1184,256]{2,1,0:T(8,128)(2,1)}, bf16[4,1184,256]{2,1,0:T(8,128)(2,1)S(1)}, u32[]{:S(2)}, u32[]{:S(2)}) collective-permute-start(bf16[4,1184,256]{2,1,0:T(8,128)(2,1)} %join.35), channel_id=1, source_target_pairs={{0,1},{1,0},{2,3},{3,2},{4,5},{5,4},{6,7},{7,6},{8,9},{9,8},{10,11... | collective-permute-start | bytes 7274504 | tf_op jit(solution)/shard_map/ppermute | solution.py:42
  119.8 4.6 %tokens.1.refs_3_.refs_0_ = bf16[1808,512]{1,0:T(8,128)(2,1)} custom-call(s32[2]{0:T(128)} %pad_add_fusion.at_ref, bf16[2272,256]{1,0:T(8,128)(2,1)} %join.26.refs_2_.refs_0_, bf16[2272,256]{1,0:T(8,128)(2,1)} %get-tuple-element.100.one_ref.refs_2_.refs_1_, bf16[1136,256]{1,0:T(8,128)(2,1)} %get-tuple-element.106.refs_2_.refs_1_, ...), custom_call_target="tpu_custom_call" | custom-call | bytes 7340032 | tf_op jit(solution)/shard_map/tokens/pallas_call | solution.py:474
  124.3 1.0 copy-done.6
  125.3 1.0 copy-done.7
  126.4 2.5 %relay.4 = (bf16[112,2368]{1,0:T(8,128)(2,1)}, bf16[112,2368]{1,0:T(8,128)(2,1)}) custom-call(bf16[224,2368]{1,0:T(8,128)(2,1)} %get-tuple-element.112.gp_ref.refs_6_, bf16[224,2368]{1,0:T(8,128)(2,1)} %get-tuple-element.113.gm_ref.refs_7_, bf16[112,2368]{1,0:T(8,128)(2,1)} %get-tuple-element.114.rp_ref, bf16[112,2368]{1,0:T(8,128)(2,1)} %get-tuple-element.115.rm_ref), custom_call_target="tpu_custom_call" | custom-call | bytes 3182592 | tf_op jit(solution)/shard_map/relay/pallas_call | solution.py:263
  129.4 0.9 collective-permute-start.32
  131.3 1.0 copy-done.29
  132.3 19.6 %update.5 = (bf16[224,2368]{1,0:T(8,128)(2,1)}, bf16[224,2368]{1,0:T(8,128)(2,1)}, bf16[112,2368]{1,0:T(8,128)(2,1)}, bf16[112,2368]{1,0:T(8,128)(2,1)}, bf16[224,2368]{1,0:T(8,128)(2,1)}) custom-call(s32[4]{0:T(128)} %and_select_fusion.block_ref, bf16[2272,256]{1,0:T(8,128)(2,1)} %join.26.refs_2_.refs_0_, ...), custom_call_target="tpu_custom_call" | custom-call | flops 8690597888 | bytes 17612800 | tf_op jit(solution)/shard_map/update/pallas_call | solution.py:232
  152.0 2.7 %collective-permute-start.27 = (bf16[224,2368]{1,0:T(8,128)(2,1)}, bf16[224,2368]{1,0:T(8,128)(2,1)S(1)}, u32[]{:S(2)}, u32[]{:S(2)}) collective-permute-start(bf16[224,2368]{1,0:T(8,128)(2,1)} %get-tuple-element.122), channel_id=1, source_target_pairs={{0,96},{32,0},{64,32},{96,64},{1,97},{33,1},{65,33},{97,65},{2,98}... | collective-permute-start | bytes 3182600 | tf_op jit(solution)/shard_map/ppermute | solution.py:42
  155.7 5.2 %up_sums.1 = (f32[224,2368]{1,0:T(8,128)}, bf16[224,2368]{1,0:T(8,128)(2,1)}) custom-call(s32[1]{0:T(128)} %bitcast.13.mine_ref, bf16[224,2368]{1,0:T(8,128)(2,1)} %get-tuple-element.84.refs_3_.refs_0_, bf16[224,2368]{1,0:T(8,128)(2,1)} %get-tuple-element.93.gp_ref.refs_1_, bf16[224,2368]{1,0:T(8,128)(2,1)} %get-tuple-element.94.gm_ref.refs_2_, ...), custom_call_target="tpu_custom_call" | custom-call | tf_op jit(solution)/shard_map/up_sums/pallas_call | solution.py:399
  161.6 17.3 %hidden.1.refs_2_ = bf16[1184,512]{1,0:T(8,128)(2,1)} custom-call(s32[1]{0:T(128)} %bitcast.c_ref, bf16[1808,512]{1,0:T(8,128)(2,1)} %join.34.mine_ref, bf16[1808,512]{1,0:T(8,128)(2,1)} %collective-permute-done.23.other_ref, bf16[1184,3584]{1,0:T(8,128)(2,1)} %bitcast.20, bf16[1184,3584]{1,0:T(8,128)(2,1)} %bitcast.19, bf16[4,1184,256]{2,1,0:T(8,128)(2,1)} %bitcast.16, ...), custom_call_target="tpu_custom_call" | custom-call | flops 11173625856 | bytes 26705920 | tf_op jit(solution)/shard_map/hidden/pallas_call | solution.py:522
  179.0 1.0 copy-done.4
  179.9 1.0 copy-done.5
  180.9 2.5 %relay.5 = (bf16[112,2368]{1,0:T(8,128)(2,1)}, bf16[112,2368]{1,0:T(8,128)(2,1)}) custom-call(bf16[224,2368]{1,0:T(8,128)(2,1)} %get-tuple-element.123.gp_ref, bf16[224,2368]{1,0:T(8,128)(2,1)} %get-tuple-element.124.gm_ref, bf16[112,2368]{1,0:T(8,128)(2,1)} %get-tuple-element.125.rp_ref, bf16[112,2368]{1,0:T(8,128)(2,1)} %get-tuple-element.126.rm_ref), custom_call_target="tpu_custom_call" | custom-call | bytes 3182592 | tf_op jit(solution)/shard_map/relay/pallas_call | solution.py:263
  183.5 2.7 %collective-permute-start.29 = (bf16[112,2368]{1,0:T(8,128)(2,1)}, bf16[112,2368]{1,0:T(8,128)(2,1)S(1)}, u32[]{:S(2)}, u32[]{:S(2)}) collective-permute-start(bf16[112,2368]{1,0:T(8,128)(2,1)} %get-tuple-element.130), channel_id=1, source_target_pairs={{0,96},{32,0},{64,32},{96,64},{1,97},{33,1},{65,33},{97,65},{2,98}... | collective-permute-start | bytes 1591304 | tf_op jit(solution)/shard_map/ppermute | solution.py:42
  186.1 4.0 %gate_early.1 = (f32[224,1184]{1,0:T(8,128)}, f32[224,1184]{1,0:T(8,128)}) custom-call(s32[1]{0:T(128)} %bitcast.c_ref, bf16[448,1184]{1,0:T(8,128)(2,1)} %get-tuple-element.120.held_ref, bf16[224,2368]{1,0:T(8,128)(2,1)} %get-tuple-element.119.refs_0_.own_ref.refs_2_, bf16[224,2368]{1,0:T(8,128)(2,1)} %get-tuple-element.123.gp_ref, ...), custom_call_target="tpu_custom_call" | custom-call | tf_op jit(solution)/shard_map/gate_early/pallas_call | solution.py:325
  190.1 1.0 copy-done.14
  191.1 3.3 %up_sum.1 = (f32[224,1184]{1,0:T(8,128)}, bf16[224,1184]{1,0:T(8,128)(2,1)}) custom-call(f32[224,2368]{1,0:T(8,128)} %get-tuple-element.139.keep_ref, bf16[224,2368]{1,0:T(8,128)(2,1)} %join.39.sent_ref), custom_call_target="tpu_custom_call" | custom-call | tf_op jit(solution)/shard_map/up_sum/pallas_call | solution.py:413
  194.4 2.0 collective-permute-start.34
  196.4 0.8 collective-permute-done.28.refs_0_
  198.9 2.9 %gate_late.1 = (bf16[224,1184]{1,0:T(8,128)(2,1)}, bf16[224,1184]{1,0:T(8,128)(2,1)}) custom-call(f32[224,1184]{1,0:T(8,128)} %get-tuple-element.128.refs_2_.near_ref.refs_1_, f32[224,1184]{1,0:T(8,128)} %get-tuple-element.129.far_ref, bf16[112,2368]{1,0:T(8,128)(2,1)} %get-tuple-element.131.fp_ref, bf16[112,2368]{1,0:T(8,128)(2,1)} %get-tuple-element.132.fm_ref), custom_call_target="tpu_custom_call" | custom-call | tf_op jit(solution)/shard_map/gate_late/pallas_call | solution.py:350
  201.8 2.4 %collective-permute-start.30 = (bf16[224,1184]{1,0:T(8,128)(2,1)}, bf16[224,1184]{1,0:T(8,128)(2,1)S(1)}, u32[]{:S(2)}, u32[]{:S(2)}) collective-permute-start(bf16[224,1184]{1,0:T(8,128)(2,1)} %get-tuple-element.134), channel_id=1, source_target_pairs={{0,1},{1,0},{2,3},{3,2},{4,5},{5,4},{6,7},{7,6},{8,9},{9,8},{10,11... | collective-permute-start | bytes 1591304 | tf_op jit(solution)/shard_map/ppermute | solution.py:42
  205.0 3.1 %renew.1 = bf16[448,1184]{1,0:T(8,128)(2,1)} custom-call(s32[1]{0:T(128)} %bitcast.c_ref, bf16[448,1184]{1,0:T(8,128)(2,1)} %get-tuple-element.135.held_ref, f32[224,1184]{1,0:T(8,128)} %get-tuple-element.141.near_ref, bf16[224,1184]{1,0:T(8,128)(2,1)} %copy-done.27), custom_call_target="tpu_custom_call" | custom-call | tf_op jit(solution)/shard_map/renew/pallas_call | solution.py:440
  208.9 2.5 %gate_rows.1 = bf16[448,1184]{1,0:T(8,128)(2,1)} custom-call(s32[1]{0:T(128)} %bitcast.c_ref, bf16[448,1184]{1,0:T(8,128)(2,1)} %get-tuple-element.120.held_ref, bf16[224,1184]{1,0:T(8,128)(2,1)} %get-tuple-element.133.near_ref, bf16[224,1184]{1,0:T(8,128)(2,1)} %copy-done.26), custom_call_target="tpu_custom_call" | custom-call | tf_op jit(solution)/shard_map/gate_rows/pallas_call | solution.py:375
  (114 shorter events, 13.6 us)
Async XLA Ops:
  0.6 20.9 %collective-permute-start.4 = (bf16[4,1184,256]{2,1,0:T(8,128)(2,1)}, bf16[4,1184,256]{2,1,0:T(8,128)(2,1)}, u32[]{:S(2)}, u32[]{:S(2)}) collective-permute-start(bf16[4,1184,256]{2,1,0:T(8,128)(2,1)} %bitcast.21), channel_id=1, source_target_pairs={{0,1},{1,0},{2,3},{3,2},{4,5},{5,4},{6,7},{7,6},{8,9},{9,8},{10,11... | collective-permute-start | bytes 7274504 | tf_op jit(solution)/shard_map/ppermute | solution.py:42
  5.2 20.8 %collective-permute-start = (bf16[1376,256]{1,0:T(8,128)(2,1)}, bf16[1376,256]{1,0:T(8,128)(2,1)S(1)}, u32[]{:S(2)}, u32[]{:S(2)}) collective-permute-start(bf16[1376,256]{1,0:T(8,128)(2,1)} %get-tuple-element.74.all_ref), channel_id=1, source_target_pairs={{0,2},{2,0},{1,3},{3,1},{4,6},{6,4},{5,7},{7,5},{8,10},{10,8},{9,1... | collective-permute-start | bytes 2113544 | tf_op jit(solution)/shard_map/ppermute | solution.py:42
  8.2 13.3 %collective-permute-start.2 = (bf16[896,256]{1,0:T(8,128)(2,1)}, bf16[896,256]{1,0:T(8,128)(2,1)}, u32[]{:S(2)}, u32[]{:S(2)}) collective-permute-start(bf16[896,256]{1,0:T(8,128)(2,1)} %get-tuple-element.75.refs_0_), channel_id=1, source_target_pairs={{0,4},{4,8},{8,12},{12,0},{1,5},{5,9},{9,13},{13,1},{2,6},{6,10},{... | collective-permute-start | bytes 1376264 | tf_op jit(solution)/shard_map/ppermute | solution.py:42
  9.4 12.1 %collective-permute-start.3 = (bf16[896,256]{1,0:T(8,128)(2,1)}, bf16[896,256]{1,0:T(8,128)(2,1)}, u32[]{:S(2)}, u32[]{:S(2)}) collective-permute-start(bf16[896,256]{1,0:T(8,128)(2,1)} %get-tuple-element.75.refs_0_), channel_id=1, source_target_pairs={{0,12},{4,0},{8,4},{12,8},{1,13},{5,1},{9,5},{13,9},{2,14},{6,2},{... | collective-permute-start | bytes 1376264 | tf_op jit(solution)/shard_map/ppermute | solution.py:42
  23.4 7.4 %collective-permute-start.5 = (bf16[448,256]{1,0:T(8,128)(2,1)}, bf16[448,256]{1,0:T(8,128)(2,1)S(1)}, u32[]{:S(2)}, u32[]{:S(2)}) collective-permute-start(bf16[448,256]{1,0:T(8,128)(2,1)} %get-tuple-element.78), channel_id=1, source_target_pairs={{0,4},{4,8},{8,12},{12,0},{1,5},{5,9},{9,13},{13,1},{2,6},{6,10},{... | collective-permute-start | bytes 688136 | tf_op jit(solution)/shard_map/ppermute | solution.py:42
  24.3 6.5 %collective-permute-start.6 = (bf16[448,256]{1,0:T(8,128)(2,1)}, bf16[448,256]{1,0:T(8,128)(2,1)S(1)}, u32[]{:S(2)}, u32[]{:S(2)}) collective-permute-start(bf16[448,256]{1,0:T(8,128)(2,1)} %get-tuple-element.79), channel_id=1, source_target_pairs={{0,12},{4,0},{8,4},{12,8},{1,13},{5,1},{9,5},{13,9},{2,14},{6,2},{... | collective-permute-start | bytes 688136 | tf_op jit(solution)/shard_map/ppermute | solution.py:42
  26.1 0.9 copy-start.1
  26.9 7.9 %copy-start.30 = (s32[4]{0:T(128)S(1)}, s32[4]{0:T(128)}, u32[]{:S(2)}) copy-start(s32[4]{0:T(128)} %constant.45) | copy-start | bytes 52
  26.9 8.5 %copy-start.22 = (bf16[896,256]{1,0:T(8,128)(2,1)S(1)}, bf16[896,256]{1,0:T(8,128)(2,1)}, u32[]{:S(2)}) copy-start(bf16[896,256]{1,0:T(8,128)(2,1)} %join.20.s_ref) | copy-start | bytes 1376260
  26.9 23.8 %collective-permute-start.9 = (bf16[896,256]{1,0:T(8,128)(2,1)}, bf16[896,256]{1,0:T(8,128)(2,1)S(1)}, u32[]{:S(2)}, u32[]{:S(2)}) collective-permute-start(bf16[896,256]{1,0:T(8,128)(2,1)} %join.20.s_ref), channel_id=1, source_target_pairs={{18,16},{16,2},{2,18},{19,17},{17,3},{3,19},{22,20},{20,6},{6,22},... | collective-permute-start | bytes 1376264 | tf_op jit(solution)/shard_map/ppermute | solution.py:559
  32.2 20.8 %collective-permute-start.7 = (bf16[1376,256]{1,0:T(8,128)(2,1)}, bf16[1376,256]{1,0:T(8,128)(2,1)S(1)}, u32[]{:S(2)}, u32[]{:S(2)}) collective-permute-start(bf16[1376,256]{1,0:T(8,128)(2,1)} %join.23.refs_7_.refs_0_.refs_5_), channel_id=1, source_target_pairs={{0,4},{4,8},{8,12},{12,0},{1,5},{5,9},{9,13},{13,1},{2,6},{6,10},{... | collective-permute-start | bytes 2113544 | tf_op jit(solution)/shard_map/ppermute | solution.py:42
  32.2 20.8 %collective-permute-start.8 = (bf16[1376,256]{1,0:T(8,128)(2,1)}, bf16[1376,256]{1,0:T(8,128)(2,1)S(1)}, u32[]{:S(2)}, u32[]{:S(2)}) collective-permute-start(bf16[1376,256]{1,0:T(8,128)(2,1)} %join.23.refs_7_.refs_0_.refs_5_), channel_id=1, source_target_pairs={{0,12},{4,0},{8,4},{12,8},{1,13},{5,1},{9,5},{13,9},{2,14},{6,2},{... | collective-permute-start | bytes 2113544 | tf_op jit(solution)/shard_map/ppermute | solution.py:42
  35.4 26.7 %collective-permute-start.1 = (bf16[896,256]{1,0:T(8,128)(2,1)S(1)}, bf16[896,256]{1,0:T(8,128)(2,1)}, u32[]{:S(2)}, u32[]{:S(2)}) collective-permute-start(bf16[896,256]{1,0:T(8,128)(2,1)S(1)} %copy-done.22), channel_id=1, source_target_pairs={{16,0},{2,16},{0,2},{17,1},{3,17},{1,3},{20,4},{6,20},{4,6},{21,5}... | collective-permute-start | bytes 1376264 | tf_op jit(solution)/shard_map/ppermute | solution.py:559
  49.0 25.9 %collective-permute-start.14 = (bf16[224,2368]{1,0:T(8,128)(2,1)}, bf16[224,2368]{1,0:T(8,128)(2,1)S(1)}, u32[]{:S(2)}, u32[]{:S(2)}) collective-permute-start(bf16[224,2368]{1,0:T(8,128)(2,1)} %get-tuple-element.91), channel_id=1, source_target_pairs={{0,32},{32,64},{64,96},{96,0},{1,33},{33,65},{65,97},{97,1},{2,34}... | collective-permute-start | bytes 3182600 | tf_op jit(solution)/shard_map/ppermute | solution.py:42
  50.8 2.2 %copy-start.23 = (bf16[896,256]{1,0:T(8,128)(2,1)}, bf16[896,256]{1,0:T(8,128)(2,1)S(1)}, u32[]{:S(2)}) copy-start(bf16[896,256]{1,0:T(8,128)(2,1)S(1)} %collective-permute-done.9.refs_2_) | copy-start | bytes 1376260
  50.8 24.2 %collective-permute-start.15 = (bf16[224,2368]{1,0:T(8,128)(2,1)}, bf16[224,2368]{1,0:T(8,128)(2,1)S(1)}, u32[]{:S(2)}, u32[]{:S(2)}) collective-permute-start(bf16[224,2368]{1,0:T(8,128)(2,1)} %get-tuple-element.92), channel_id=1, source_target_pairs={{0,96},{32,0},{64,32},{96,64},{1,97},{33,1},{65,33},{97,65},{2,98}... | collective-permute-start | bytes 3182600 | tf_op jit(solution)/shard_map/ppermute | solution.py:42
  53.0 0.9 copy-start.2
  53.0 1.1 copy-start.12
  56.1 9.6 %collective-permute-start.10 = (bf16[688,256]{1,0:T(8,128)(2,1)}, bf16[688,256]{1,0:T(8,128)(2,1)S(1)}, u32[]{:S(2)}, u32[]{:S(2)}) collective-permute-start(bf16[688,256]{1,0:T(8,128)(2,1)} %get-tuple-element.88), channel_id=1, source_target_pairs={{0,4},{4,8},{8,12},{12,0},{1,5},{5,9},{9,13},{13,1},{2,6},{6,10},{... | collective-permute-start | bytes 1056776 | tf_op jit(solution)/shard_map/ppermute | solution.py:42
  56.1 9.6 %collective-permute-start.11 = (bf16[688,256]{1,0:T(8,128)(2,1)}, bf16[688,256]{1,0:T(8,128)(2,1)S(1)}, u32[]{:S(2)}, u32[]{:S(2)}) collective-permute-start(bf16[688,256]{1,0:T(8,128)(2,1)} %get-tuple-element.89), channel_id=1, source_target_pairs={{0,12},{4,0},{8,4},{12,8},{1,13},{5,1},{9,5},{13,9},{2,14},{6,2},{... | collective-permute-start | bytes 1056776 | tf_op jit(solution)/shard_map/ppermute | solution.py:42
  64.7 59.6 %collective-permute-start.22 = (bf16[4,1184,256]{2,1,0:T(8,128)(2,1)}, bf16[4,1184,256]{2,1,0:T(8,128)(2,1)}, u32[]{:S(2)}, u32[]{:S(2)}) collective-permute-start(bf16[4,1184,256]{2,1,0:T(8,128)(2,1)} %join.32), channel_id=1, source_target_pairs={{0,16},{16,0},{1,17},{17,1},{2,18},{18,2},{3,19},{19,3},{4,20},{20... | collective-permute-start | bytes 7274504 | tf_op jit(solution)/shard_map/ppermute | solution.py:42
  65.7 0.7 copy-start.15
  66.5 0.7 copy-start.24
  67.2 26.5 %collective-permute-start.12 = (bf16[2272,256]{1,0:T(8,128)(2,1)}, bf16[2272,256]{1,0:T(8,128)(2,1)S(1)}, u32[]{:S(2)}, u32[]{:S(2)}) collective-permute-start(bf16[2272,256]{1,0:T(8,128)(2,1)} %join.26.refs_2_.refs_0_), channel_id=1, source_target_pairs={{0,4},{4,8},{8,12},{12,0},{1,5},{5,9},{9,13},{13,1},{2,6},{6,10},{... | collective-permute-start | bytes 3489800 | tf_op jit(solution)/shard_map/ppermute | solution.py:42
  67.2 26.5 %collective-permute-start.13 = (bf16[2272,256]{1,0:T(8,128)(2,1)}, bf16[2272,256]{1,0:T(8,128)(2,1)S(1)}, u32[]{:S(2)}, u32[]{:S(2)}) collective-permute-start(bf16[2272,256]{1,0:T(8,128)(2,1)} %join.26.refs_2_.refs_0_), channel_id=1, source_target_pairs={{0,12},{4,0},{8,4},{12,8},{1,13},{5,1},{9,5},{13,9},{2,14},{6,2},{... | collective-permute-start | bytes 3489800 | tf_op jit(solution)/shard_map/ppermute | solution.py:42
  74.9 1.0 copy-start.8
  75.9 1.0 copy-start.9
  79.5 15.6 %collective-permute-start.18 = (bf16[112,2368]{1,0:T(8,128)(2,1)}, bf16[112,2368]{1,0:T(8,128)(2,1)S(1)}, u32[]{:S(2)}, u32[]{:S(2)}) collective-permute-start(bf16[112,2368]{1,0:T(8,128)(2,1)} %get-tuple-element.97.refs_7_.refs_2_), channel_id=1, source_target_pairs={{0,32},{32,64},{64,96},{96,0},{1,33},{33,65},{65,97},{97,1},{2,34}... | collective-permute-start | bytes 1591304 | tf_op jit(solution)/shard_map/ppermute | solution.py:42
  79.5 15.6 %collective-permute-start.19 = (bf16[112,2368]{1,0:T(8,128)(2,1)}, bf16[112,2368]{1,0:T(8,128)(2,1)S(1)}, u32[]{:S(2)}, u32[]{:S(2)}) collective-permute-start(bf16[112,2368]{1,0:T(8,128)(2,1)} %get-tuple-element.104), channel_id=1, source_target_pairs={{0,96},{32,0},{64,32},{96,64},{1,97},{33,1},{65,33},{97,65},{2,98}... | collective-permute-start | bytes 1591304 | tf_op jit(solution)/shard_map/ppermute | solution.py:42
  93.7 1.0 copy-start
  93.7 1.4 copy-start.3
  95.1 0.8 copy-start.11
  95.1 1.0 copy-start.21
  96.1 7.6 %copy-start.10 = (bf16[256,4,1184]{0,2,1:T(8,128)(2,1)S(1)}, bf16[256,4,1184]{0,2,1:T(8,128)(2,1)}, u32[]{:S(2)}) copy-start(bf16[256,4,1184]{0,2,1:T(8,128)(2,1)} %param.14) | copy-start | bytes 7274500
  96.1 28.2 %collective-permute-start.20 = (bf16[224,2368]{1,0:T(8,128)(2,1)}, bf16[224,2368]{1,0:T(8,128)(2,1)S(1)}, u32[]{:S(2)}, u32[]{:S(2)}) collective-permute-start(bf16[224,2368]{1,0:T(8,128)(2,1)} %get-tuple-element.110), channel_id=1, source_target_pairs={{0,32},{32,64},{64,96},{96,0},{1,33},{33,65},{65,97},{97,1},{2,34}... | collective-permute-start | bytes 3182600 | tf_op jit(solution)/shard_map/ppermute | solution.py:42
  96.1 28.2 %collective-permute-start.21 = (bf16[224,2368]{1,0:T(8,128)(2,1)}, bf16[224,2368]{1,0:T(8,128)(2,1)S(1)}, u32[]{:S(2)}, u32[]{:S(2)}) collective-permute-start(bf16[224,2368]{1,0:T(8,128)(2,1)} %get-tuple-element.111), channel_id=1, source_target_pairs={{0,96},{32,0},{64,32},{96,64},{1,97},{33,1},{65,33},{97,65},{2,98}... | collective-permute-start | bytes 3182600 | tf_op jit(solution)/shard_map/ppermute | solution.py:42
  101.1 11.8 %collective-permute-start.16 = (bf16[1136,256]{1,0:T(8,128)(2,1)}, bf16[1136,256]{1,0:T(8,128)(2,1)S(1)}, u32[]{:S(2)}, u32[]{:S(2)}) collective-permute-start(bf16[1136,256]{1,0:T(8,128)(2,1)} %get-tuple-element.102), channel_id=1, source_target_pairs={{0,4},{4,8},{8,12},{12,0},{1,5},{5,9},{9,13},{13,1},{2,6},{6,10},{... | collective-permute-start | bytes 1744904 | tf_op jit(solution)/shard_map/ppermute | solution.py:42
  101.7 11.2 %collective-permute-start.17 = (bf16[1136,256]{1,0:T(8,128)(2,1)}, bf16[1136,256]{1,0:T(8,128)(2,1)S(1)}, u32[]{:S(2)}, u32[]{:S(2)}) collective-permute-start(bf16[1136,256]{1,0:T(8,128)(2,1)} %get-tuple-element.103), channel_id=1, source_target_pairs={{0,12},{4,0},{8,4},{12,8},{1,13},{5,1},{9,5},{13,9},{2,14},{6,2},{... | collective-permute-start | bytes 1744904 | tf_op jit(solution)/shard_map/ppermute | solution.py:42
  112.9 0.9 copy-start.13
  113.7 0.8 copy-start.16
  114.6 16.3 %collective-permute-start.24 = (bf16[4,1184,256]{2,1,0:T(8,128)(2,1)}, bf16[4,1184,256]{2,1,0:T(8,128)(2,1)S(1)}, u32[]{:S(2)}, u32[]{:S(2)}) collective-permute-start(bf16[4,1184,256]{2,1,0:T(8,128)(2,1)} %join.35), channel_id=1, source_target_pairs={{0,1},{1,0},{2,3},{3,2},{4,5},{5,4},{6,7},{7,6},{8,9},{9,8},{10,11... | collective-permute-start | bytes 7274504 | tf_op jit(solution)/shard_map/ppermute | solution.py:42
  124.3 1.0 copy-start.6
  125.3 1.0 copy-start.7
  126.3 5.0 %collective-permute-start.25 = (bf16[4,1184,256]{2,1,0:T(8,128)(2,1)}, bf16[4,1184,256]{2,1,0:T(8,128)(2,1)}, u32[]{:S(2)}, u32[]{:S(2)}) collective-permute-start(bf16[4,1184,256]{2,1,0:T(8,128)(2,1)} %get-tuple-element.117.refs_7_), channel_id=1, source_target_pairs={{0,1},{1,0},{2,3},{3,2},{4,5},{5,4},{6,7},{7,6},{8,9},{9,8},{10,11... | collective-permute-start | bytes 7274504 | tf_op jit(solution)/shard_map/ppermute | solution.py:42
  128.9 32.8 %collective-permute-start.23 = (bf16[1808,512]{1,0:T(8,128)(2,1)}, bf16[1808,512]{1,0:T(8,128)(2,1)}, u32[]{:S(2)}, u32[]{:S(2)}) collective-permute-start(bf16[1808,512]{1,0:T(8,128)(2,1)} %join.34.mine_ref), channel_id=1, source_target_pairs={{0,1},{1,0},{2,3},{3,2},{4,5},{5,4},{6,7},{7,6},{8,9},{9,8},{10,11... | collective-permute-start | bytes 5554184 | tf_op jit(solution)/shard_map/ppermute | solution.py:42
  129.4 25.3 %collective-permute-start.32 = (bf16[112,2368]{1,0:T(8,128)(2,1)}, bf16[112,2368]{1,0:T(8,128)(2,1)S(1)}, u32[]{:S(2)}, u32[]{:S(2)}) collective-permute-start(bf16[112,2368]{1,0:T(8,128)(2,1)} %get-tuple-element.116.refs_1_), channel_id=1, source_target_pairs={{0,96},{32,0},{64,32},{96,64},{1,97},{33,1},{65,33},{97,65},{2,98}... | collective-permute-start | bytes 1591304 | tf_op jit(solution)/shard_map/ppermute | solution.py:42
  130.3 24.4 %collective-permute-start.31 = (bf16[112,2368]{1,0:T(8,128)(2,1)}, bf16[112,2368]{1,0:T(8,128)(2,1)S(1)}, u32[]{:S(2)}, u32[]{:S(2)}) collective-permute-start(bf16[112,2368]{1,0:T(8,128)(2,1)} %get-tuple-element.118.refs_9_), channel_id=1, source_target_pairs={{0,32},{32,64},{64,96},{96,0},{1,33},{33,65},{65,97},{97,1},{2,34}... | collective-permute-start | bytes 1591304 | tf_op jit(solution)/shard_map/ppermute | solution.py:42
  130.8 1.5 copy-start.29
  152.0 27.0 %collective-permute-start.26 = (bf16[224,2368]{1,0:T(8,128)(2,1)}, bf16[224,2368]{1,0:T(8,128)(2,1)S(1)}, u32[]{:S(2)}, u32[]{:S(2)}) collective-permute-start(bf16[224,2368]{1,0:T(8,128)(2,1)} %get-tuple-element.121), channel_id=1, source_target_pairs={{0,32},{32,64},{64,96},{96,0},{1,33},{33,65},{65,97},{97,1},{2,34}... | collective-permute-start | bytes 3182600 | tf_op jit(solution)/shard_map/ppermute | solution.py:42
  152.0 26.9 %collective-permute-start.27 = (bf16[224,2368]{1,0:T(8,128)(2,1)}, bf16[224,2368]{1,0:T(8,128)(2,1)S(1)}, u32[]{:S(2)}, u32[]{:S(2)}) collective-permute-start(bf16[224,2368]{1,0:T(8,128)(2,1)} %get-tuple-element.122), channel_id=1, source_target_pairs={{0,96},{32,0},{64,32},{96,64},{1,97},{33,1},{65,33},{97,65},{2,98}... | collective-permute-start | bytes 3182600 | tf_op jit(solution)/shard_map/ppermute | solution.py:42
  154.7 0.8 copy-start.18
  154.7 1.0 copy-start.17
  161.0 29.1 %collective-permute-start.33 = (bf16[224,2368]{1,0:T(8,128)(2,1)}, bf16[224,2368]{1,0:T(8,128)(2,1)S(1)}, u32[]{:S(2)}, u32[]{:S(2)}) collective-permute-start(bf16[224,2368]{1,0:T(8,128)(2,1)} %get-tuple-element.140), channel_id=1, source_target_pairs={{0,16},{16,0},{1,17},{17,1},{2,18},{18,2},{3,19},{19,3},{4,20},{20... | collective-permute-start | bytes 3182600 | tf_op jit(solution)/shard_map/ppermute | solution.py:42
  178.9 1.0 copy-start.4
  179.9 1.0 copy-start.5
  183.5 13.8 %collective-permute-start.28 = (bf16[112,2368]{1,0:T(8,128)(2,1)}, bf16[112,2368]{1,0:T(8,128)(2,1)S(1)}, u32[]{:S(2)}, u32[]{:S(2)}) collective-permute-start(bf16[112,2368]{1,0:T(8,128)(2,1)} %get-tuple-element.127.refs_0_), channel_id=1, source_target_pairs={{0,32},{32,64},{64,96},{96,0},{1,33},{33,65},{65,97},{97,1},{2,34}... | collective-permute-start | bytes 1591304 | tf_op jit(solution)/shard_map/ppermute | solution.py:42
  183.5 13.8 %collective-permute-start.29 = (bf16[112,2368]{1,0:T(8,128)(2,1)}, bf16[112,2368]{1,0:T(8,128)(2,1)S(1)}, u32[]{:S(2)}, u32[]{:S(2)}) collective-permute-start(bf16[112,2368]{1,0:T(8,128)(2,1)} %get-tuple-element.130), channel_id=1, source_target_pairs={{0,96},{32,0},{64,32},{96,64},{1,97},{33,1},{65,33},{97,65},{2,98}... | collective-permute-start | bytes 1591304 | tf_op jit(solution)/shard_map/ppermute | solution.py:42
  190.1 1.0 copy-start.14
  194.4 9.8 %collective-permute-start.34 = (bf16[224,1184]{1,0:T(8,128)(2,1)}, bf16[224,1184]{1,0:T(8,128)(2,1)S(1)}, u32[]{:S(2)}, u32[]{:S(2)}) collective-permute-start(bf16[224,1184]{1,0:T(8,128)(2,1)} %get-tuple-element.142), channel_id=1, source_target_pairs={{0,1},{1,0},{2,3},{3,2},{4,5},{5,4},{6,7},{7,6},{8,9},{9,8},{10,11... | collective-permute-start | bytes 1591304 | tf_op jit(solution)/shard_map/ppermute | solution.py:42
  197.3 0.8 copy-start.19
  198.1 0.8 copy-start.20
  201.8 6.3 %collective-permute-start.30 = (bf16[224,1184]{1,0:T(8,128)(2,1)}, bf16[224,1184]{1,0:T(8,128)(2,1)S(1)}, u32[]{:S(2)}, u32[]{:S(2)}) collective-permute-start(bf16[224,1184]{1,0:T(8,128)(2,1)} %get-tuple-element.134), channel_id=1, source_target_pairs={{0,1},{1,0},{2,3},{3,2},{4,5},{5,4},{6,7},{7,6},{8,9},{9,8},{10,11... | collective-permute-start | bytes 1591304 | tf_op jit(solution)/shard_map/ppermute | solution.py:42
  204.2 0.8 copy-start.27
  208.1 0.8 copy-start.26
  (2 other events, 1.4 us)
